TPU v7x, 256 devices: a whole 4x4x8 slice. The times are simulated.
256 devices in a mesh: dp: 8 (over z_lo, core), row: 4 (over x), col: 8 (over z_hi, y).
Axes of the slice: x: 4, y: 4, z: 8 (z_hi: 2, z_lo: 4; z = z_hi * 4 + z_lo), core: 2. Of those that a mesh axis runs over, the one named last changes fastest.
Arguments:
- inputs: bfloat16 [1024, 8192], P('dp', ('row', 'col')), may hold values from -6 to 6
- grad_out: bfloat16 [1024, 8192], P('dp', ('row', 'col')), may hold values from -6 to 6
- up_blocks: bfloat16 [4096, 128, 128], P(('row', 'col')), may hold values from -0.125 to 0.125
- up_index: int32 [4096], P(('row', 'col')), may hold values from 0 to 63, as said below
- down_blocks: bfloat16 [4096, 128, 128], P(('row', 'col')), may hold values from -0.0625 to 0.0625
- down_index: int32 [4096], P(('row', 'col')), may hold values from 0 to 255, as said below
Outputs:
- outputs: bfloat16 [1024, 8192], P('dp', ('row', 'col'))
- grad_in: bfloat16 [1024, 8192], P('dp', ('row', 'col'))
- grad_up: float32 [4096, 128, 128], P(('row', 'col'), 'dp')
- grad_down: float32 [4096, 128, 128], P(('row', 'col'), 'dp')
Inputs may be any that keep to these rules, and one draw needn't show every extreme that they name: `up_index`: for each row tile r and column block j, the 4 entries of run (r, j) name distinct row blocks of row tile r. Within row tile r and column tile c they are r * 16 + ((j mod 16) XOR m XOR o), m over a set of 4 values closed under XOR, o fixed for the tile. `down_index`: for each row tile r, column tile c and feature block i of row tile r, the 8 entries name distinct hidden-unit blocks of column tile c: c * 32 + ((i mod 32) XOR m XOR o), m over a set of 8 values closed under XOR, o fixed for the tile.
All inputs are finite; a program needn't handle non-finite values.
Results may differ from a plain program's by a relative error of at most 0.024.
Values may be sent and summed in bfloat16 or wider, within the bound.
No kernel may reach another device: no remote copies, remote signals or barrier semaphores. Data moves between devices by JAX's collectives and lax.ppermute only.
A program may use at most 128 MiB of HBM per device.

v0:
```python
import jax
import jax.numpy as jnp
from jax import lax
from jax.experimental import pallas as pl
from jax.experimental.pallas import tpu as pltpu
from jax.sharding import Mesh
from jax.sharding import PartitionSpec as P

KB = 4
KB2 = 8
BS = 128
ROWS = 16
COLS = 32
BF = jnp.bfloat16
F32 = jnp.float32

gelu_scale = 0.7978845608028654
cubic_term = 0.044715


def gelu_both(values):
    tangent = jnp.tanh(gelu_scale * (values + cubic_term * values * values * values))
    value = 0.5 * values * (1.0 + tangent)
    slope = 0.5 * (1.0 + tangent) + 0.5 * values * (1.0 - tangent * tangent) * gelu_scale * (
        1.0 + 3.0 * cubic_term * values * values
    )
    return value, slope


SMEM = pl.BlockSpec(memory_space=pltpu.SMEM)
VMEM = pl.BlockSpec(memory_space=pltpu.VMEM)
HBM = pl.BlockSpec(memory_space=pltpu.HBM)


def call(kernel, scalars, arrays, outs, scratch=(), weights=(), flops=1.1e9, name=None):
    moved = sum(a.size * a.dtype.itemsize for a in (*arrays, *weights))
    held = [pltpu.VMEM(w.shape, w.dtype) for w in weights] + [pltpu.SemaphoreType.DMA((4,)) for w in weights]
    return pl.pallas_call(
        kernel,
        out_shape=outs,
        in_specs=[SMEM] * len(scalars) + [VMEM] * len(arrays) + [HBM] * len(weights),
        out_specs=[VMEM] * len(outs),
        scratch_shapes=list(scratch) + held,
        compiler_params=pltpu.CompilerParams(vmem_limit_bytes=62 * 2**20),
        cost_estimate=pl.CostEstimate(flops=int(flops), bytes_accessed=int(moved), transcendentals=0),
        name=name,
    )(*scalars, *arrays, *weights)


def fetch(source, held, sems, firsts):
    copies = []
    for n, first in enumerate(firsts):
        part = pl.ds(first, 32)
        copies.append(pltpu.make_async_copy(source.at[part], held.at[part], sems.at[n]))
        copies[-1].start()
    return copies


def lanes(half):
    return pl.ds(pl.multiple_of(half * BS, BS), BS)


def block(ref, at):
    return ref[at // 2, :, lanes(at % 2)]


def up_kernel(order, where, x0, x1, x2, x3, source, o0, o1, o2, o3, x, w, sems):
    outs = (o0, o1, o2, o3)
    copies = fetch(source, w, sems, [order[slot * 8] * KB for slot in range(4)])
    for n, piece in enumerate((x0, x1, x2, x3)):
        x[n * 2:n * 2 + 2] = piece[...]
    for slot in (1, 2, 3, 0):
        out = outs[slot]
        copies[slot].wait()

        def step(jj, carry):
            j = order[slot * 8 + jj]
            lhs = jnp.concatenate([block(x, where[j * KB + k]) for k in range(KB)], axis=1)
            rhs = w[pl.ds(j * KB, KB)].reshape(KB * BS, BS)
            out[jj] = jnp.dot(lhs, rhs, preferred_element_type=F32).astype(BF)
            return carry

        lax.fori_loop(0, 8, step, 0, unroll=4)


def add_back(acc, run, where, width, rows, w):
    rhs = w[pl.ds(run * width, width)].reshape(width * BS, BS)
    got = lax.dot_general(rows, rhs, (((1,), (1,)), ((), ())), preferred_element_type=F32)
    for k in range(width):
        at = where[run * width + k]
        acc[at] = acc[at] + got[:, k * BS:(k + 1) * BS]


def back_kernel(spot, where, g0, g1, g2, g3, source, o0, o1, o2, o3, g, acc, w, sems):
    copies = fetch(source, w, sems, [0, 32, 64, 96])
    for n, piece in enumerate((g0, g1, g2, g3)):
        g[n * 2:n * 2 + 2] = piece[...]
    acc[...] = jnp.zeros_like(acc)
    for part in range(4):
        copies[part].wait()

        def step(ii, carry):
            i = part * 4 + ii
            add_back(acc, i, where, KB2, block(g, spot[i]), w)
            return carry

        lax.fori_loop(0, 4, step, 0, unroll=2)
    for slot, out in enumerate((o0, o1, o2, o3)):
        out[...] = acc[slot * 8:(slot + 1) * 8].astype(BF)


def act_kernel(p0, p1, p2, p3, active, slope, rows):
    def step(b, carry):
        hidden = p0[b].astype(F32) + p1[b].astype(F32) + p2[b].astype(F32) + p3[b].astype(F32)
        value, slopes = gelu_both(hidden)
        slope[b] = slopes
        value = value.astype(BF)
        active[b] = value
        turned = value.T.reshape(8, 16, BS)
        for d in range(8):
            rows[d, b] = turned[d]
        return carry

    lax.fori_loop(0, 8, step, 0, unroll=2)


def turn_kernel(place, x, x2, out):
    z, q = place[0], place[1]

    def step(p, carry):
        for half in range(2):
            for group, ref in enumerate((x, x2)):
                rows = ref[p, :, half * BS:(half + 1) * BS].T.reshape(4, 2, 16, BS)
                for zz in range(4):
                    mine = jnp.where(q == 0, rows[zz, 0], rows[zz, 1])
                    out[p * 2 + half, jnp.bitwise_xor(zz, z), :, group * BS:(group + 1) * BS] = mine
        return carry

    lax.fori_loop(0, 8, step, 0, unroll=2)


def up_terms_kernel(spot, where, xt, v0, v1, *outs):
    for chunk in range(2):
        near, far = outs[chunk * 2:chunk * 2 + 2]

        def step(n, carry):
            j = chunk * 16 + n
            at = spot[j]
            lhs = jnp.concatenate([xt[where[j * KB + k]].reshape(64, 2 * BS) for k in range(KB)], axis=0)
            rhs = jnp.concatenate([v0[at], v1[at]], axis=0)
            got = jnp.dot(lhs, rhs, preferred_element_type=F32).astype(BF).reshape(KB, 4, 16, BS)
            for s, out in enumerate((near, far, near, far)):
                out[s // 2, pl.ds(n * KB, KB)] = got[:, s]
            return carry

        lax.fori_loop(0, 16, step, 0, unroll=2)


def ends_kernel(feature_order, spot, up_where, down_where, v, a0, a1, a2, a3, source1, source2, *rest):
    outs, a, acc, w1, w2, sems1, sems2 = rest[:4], *rest[4:]
    copies1 = fetch(source1, w1, sems1, [0, 32, 64, 96])
    copies2 = fetch(source2, w2, sems2, [0, 32, 64, 96])
    for n, piece in enumerate((a0, a1, a2, a3)):
        a[n * 16:n * 16 + 16] = piece[...]
    acc[...] = jnp.zeros_like(acc)
    for part in range(4):
        copies1[part].wait()

        def step(jj, carry):
            j = part * 8 + jj
            add_back(acc, j, up_where, KB, v[spot[j]], w1)
            return carry

        lax.fori_loop(0, 8, step, 0, unroll=4)
    for part in range(4):
        copies2[part].wait()
    for slot, out in enumerate(outs):
        for t in range(2):
            for half in range(2):
                loc = slot * 4 + t * 2 + half
                at = slice(half * BS, (half + 1) * BS)
                out[t, 1, :, at] = acc[loc].astype(BF)
                i = feature_order[loc]
                runs = [down_where[i * KB2 + k] for k in range(KB2)]
                lhs = jnp.concatenate([a[u // 8 * 16 + u % 8] for u in runs], axis=1)
                rhs = w2[pl.ds(i * KB2, KB2)].reshape(KB2 * BS, BS)
                out[t, 0, :, at] = jnp.dot(lhs, rhs, preferred_element_type=F32).astype(BF)


def down_terms_kernel(place, spot, where, a, g0, g1, f0, f1, out):
    z, q = place[0], place[1]

    def step(i, carry):
        at = spot[i]
        runs = [where[i * KB2 + k] for k in range(KB2)]
        lhs, rhs = [], []
        for tq, (g, f) in enumerate(((g0, f0), (g1, f1))):
            for tz in range(4):
                source = jnp.bitwise_xor(z, tz) * 2 + jnp.bitwise_xor(q, tq) + 8
                lhs.append(jnp.concatenate(
                    [a[u // 8 * 16 + source, pl.ds(pl.multiple_of(u % 8 * 16, 16), 16), :] for u in runs], axis=0
                ))
                rhs.append(block(g, at) if tz == 0 else f[at // 4, tz - 1, at // 2 % 2, :, lanes(at % 2)])
        got = jnp.dot(jnp.concatenate(lhs, axis=1), jnp.concatenate(rhs, axis=0), preferred_element_type=F32)
        out[pl.ds(i * KB2, KB2)] = got.reshape(KB2, 16, BS)
        return carry

    lax.fori_loop(0, ROWS, step, 0, unroll=2)


def close_kernel(n0, r0, s0, n1, r1, s1, out):
    for chunk, (near, got, last) in enumerate(((n0, r0, s0), (n1, r1, s1))):
        out[chunk * 64:chunk * 64 + 64] = near[0].astype(F32) + got[0].astype(F32) + last[...].astype(F32)


def shift(value, axis, by):
    return lax.ppermute(value, axis, [(i, (i + by) % 4) for i in range(4)])


def swap(value, axis):
    return lax.ppermute(value, axis, [(0, 1), (1, 0)])


def across(value, by):
    return lax.ppermute(value, "z", [(i, i ^ by) for i in range(4)])


def after(value, *events):
    return lax.optimization_barrier((value, *events))[0]


def pieces(own, axis):
    return [own] + [shift(own, axis, -s) for s in (1, 2, 3)]


def exchange(parts, axis):
    return [parts[0]] + [shift(parts[s], axis, s) for s in (1, 2, 3)]


def total(parts):
    return sum((p.astype(F32) for p in parts[1:]), parts[0].astype(F32))


def local(inputs, grad_out, up_blocks, up_index, down_blocks, down_index):
    z, q, r, h, y = (lax.axis_index(a).astype(jnp.int32) for a in ("z", "q", "row", "h", "y"))
    place = jnp.stack([z, q])
    c = h * 4 + y

    def feature_spot(b):
        return ((b // 2 % 4 - y) % 4) * 4 + jnp.bitwise_xor(b // 8, h) * 2 + b % 2

    def feature_at(s):
        return jnp.bitwise_xor(s // 2 % 2, h) * 8 + ((s // 4 + y) % 4) * 2 + s % 2

    def hidden_spot(f):
        return ((f // 8 - r) % 4) * 8 + f % 8

    def hidden_at(s):
        return ((s // 8 + r) % 4) * 8 + s % 8

    features, units = jnp.arange(ROWS, dtype=jnp.int32), jnp.arange(COLS, dtype=jnp.int32)
    up_where = feature_spot(up_index - r * ROWS)
    down_where = hidden_spot(down_index - c * COLS)
    feature_spots, feature_order = feature_spot(features), feature_at(features)
    hidden_spots, hidden_order = hidden_spot(units), hidden_at(units)

    def shape(*dims, dtype=BF):
        return jax.ShapeDtypeStruct(dims, dtype)

    x_own = jnp.stack([inputs, swap(inputs, "h")])
    g_own = jnp.stack([grad_out, swap(grad_out, "h")])
    panel, piece = shape(8, BS, 2 * BS), shape(8, BS, BS)

    features_in, cotangents = pieces(x_own, "y"), pieces(g_own, "y")
    features_in[0] = after(features_in[0], cotangents[1])
    *up, x = call(
        up_kernel, (hidden_order, up_where), features_in, [piece] * 4 + [panel], weights=(up_blocks,), name="up"
    )
    up = exchange(up, "row")
    far1 = across(after(g_own, x), 1)
    far2 = across(after(jnp.stack([g_own, far1]), up[1]), 2)
    cotangents[0] = after(cotangents[0], up[1])
    *back, g = call(
        back_kernel, (feature_spots, down_where), cotangents, [piece] * 4 + [panel],
        [pltpu.VMEM((COLS, BS, BS), F32)], weights=(down_blocks,), name="back",
    )
    back = exchange(back, "row")
    x2 = swap(after(x, g), "q")
    (turned,) = call(turn_kernel, (place,), (x, x2), [shape(ROWS, 4, 16, 2 * BS)], flops=1e7, name="turn")
    active, slope, rows = call(
        act_kernel, (), up, [piece, shape(8, BS, BS, dtype=F32), shape(8, 8, 16, BS)], flops=1e7, name="act"
    )
    rows = lax.all_to_all(after(rows, back[0]), ("z", "q"), 0, 0, tiled=True)
    slope = after(slope, rows, turned, far2)

    own = (total(back) * slope).astype(BF)
    hidden = jnp.concatenate(pieces(own, "row"), axis=0)
    far = pieces(jnp.concatenate([far1[None], far2])[None], "y")
    hidden2 = swap(after(hidden, far[1]), "q")
    far = jnp.concatenate(far, axis=0)

    near0, send0, near1, send1 = call(
        up_terms_kernel, (hidden_spots, up_where), (turned, hidden, hidden2), [shape(2, 64, 16, BS)] * 4, name="up_terms"
    )
    got0, got1 = across(send0, 1), across(send1, 1)
    both = jnp.concatenate([active, rows.reshape(8, BS, BS)])
    both = pieces(after(both, send0, far), "row")
    last0 = across((near0[1].astype(F32) + got0[1].astype(F32)).astype(BF), 2)
    last1 = across((near1[1].astype(F32) + got1[1].astype(F32)).astype(BF), 2)

    *ends, a = call(
        ends_kernel, (feature_order, hidden_spots, up_where, down_where), (after(hidden, got0), *both),
        [shape(2, 2, BS, 2 * BS)] * 4 + [shape(64, BS, BS)], [pltpu.VMEM((ROWS, BS, BS), F32)],
        weights=(up_blocks, down_blocks), flops=2.2e9, name="ends",
    )
    mine = total(exchange(ends, "y"))
    ends = (mine[0] + swap(mine[1].astype(BF), "h").astype(F32)).astype(BF)

    g2, far3 = swap(after(g, send0), "q"), swap(after(far, send0), "q")
    (grad_down,) = call(
        down_terms_kernel, (place, feature_spots, down_where), (a, g, g2, far, far3),
        [shape(128, 16, BS, dtype=F32)], name="down_terms",
    )
    (grad_up,) = call(
        close_kernel, (), (near0, got0, last0, near1, got1, last1), [shape(128, 16, BS, dtype=F32)], flops=1e6, name="close"
    )
    return ends[0], ends[1], grad_up, grad_down


def solution(mesh):
    fine = Mesh(mesh.devices.reshape(4, 2, 4, 2, 4), ("z", "q", "row", "h", "y"))
    tokens, width = ("z", "q"), ("row", "h", "y")
    placed = (
        P(tokens, width),
        P(tokens, width),
        P(width, None, None),
        P(width),
        P(width, None, None),
        P(width),
    )
    return jax.shard_map(
        local,
        mesh=fine,
        in_specs=placed,
        out_specs=(P(tokens, width), P(tokens, width), P(width, tokens, None), P(width, tokens, None)),
        check_vma=False,
    )
```

profile of v0, /device:TPU:32, one launch (start us, length us, event | category | flops | bytes accessed | tf_op | source)
XLA Modules:
  0.0 206.7 jit_solution(17869253612295283355)
XLA Ops:
  0.6 6.4 %collective-permute-start.1 = (bf16[128,256]{1,0:T(8,128)(2,1)}, bf16[128,256]{1,0:T(8,128)(2,1)S(1)}, u32[]{:S(2)}, u32[]{:S(2)}) collective-permute-start(bf16[128,256]{1,0:T(8,128)(2,1)} %param.6), channel_id=1, source_target_pairs={{0,4},{4,0},{1,5},{5,1},{2,6},{6,2},{3,7},{7,3},{8,12},{12,8},{9,1... | collective-permute-start | bytes 196616 | tf_op jit(solution)/shard_map/ppermute | solution.py:221
  7.1 5.1 %collective-permute-done.1 = bf16[128,256]{1,0:T(8,128)(2,1)S(1)} collective-permute-done((bf16[128,256]{1,0:T(8,128)(2,1)}, bf16[128,256]{1,0:T(8,128)(2,1)S(1)}, u32[]{:S(2)}, u32[]{:S(2)}) %collective-permute-start.1) | collective-permute-done | bytes 65568 | tf_op jit(solution)/shard_map/ppermute | solution.py:221
  13.1 3.1 %collective-permute-start.3 = (bf16[2,128,256]{2,1,0:T(8,128)(2,1)S(1)}, bf16[2,128,256]{2,1,0:T(8,128)(2,1)S(1)}, u32[]{:S(2)}, u32[]{:S(2)}) collective-permute-start(bf16[2,128,256]{2,1,0:T(8,128)(2,1)S(1)} %pad_maximum_fusion.5.x0), channel_id=1, source_target_pairs={{0,3},{1,0},{2,1},{3,2},{4,7},{5,4},{6,5},{7,6},{8,11},{9,8},{10,9... | collective-permute-start | bytes 393224 | tf_op jit(solution)/shard_map/ppermute | solution.py:217
  27.7 6.2 %up.1 = (bf16[8,128,128]{2,1,0:T(8,128)(2,1)}, bf16[8,128,128]{2,1,0:T(8,128)(2,1)}, bf16[8,128,128]{2,1,0:T(8,128)(2,1)}, bf16[8,128,128]{2,1,0:T(8,128)(2,1)}, bf16[8,128,256]{2,1,0:T(8,128)(2,1)}) custom-call(s32[32]{0:T(128)} %fusion.27.order, s32[128]{0:T(128)} %fusion.5.where.up_where, bf16[2,128,256]{2,1,0:T(8,128)(2,1)} %copy-done.9, ...), custom_call_target="tpu_custom_call" | custom-call | flops 1100000000 | bytes 4718592 | tf_op jit(solution)/shard_map/up/pallas_call | solution.py:38
  36.1 2.7 %collective-permute-start.12 = (bf16[8,128,128]{2,1,0:T(8,128)(2,1)}, bf16[8,128,128]{2,1,0:T(8,128)(2,1)S(1)}, u32[]{:S(2)}, u32[]{:S(2)}) collective-permute-start(bf16[8,128,128]{2,1,0:T(8,128)(2,1)} %get-tuple-element.46), channel_id=1, source_target_pairs={{0,16},{8,24},{16,0},{24,8},{1,17},{9,25},{17,1},{25,9},{2,18},{10... | collective-permute-start | bytes 786440 | tf_op jit(solution)/shard_map/ppermute | solution.py:217
  40.7 3.9 %collective-permute-done.6.p1 = bf16[8,128,128]{2,1,0:T(8,128)(2,1)S(1)} collective-permute-done((bf16[8,128,128]{2,1,0:T(8,128)(2,1)}, bf16[8,128,128]{2,1,0:T(8,128)(2,1)S(1)}, u32[]{:S(2)}, u32[]{:S(2)}) %collective-permute-start.6) | collective-permute-done | bytes 262176 | tf_op jit(solution)/shard_map/ppermute | solution.py:217
  45.9 6.1 %back.1 = (bf16[8,128,128]{2,1,0:T(8,128)(2,1)}, bf16[8,128,128]{2,1,0:T(8,128)(2,1)}, bf16[8,128,128]{2,1,0:T(8,128)(2,1)}, bf16[8,128,128]{2,1,0:T(8,128)(2,1)}, bf16[8,128,256]{2,1,0:T(8,128)(2,1)}) custom-call(s32[16]{0:T(128)} %fusion.23.spot, s32[128]{0:T(128)} %fusion.6.where.down_where, bf16[2,128,256]{2,1,0:T(8,128)(2,1)} %copy-done.8, ...), custom_call_target="tpu_custom_call" | custom-call | flops 1100000000 | bytes 4718592 | tf_op jit(solution)/shard_map/back/pallas_call | solution.py:38
  53.1 2.8 %act.1 = (bf16[8,128,128]{2,1,0:T(8,128)(2,1)}, f32[8,128,128]{2,1,0:T(8,128)}, bf16[8,8,16,128]{3,2,1,0:T(8,128)(2,1)}) custom-call(bf16[8,128,128]{2,1,0:T(8,128)(2,1)} %get-tuple-element.45.p0, bf16[8,128,128]{2,1,0:T(8,128)(2,1)} %copy-done.15, bf16[8,128,128]{2,1,0:T(8,128)(2,1)} %copy-done.17, bf16[8,128,128]{2,1,0:T(8,128)(2,1)} %copy-done.18), custom_call_target="tpu_custom_call" | custom-call | flops 10000000 | bytes 1048576 | tf_op jit(solution)/shard_map/act/pallas_call | solution.py:38
  55.9 5.5 %all-to-all-start = ((bf16[8,8,16,128]{3,2,1,0:T(8,128)(2,1)}), bf16[8,8,16,128]{3,2,1,0:T(8,128)(2,1)S(1)}, u32[]{:S(2)}, u32[]{:S(2)}) async-start(bf16[8,8,16,128]{3,2,1,0:T(8,128)(2,1)} %get-tuple-element.50), calls=%async_computation | async-start | bytes 524288 | tf_op jit(solution)/shard_map/all_to_all | solution.py:293
  71.8 7.0 %collective-permute-done.16 = bf16[2,2,128,256]{3,2,1,0:T(8,128)(2,1)} collective-permute-done((bf16[2,2,128,256]{3,2,1,0:T(8,128)(2,1)}, bf16[2,2,128,256]{3,2,1,0:T(8,128)(2,1)}, u32[]{:S(2)}, u32[]{:S(2)}) %collective-permute-start.16) | collective-permute-done | bytes 262176 | tf_op jit(solution)/shard_map/ppermute | solution.py:225
  87.3 2.7 %collective-permute-start.20 = (bf16[1,3,2,128,256]{4,3,2,1,0:T(8,128)(2,1)S(1)}, bf16[1,3,2,128,256]{4,3,2,1,0:T(8,128)(2,1)S(1)}, u32[]{:S(2)}, u32[]{:S(2)}) collective-permute-start(bf16[1,3,2,128,256]{4,3,2,1,0:T(8,128)(2,1)S(1)} %maximum_bitcast_fusion), channel_id=1, source_target_pairs={{0,3},{1,0},{2,1},{3,2},{4,7},{5,4},{6,5},{7,6},{8,11},{9,8},{10,9... | collective-permute-start | bytes 1179656 | tf_op jit(solution)/shard_map/ppermute | solution.py:217
  89.9 7.8 %collective-permute-done.19 = bf16[8,128,128]{2,1,0:T(8,128)(2,1)S(1)} collective-permute-done((bf16[8,128,128]{2,1,0:T(8,128)(2,1)S(1)}, bf16[8,128,128]{2,1,0:T(8,128)(2,1)S(1)}, u32[]{:S(2)}, u32[]{:S(2)}) %collective-permute-start.19) | collective-permute-done | bytes 262176 | tf_op jit(solution)/shard_map/ppermute | solution.py:217
  99.8 3.1 %collective-permute-start.23 = (bf16[1,3,2,128,256]{4,3,2,1,0:T(8,128)(2,1)S(1)}, bf16[1,3,2,128,256]{4,3,2,1,0:T(8,128)(2,1)}, u32[]{:S(2)}, u32[]{:S(2)}) collective-permute-start(bf16[1,3,2,128,256]{4,3,2,1,0:T(8,128)(2,1)S(1)} %maximum_bitcast_fusion), channel_id=1, source_target_pairs={{0,2},{1,3},{2,0},{3,1},{4,6},{5,7},{6,4},{7,5},{8,10},{9,11},{10,... | collective-permute-start | bytes 1179656 | tf_op jit(solution)/shard_map/ppermute | solution.py:217
  104.3 6.3 %up_terms.1 = (bf16[2,64,16,128]{3,2,1,0:T(8,128)(2,1)}, bf16[2,64,16,128]{3,2,1,0:T(8,128)(2,1)}, bf16[2,64,16,128]{3,2,1,0:T(8,128)(2,1)}, bf16[2,64,16,128]{3,2,1,0:T(8,128)(2,1)}) custom-call(s32[32]{0:T(128)} %fusion.15.spot, s32[128]{0:T(128)} %fusion.5.where.up_where, bf16[16,4,16,256]{3,2,1,0:T(8,128)(2,1)} %turn.1.xt, ...), custom_call_target="tpu_custom_call" | custom-call | flops 1100000000 | bytes 2621440 | tf_op jit(solution)/shard_map/up_terms/pallas_call | solution.py:38
  111.4 9.6 %collective-permute-done.23 = bf16[1,3,2,128,256]{4,3,2,1,0:T(8,128)(2,1)} collective-permute-done((bf16[1,3,2,128,256]{4,3,2,1,0:T(8,128)(2,1)S(1)}, bf16[1,3,2,128,256]{4,3,2,1,0:T(8,128)(2,1)}, u32[]{:S(2)}, u32[]{:S(2)}) %collective-permute-start.23) | collective-permute-done | bytes 393248 | tf_op jit(solution)/shard_map/ppermute | solution.py:217
  127.6 19.7 %collective-permute-done.25.a1 = bf16[16,128,128]{2,1,0:T(8,128)(2,1)S(1)} collective-permute-done((bf16[16,128,128]{2,1,0:T(8,128)(2,1)S(1)}, bf16[16,128,128]{2,1,0:T(8,128)(2,1)S(1)}, u32[]{:S(2)}, u32[]{:S(2)}) %collective-permute-start.25) | collective-permute-done | bytes 524320 | tf_op jit(solution)/shard_map/ppermute | solution.py:217
  151.0 8.8 %ends.1 = (bf16[2,2,128,256]{3,2,1,0:T(8,128)(2,1)}, bf16[2,2,128,256]{3,2,1,0:T(8,128)(2,1)}, bf16[2,2,128,256]{3,2,1,0:T(8,128)(2,1)}, bf16[2,2,128,256]{3,2,1,0:T(8,128)(2,1)}, bf16[64,128,128]{2,1,0:T(8,128)(2,1)}) custom-call(s32[16]{0:T(128)} %fusion.11.feature_order, s32[32]{0:T(128)} %fusion.15.spot, s32[128]{0:T(128)} %fusion.5.where.up_where, ...), custom_call_target="tpu_custom_call" | custom-call | flops 2200000000 | bytes 11534336 | tf_op jit(solution)/shard_map/ends/pallas_call | solution.py:38
  165.9 3.5 %collective-permute-done.30 = bf16[2,2,128,256]{3,2,1,0:T(8,128)(2,1)S(1)} collective-permute-done((bf16[2,2,128,256]{3,2,1,0:T(8,128)(2,1)}, bf16[2,2,128,256]{3,2,1,0:T(8,128)(2,1)S(1)}, u32[]{:S(2)}, u32[]{:S(2)}) %collective-permute-start.30) | collective-permute-done | bytes 262176 | tf_op jit(solution)/shard_map/ppermute | solution.py:217
  171.0 4.5 %collective-permute-done.28 = bf16[2,2,128,256]{3,2,1,0:T(8,128)(2,1)S(1)} collective-permute-done((bf16[2,2,128,256]{3,2,1,0:T(8,128)(2,1)}, bf16[2,2,128,256]{3,2,1,0:T(8,128)(2,1)S(1)}, u32[]{:S(2)}, u32[]{:S(2)}) %collective-permute-start.28) | collective-permute-done | bytes 262176 | tf_op jit(solution)/shard_map/ppermute | solution.py:217
  176.5 4.4 %collective-permute-start.31 = (bf16[2,128,256]{2,1,0:T(8,128)(2,1)S(1)}, bf16[2,128,256]{2,1,0:T(8,128)(2,1)}, u32[]{:S(2)}, u32[]{:S(2)}) collective-permute-start(bf16[2,128,256]{2,1,0:T(8,128)(2,1)S(1)} %fusion.4), channel_id=1, source_target_pairs={{0,4},{4,0},{1,5},{5,1},{2,6},{6,2},{3,7},{7,3},{8,12},{12,8},{9,1... | collective-permute-start | bytes 393224 | tf_op jit(solution)/shard_map/ppermute | solution.py:221
  180.9 8.0 %collective-permute-done.34.s1 = bf16[64,16,128]{2,1,0:T(8,128)(2,1)} collective-permute-done((bf16[64,16,128]{2,1,0:T(8,128)(2,1)S(1)}, bf16[64,16,128]{2,1,0:T(8,128)(2,1)}, u32[]{:S(2)}, u32[]{:S(2)}) %collective-permute-start.34) | collective-permute-done | bytes 262176 | tf_op jit(solution)/shard_map/ppermute | solution.py:225
  188.9 2.8 %close.1 = f32[128,16,128]{2,1,0:T(8,128)} custom-call(bf16[2,64,16,128]{3,2,1,0:T(8,128)(2,1)} %get-tuple-element.66.n0, bf16[2,64,16,128]{3,2,1,0:T(8,128)(2,1)} %copy-done.4, bf16[64,16,128]{2,1,0:T(8,128)(2,1)} %copy-done.13, bf16[2,64,16,128]{3,2,1,0:T(8,128)(2,1)} %get-tuple-element.67.n1, bf16[2,64,16,128]{3,2,1,0:T(8,128)(2,1)} %collective-permute-done.33.r1, ...), custom_call_target="tpu_custom_call" | custom-call | flops 1000000 | bytes 2621440 | tf_op jit(solution)/shard_map/close/pallas_call | solution.py:38
  191.7 5.9 %collective-permute-done.31 = bf16[2,128,256]{2,1,0:T(8,128)(2,1)} collective-permute-done((bf16[2,128,256]{2,1,0:T(8,128)(2,1)S(1)}, bf16[2,128,256]{2,1,0:T(8,128)(2,1)}, u32[]{:S(2)}, u32[]{:S(2)}) %collective-permute-start.31) | collective-permute-done | bytes 131104 | tf_op jit(solution)/shard_map/ppermute | solution.py:221
  199.3 7.4 %down_terms.1 = f32[128,16,128]{2,1,0:T(8,128)} custom-call(s32[2]{0:T(128)} %pad_add_fusion.place, s32[16]{0:T(128)} %fusion.23.spot, s32[128]{0:T(128)} %fusion.6.where.down_where, bf16[64,128,128]{2,1,0:T(8,128)(2,1)} %get-tuple-element.69.a, bf16[8,128,256]{2,1,0:T(8,128)(2,1)} %get-tuple-element.70.g0, bf16[8,128,256]{2,1,0:T(8,128)(2,1)} %collective-permute-done.35.g1, ...), custom_call_target="tpu_custom_call" | custom-call | flops 1100000000 | bytes 6291456 | tf_op jit(solution)/shard_map/down_terms/pallas_call | solution.py:38
  (133 shorter events, 62.5 us)
Async XLA Ops:
  22.7 21.9 %collective-permute-start.7 = (bf16[2,128,256]{2,1,0:T(8,128)(2,1)S(1)}, bf16[2,128,256]{2,1,0:T(8,128)(2,1)S(1)}, u32[]{:S(2)}, u32[]{:S(2)}) collective-permute-start(bf16[2,128,256]{2,1,0:T(8,128)(2,1)S(1)} %get-tuple-element.54.g0), channel_id=1, source_target_pairs={{0,2},{1,3},{2,0},{3,1},{4,6},{5,7},{6,4},{7,5},{8,10},{9,11},{10,... | collective-permute-start | bytes 393224 | tf_op jit(solution)/shard_map/ppermute | solution.py:217
  24.4 20.2 %collective-permute-start.8 = (bf16[2,128,256]{2,1,0:T(8,128)(2,1)S(1)}, bf16[2,128,256]{2,1,0:T(8,128)(2,1)S(1)}, u32[]{:S(2)}, u32[]{:S(2)}) collective-permute-start(bf16[2,128,256]{2,1,0:T(8,128)(2,1)S(1)} %get-tuple-element.54.g0), channel_id=1, source_target_pairs={{0,1},{1,2},{2,3},{3,0},{4,5},{5,6},{6,7},{7,4},{8,9},{9,10},{10,1... | collective-permute-start | bytes 393224 | tf_op jit(solution)/shard_map/ppermute | solution.py:217
  36.1 16.2 %collective-permute-start.12 = (bf16[8,128,128]{2,1,0:T(8,128)(2,1)}, bf16[8,128,128]{2,1,0:T(8,128)(2,1)S(1)}, u32[]{:S(2)}, u32[]{:S(2)}) collective-permute-start(bf16[8,128,128]{2,1,0:T(8,128)(2,1)} %get-tuple-element.46), channel_id=1, source_target_pairs={{0,16},{8,24},{16,0},{24,8},{1,17},{9,25},{17,1},{25,9},{2,18},{10... | collective-permute-start | bytes 786440 | tf_op jit(solution)/shard_map/ppermute | solution.py:217
  38.8 13.5 %collective-permute-start.13 = (bf16[8,128,128]{2,1,0:T(8,128)(2,1)}, bf16[8,128,128]{2,1,0:T(8,128)(2,1)S(1)}, u32[]{:S(2)}, u32[]{:S(2)}) collective-permute-start(bf16[8,128,128]{2,1,0:T(8,128)(2,1)} %get-tuple-element.47), channel_id=1, source_target_pairs={{0,24},{8,0},{16,8},{24,16},{1,25},{9,1},{17,9},{25,17},{2,26},{10... | collective-permute-start | bytes 786440 | tf_op jit(solution)/shard_map/ppermute | solution.py:217
  52.1 16.4 %collective-permute-start.14 = (bf16[8,128,256]{2,1,0:T(8,128)(2,1)S(1)}, bf16[8,128,256]{2,1,0:T(8,128)(2,1)S(1)}, u32[]{:S(2)}, u32[]{:S(2)}) collective-permute-start(bf16[8,128,256]{2,1,0:T(8,128)(2,1)S(1)} %copy-done.10), channel_id=1, source_target_pairs={{0,32},{32,0},{1,33},{33,1},{2,34},{34,2},{3,35},{35,3},{4,36},{36... | collective-permute-start | bytes 1572872 | tf_op jit(solution)/shard_map/ppermute | solution.py:221
  55.9 23.0 %all-to-all-start = ((bf16[8,8,16,128]{3,2,1,0:T(8,128)(2,1)}), bf16[8,8,16,128]{3,2,1,0:T(8,128)(2,1)S(1)}, u32[]{:S(2)}, u32[]{:S(2)}) async-start(bf16[8,8,16,128]{3,2,1,0:T(8,128)(2,1)} %get-tuple-element.50), calls=%async_computation | async-start | bytes 524288 | tf_op jit(solution)/shard_map/all_to_all | solution.py:293
  63.0 15.9 %collective-permute-start.16 = (bf16[2,2,128,256]{3,2,1,0:T(8,128)(2,1)}, bf16[2,2,128,256]{3,2,1,0:T(8,128)(2,1)}, u32[]{:S(2)}, u32[]{:S(2)}) collective-permute-start(bf16[2,2,128,256]{3,2,1,0:T(8,128)(2,1)} %pad_maximum_fusion.3), channel_id=1, source_target_pairs={{0,128},{64,192},{128,0},{192,64},{1,129},{65,193},{129,1},{193,65... | collective-permute-start | bytes 786440 | tf_op jit(solution)/shard_map/ppermute | solution.py:225
  65.4 13.5 %collective-permute-start.11 = (bf16[8,128,128]{2,1,0:T(8,128)(2,1)}, bf16[8,128,128]{2,1,0:T(8,128)(2,1)}, u32[]{:S(2)}, u32[]{:S(2)}) collective-permute-start(bf16[8,128,128]{2,1,0:T(8,128)(2,1)} %get-tuple-element.44), channel_id=1, source_target_pairs={{0,24},{8,0},{16,8},{24,16},{1,25},{9,1},{17,9},{25,17},{2,26},{10... | collective-permute-start | bytes 786440 | tf_op jit(solution)/shard_map/ppermute | solution.py:217
  66.9 14.3 %collective-permute-start.9 = (bf16[8,128,128]{2,1,0:T(8,128)(2,1)}, bf16[8,128,128]{2,1,0:T(8,128)(2,1)}, u32[]{:S(2)}, u32[]{:S(2)}) collective-permute-start(bf16[8,128,128]{2,1,0:T(8,128)(2,1)} %get-tuple-element.42), channel_id=1, source_target_pairs={{0,8},{8,16},{16,24},{24,0},{1,9},{9,17},{17,25},{25,1},{2,10},{10... | collective-permute-start | bytes 786440 | tf_op jit(solution)/shard_map/ppermute | solution.py:217
  82.5 15.1 %collective-permute-start.19 = (bf16[8,128,128]{2,1,0:T(8,128)(2,1)S(1)}, bf16[8,128,128]{2,1,0:T(8,128)(2,1)S(1)}, u32[]{:S(2)}, u32[]{:S(2)}) collective-permute-start(bf16[8,128,128]{2,1,0:T(8,128)(2,1)S(1)} %multiply_convert_fusion), channel_id=1, source_target_pairs={{0,8},{8,16},{16,24},{24,0},{1,9},{9,17},{17,25},{25,1},{2,10},{10... | collective-permute-start | bytes 786440 | tf_op jit(solution)/shard_map/ppermute | solution.py:217
  82.6 15.0 %collective-permute-start.18 = (bf16[8,128,128]{2,1,0:T(8,128)(2,1)S(1)}, bf16[8,128,128]{2,1,0:T(8,128)(2,1)S(1)}, u32[]{:S(2)}, u32[]{:S(2)}) collective-permute-start(bf16[8,128,128]{2,1,0:T(8,128)(2,1)S(1)} %multiply_convert_fusion), channel_id=1, source_target_pairs={{0,16},{8,24},{16,0},{24,8},{1,17},{9,25},{17,1},{25,9},{2,18},{10... | collective-permute-start | bytes 786440 | tf_op jit(solution)/shard_map/ppermute | solution.py:217
  85.0 13.3 %collective-permute-start.17 = (bf16[8,128,128]{2,1,0:T(8,128)(2,1)S(1)}, bf16[8,128,128]{2,1,0:T(8,128)(2,1)S(1)}, u32[]{:S(2)}, u32[]{:S(2)}) collective-permute-start(bf16[8,128,128]{2,1,0:T(8,128)(2,1)S(1)} %multiply_convert_fusion), channel_id=1, source_target_pairs={{0,24},{8,0},{16,8},{24,16},{1,25},{9,1},{17,9},{25,17},{2,26},{10... | collective-permute-start | bytes 786440 | tf_op jit(solution)/shard_map/ppermute | solution.py:217
  99.8 21.2 %collective-permute-start.23 = (bf16[1,3,2,128,256]{4,3,2,1,0:T(8,128)(2,1)S(1)}, bf16[1,3,2,128,256]{4,3,2,1,0:T(8,128)(2,1)}, u32[]{:S(2)}, u32[]{:S(2)}) collective-permute-start(bf16[1,3,2,128,256]{4,3,2,1,0:T(8,128)(2,1)S(1)} %maximum_bitcast_fusion), channel_id=1, source_target_pairs={{0,2},{1,3},{2,0},{3,1},{4,6},{5,7},{6,4},{7,5},{8,10},{9,11},{10,... | collective-permute-start | bytes 1179656 | tf_op jit(solution)/shard_map/ppermute | solution.py:217
  110.6 17.0 %collective-permute-start.22 = (bf16[2,64,16,128]{3,2,1,0:T(8,128)(2,1)}, bf16[2,64,16,128]{3,2,1,0:T(8,128)(2,1)S(1)}, u32[]{:S(2)}, u32[]{:S(2)}) collective-permute-start(bf16[2,64,16,128]{3,2,1,0:T(8,128)(2,1)} %get-tuple-element.58), channel_id=1, source_target_pairs={{0,64},{64,0},{128,192},{192,128},{1,65},{65,1},{129,193},{193,129... | collective-permute-start | bytes 1572872 | tf_op jit(solution)/shard_map/ppermute | solution.py:225
  122.5 24.8 %collective-permute-start.25 = (bf16[16,128,128]{2,1,0:T(8,128)(2,1)S(1)}, bf16[16,128,128]{2,1,0:T(8,128)(2,1)S(1)}, u32[]{:S(2)}, u32[]{:S(2)}) collective-permute-start(bf16[16,128,128]{2,1,0:T(8,128)(2,1)S(1)} %copy-done.2), channel_id=1, source_target_pairs={{0,24},{8,0},{16,8},{24,16},{1,25},{9,1},{17,9},{25,17},{2,26},{10... | collective-permute-start | bytes 1572872 | tf_op jit(solution)/shard_map/ppermute | solution.py:217
  124.9 22.4 %collective-permute-start.26 = (bf16[16,128,128]{2,1,0:T(8,128)(2,1)S(1)}, bf16[16,128,128]{2,1,0:T(8,128)(2,1)S(1)}, u32[]{:S(2)}, u32[]{:S(2)}) collective-permute-start(bf16[16,128,128]{2,1,0:T(8,128)(2,1)S(1)} %copy-done.2), channel_id=1, source_target_pairs={{0,16},{8,24},{16,0},{24,8},{1,17},{9,25},{17,1},{25,9},{2,18},{10... | collective-permute-start | bytes 1572872 | tf_op jit(solution)/shard_map/ppermute | solution.py:217
  125.4 25.6 %collective-permute-start.27 = (bf16[16,128,128]{2,1,0:T(8,128)(2,1)S(1)}, bf16[16,128,128]{2,1,0:T(8,128)(2,1)}, u32[]{:S(2)}, u32[]{:S(2)}) collective-permute-start(bf16[16,128,128]{2,1,0:T(8,128)(2,1)S(1)} %copy-done.2), channel_id=1, source_target_pairs={{0,8},{8,16},{16,24},{24,0},{1,9},{9,17},{17,25},{25,1},{2,10},{10... | collective-permute-start | bytes 1572872 | tf_op jit(solution)/shard_map/ppermute | solution.py:217
  126.5 37.4 %collective-permute-start.33 = (bf16[2,64,16,128]{3,2,1,0:T(8,128)(2,1)}, bf16[2,64,16,128]{3,2,1,0:T(8,128)(2,1)}, u32[]{:S(2)}, u32[]{:S(2)}) collective-permute-start(bf16[2,64,16,128]{3,2,1,0:T(8,128)(2,1)} %get-tuple-element.68), channel_id=1, source_target_pairs={{0,64},{64,0},{128,192},{192,128},{1,65},{65,1},{129,193},{193,129... | collective-permute-start | bytes 1572872 | tf_op jit(solution)/shard_map/ppermute | solution.py:225
  127.6 71.7 %collective-permute-start.36 = (bf16[4,3,2,128,256]{4,3,2,1,0:T(8,128)(2,1)S(1)}, bf16[4,3,2,128,256]{4,3,2,1,0:T(8,128)(2,1)}, u32[]{:S(2)}, u32[]{:S(2)}) collective-permute-start(bf16[4,3,2,128,256]{4,3,2,1,0:T(8,128)(2,1)S(1)} %pad_maximum_fusion.f0), channel_id=1, source_target_pairs={{0,32},{32,0},{1,33},{33,1},{2,34},{34,2},{3,35},{35,3},{4,36},{36... | collective-permute-start | bytes 4718600 | tf_op jit(solution)/shard_map/ppermute | solution.py:221
  161.5 14.1 %collective-permute-start.28 = (bf16[2,2,128,256]{3,2,1,0:T(8,128)(2,1)}, bf16[2,2,128,256]{3,2,1,0:T(8,128)(2,1)S(1)}, u32[]{:S(2)}, u32[]{:S(2)}) collective-permute-start(bf16[2,2,128,256]{3,2,1,0:T(8,128)(2,1)} %get-tuple-element.63), channel_id=1, source_target_pairs={{0,1},{1,2},{2,3},{3,0},{4,5},{5,6},{6,7},{7,4},{8,9},{9,10},{10,1... | collective-permute-start | bytes 786440 | tf_op jit(solution)/shard_map/ppermute | solution.py:217
  163.9 17.0 %collective-permute-start.32 = (bf16[64,16,128]{2,1,0:T(8,128)(2,1)S(1)}, bf16[64,16,128]{2,1,0:T(8,128)(2,1)S(1)}, u32[]{:S(2)}, u32[]{:S(2)}) collective-permute-start(bf16[64,16,128]{2,1,0:T(8,128)(2,1)S(1)} %fusion), channel_id=1, source_target_pairs={{0,128},{64,192},{128,0},{192,64},{1,129},{65,193},{129,1},{193,65... | collective-permute-start | bytes 786440 | tf_op jit(solution)/shard_map/ppermute | solution.py:225
  169.4 19.5 %collective-permute-start.34 = (bf16[64,16,128]{2,1,0:T(8,128)(2,1)S(1)}, bf16[64,16,128]{2,1,0:T(8,128)(2,1)}, u32[]{:S(2)}, u32[]{:S(2)}) collective-permute-start(bf16[64,16,128]{2,1,0:T(8,128)(2,1)S(1)} %fusion.1), channel_id=1, source_target_pairs={{0,128},{64,192},{128,0},{192,64},{1,129},{65,193},{129,1},{193,65... | collective-permute-start | bytes 786440 | tf_op jit(solution)/shard_map/ppermute | solution.py:225
  176.5 21.1 %collective-permute-start.31 = (bf16[2,128,256]{2,1,0:T(8,128)(2,1)S(1)}, bf16[2,128,256]{2,1,0:T(8,128)(2,1)}, u32[]{:S(2)}, u32[]{:S(2)}) collective-permute-start(bf16[2,128,256]{2,1,0:T(8,128)(2,1)S(1)} %fusion.4), channel_id=1, source_target_pairs={{0,4},{4,0},{1,5},{5,1},{2,6},{6,2},{3,7},{7,3},{8,12},{12,8},{9,1... | collective-permute-start | bytes 393224 | tf_op jit(solution)/shard_map/ppermute | solution.py:221
  180.8 18.5 %collective-permute-start.35 = (bf16[8,128,256]{2,1,0:T(8,128)(2,1)}, bf16[8,128,256]{2,1,0:T(8,128)(2,1)}, u32[]{:S(2)}, u32[]{:S(2)}) collective-permute-start(bf16[8,128,256]{2,1,0:T(8,128)(2,1)} %get-tuple-element.70.g0), channel_id=1, source_target_pairs={{0,32},{32,0},{1,33},{33,1},{2,34},{34,2},{3,35},{35,3},{4,36},{36... | collective-permute-start | bytes 1572872 | tf_op jit(solution)/shard_map/ppermute | solution.py:221
  (40 other events, 383.2 us)
where the time goes:
time: 208 us; the launch traced here: 207 us
  waiting for transfers between devices  81 us (39%)
  starting transfers between devices  58.3 us (28%)
  Pallas kernels  43.1 us (21%)
  other arithmetic  16 us (8%)
  local copies, waits for them, and re-layouts  7.34 us (4%)
    ppermute x24, waiting for transfers between devices, shift(): return lax.ppermute(value, axis, [(i, (i + by) % 4) for i in range(4)])  54.9 us
    pallas_call x8, Pallas kernels, call(): pl.pallas_call(kernel, out_shape=outs, in_specs=[SMEM] * len(scalars) + [...  43.1 us
    ppermute x24, starting transfers between devices, shift(): return lax.ppermute(value, axis, [(i, (i + by) % 4) for i in range(4)])  36.3 us
    ppermute x6, waiting for transfers between devices, across(): return lax.ppermute(value, 'z', [(i, i ^ by) for i in range(4)])  15.1 us
    ppermute x7, starting transfers between devices, swap(): return lax.ppermute(value, axis, [(0, 1), (1, 0)])  11 us
    ppermute x7, waiting for transfers between devices, swap(): return lax.ppermute(value, axis, [(0, 1), (1, 0)])  11 us
    unnamed x52, local copies, waits for them, and re-layouts  6.66 us
    ppermute x6, starting transfers between devices, across(): return lax.ppermute(value, 'z', [(i, i ^ by) for i in range(4)])  5.51 us
  transfers between devices with their start and end apart: 38, of which 14 were waited for; matrix products, arithmetic and copies ran while one was open for 7% of the time, Pallas kernels for 17%

commit v1 on v0

v1 whole, which is shorter than its diff:
```python
import jax
import jax.numpy as jnp
from jax import lax
from jax.experimental import pallas as pl
from jax.experimental.pallas import tpu as pltpu
from jax.sharding import Mesh
from jax.sharding import PartitionSpec as P

KB = 4
KB2 = 8
BS = 128
ROWS = 16
COLS = 32
BF = jnp.bfloat16
F32 = jnp.float32

gelu_scale = 0.7978845608028654
cubic_term = 0.044715


def gelu_both(values):
    tangent = jnp.tanh(gelu_scale * (values + cubic_term * values * values * values))
    value = 0.5 * values * (1.0 + tangent)
    slope = 0.5 * (1.0 + tangent) + 0.5 * values * (1.0 - tangent * tangent) * gelu_scale * (
        1.0 + 3.0 * cubic_term * values * values
    )
    return value, slope


SMEM = pl.BlockSpec(memory_space=pltpu.SMEM)
VMEM = pl.BlockSpec(memory_space=pltpu.VMEM)


def call(kernel, scalars, arrays, outs, scratch=(), name=None):
    return pl.pallas_call(
        kernel,
        out_shape=outs,
        in_specs=[SMEM] * len(scalars) + [VMEM] * len(arrays),
        out_specs=[VMEM] * len(outs),
        scratch_shapes=list(scratch),
        compiler_params=pltpu.CompilerParams(vmem_limit_bytes=28 * 2**20),
        cost_estimate=pl.CostEstimate(flops=1024, bytes_accessed=1024, transcendentals=0),
        name=name,
    )(*scalars, *arrays)


def lanes(half):
    return pl.ds(pl.multiple_of(half * BS, BS), BS)


def block(ref, at):
    return ref[at // 2, :, lanes(at % 2)]


def add_back(acc, run, where, width, rows, w):
    rhs = w[pl.ds(run * width, width)].reshape(width * BS, BS)
    got = lax.dot_general(rows, rhs, (((1,), (1,)), ((), ())), preferred_element_type=F32)
    for k in range(width):
        at = where[run * width + k]
        acc[at] = acc[at] + got[:, k * BS:(k + 1) * BS]


def first_kernel(order, spot, up_where, down_where, x0, x1, x2, x3, g0, g1, g2, g3, w1, w2, *rest):
    outs, x, g, acc = rest[:4], *rest[4:]
    for n, piece in enumerate((x0, x1, x2, x3)):
        x[n * 2:n * 2 + 2] = piece[...]
    for n, piece in enumerate((g0, g1, g2, g3)):
        g[n * 2:n * 2 + 2] = piece[...]
    acc[...] = jnp.zeros_like(acc)

    def back(i, carry):
        add_back(acc, i, down_where, KB2, block(g, spot[i]), w2)
        return carry

    lax.fori_loop(0, ROWS, back, 0, unroll=2)
    for slot, out in enumerate(outs):
        out[1] = acc[slot * 8:(slot + 1) * 8].astype(BF)

        def up(jj, carry):
            j = order[slot * 8 + jj]
            lhs = jnp.concatenate([block(x, up_where[j * KB + k]) for k in range(KB)], axis=1)
            rhs = w1[pl.ds(j * KB, KB)].reshape(KB * BS, BS)
            out[0, jj] = jnp.dot(lhs, rhs, preferred_element_type=F32).astype(BF)
            return carry

        lax.fori_loop(0, 8, up, 0, unroll=4)


def act_kernel(p0, p1, p2, p3, active, own, rows):
    def step(b, carry):
        hidden, grad = (
            p0[n, b].astype(F32) + p1[n, b].astype(F32) + p2[n, b].astype(F32) + p3[n, b].astype(F32) for n in range(2)
        )
        value, slope = gelu_both(hidden)
        own[b] = (grad * slope).astype(BF)
        value = value.astype(BF)
        active[b] = value
        turned = value.T.reshape(8, 16, BS)
        for d in range(8):
            rows[d, b] = turned[d]
        return carry

    lax.fori_loop(0, 8, step, 0, unroll=2)


def turn_kernel(place, x, x2, out):
    z, q = place[0], place[1]

    def step(p, carry):
        for half in range(2):
            for group, ref in enumerate((x, x2)):
                rows = ref[p, :, half * BS:(half + 1) * BS].T.reshape(4, 2, 16, BS)
                for zz in range(4):
                    mine = jnp.where(q == 0, rows[zz, 0], rows[zz, 1])
                    out[p * 2 + half, jnp.bitwise_xor(zz, z), :, group * BS:(group + 1) * BS] = mine
        return carry

    lax.fori_loop(0, 8, step, 0, unroll=2)


def up_terms_kernel(spot, where, xt, v0, v1, *outs):
    for chunk in range(2):
        near, far = outs[chunk * 2:chunk * 2 + 2]

        def step(n, carry):
            j = chunk * 16 + n
            at = spot[j]
            lhs = jnp.concatenate([xt[where[j * KB + k]].reshape(64, 2 * BS) for k in range(KB)], axis=0)
            rhs = jnp.concatenate([v0[at], v1[at]], axis=0)
            got = jnp.dot(lhs, rhs, preferred_element_type=F32).astype(BF).reshape(KB, 4, 16, BS)
            for s, out in enumerate((near, far, near, far)):
                out[s // 2, pl.ds(n * KB, KB)] = got[:, s]
            return carry

        lax.fori_loop(0, 16, step, 0, unroll=2)


def into_kernel(spot, where, v, w, o0, o1, o2, o3, acc):
    acc[...] = jnp.zeros_like(acc)

    def step(j, carry):
        add_back(acc, j, where, KB, v[spot[j]], w)
        return carry

    lax.fori_loop(0, COLS, step, 0, unroll=4)
    for slot, out in enumerate((o0, o1, o2, o3)):
        for t in range(2):
            for half in range(2):
                out[t, :, half * BS:(half + 1) * BS] = acc[slot * 4 + t * 2 + half].astype(BF)


def down_kernel(order, where, a0, a1, a2, a3, w, o0, o1, o2, o3, a):
    for n, piece in enumerate((a0, a1, a2, a3)):
        a[n * 16:n * 16 + 16] = piece[...]
    for slot, out in enumerate((o0, o1, o2, o3)):
        for t in range(2):
            for half in range(2):
                i = order[slot * 4 + t * 2 + half]
                runs = [where[i * KB2 + k] for k in range(KB2)]
                lhs = jnp.concatenate([a[u // 8 * 16 + u % 8] for u in runs], axis=1)
                rhs = w[pl.ds(i * KB2, KB2)].reshape(KB2 * BS, BS)
                out[t, :, half * BS:(half + 1) * BS] = jnp.dot(lhs, rhs, preferred_element_type=F32).astype(BF)


def down_terms_kernel(place, spot, where, a, g0, g1, f0, f1, out):
    z, q = place[0], place[1]

    def step(i, carry):
        at = spot[i]
        runs = [where[i * KB2 + k] for k in range(KB2)]
        lhs, rhs = [], []
        for tq, (g, f) in enumerate(((g0, f0), (g1, f1))):
            for tz in range(4):
                source = jnp.bitwise_xor(z, tz) * 2 + jnp.bitwise_xor(q, tq) + 8
                lhs.append(jnp.concatenate(
                    [a[u // 8 * 16 + source, pl.ds(pl.multiple_of(u % 8 * 16, 16), 16), :] for u in runs], axis=0
                ))
                rhs.append(block(g, at) if tz == 0 else f[at // 4, tz - 1, at // 2 % 2, :, lanes(at % 2)])
        got = jnp.dot(jnp.concatenate(lhs, axis=1), jnp.concatenate(rhs, axis=0), preferred_element_type=F32)
        out[pl.ds(i * KB2, KB2)] = got.reshape(KB2, 16, BS)
        return carry

    lax.fori_loop(0, ROWS, step, 0, unroll=2)


def close_kernel(n0, r0, s0, n1, r1, s1, out):
    for chunk, (near, got, last) in enumerate(((n0, r0, s0), (n1, r1, s1))):
        out[chunk * 64:chunk * 64 + 64] = near[0].astype(F32) + got[0].astype(F32) + last[...].astype(F32)


def shift(value, axis, by):
    return lax.ppermute(value, axis, [(i, (i + by) % 4) for i in range(4)])


def swap(value, axis):
    return lax.ppermute(value, axis, [(0, 1), (1, 0)])


def across(value, by):
    return lax.ppermute(value, "z", [(i, i ^ by) for i in range(4)])


def after(value, *events):
    return lax.optimization_barrier((value, *events))[0]


def pieces(own, axis):
    return [own] + [shift(own, axis, -s) for s in (1, 2, 3)]


def exchange(parts, axis):
    return [parts[0]] + [shift(parts[s], axis, s) for s in (1, 2, 3)]


def scatter_features(parts):
    mine = total(exchange(parts, "y"))
    return (mine[0] + swap(mine[1].astype(BF), "h").astype(F32)).astype(BF)


def total(parts):
    return sum((p.astype(F32) for p in parts[1:]), parts[0].astype(F32))


def local(inputs, grad_out, up_blocks, up_index, down_blocks, down_index):
    z, q, r, h, y = (lax.axis_index(a).astype(jnp.int32) for a in ("z", "q", "row", "h", "y"))
    place = jnp.stack([z, q])
    c = h * 4 + y

    def feature_spot(b):
        return ((b // 2 % 4 - y) % 4) * 4 + jnp.bitwise_xor(b // 8, h) * 2 + b % 2

    def feature_at(s):
        return jnp.bitwise_xor(s // 2 % 2, h) * 8 + ((s // 4 + y) % 4) * 2 + s % 2

    def hidden_spot(f):
        return ((f // 8 - r) % 4) * 8 + f % 8

    def hidden_at(s):
        return ((s // 8 + r) % 4) * 8 + s % 8

    features, units = jnp.arange(ROWS, dtype=jnp.int32), jnp.arange(COLS, dtype=jnp.int32)
    up_where = feature_spot(up_index - r * ROWS)
    down_where = hidden_spot(down_index - c * COLS)
    feature_spots, feature_order = feature_spot(features), feature_at(features)
    hidden_spots, hidden_order = hidden_spot(units), hidden_at(units)

    def shape(*dims, dtype=BF):
        return jax.ShapeDtypeStruct(dims, dtype)

    x_own = jnp.stack([inputs, swap(inputs, "h")])
    g_own = jnp.stack([grad_out, swap(grad_out, "h")])
    panel, piece = shape(8, BS, 2 * BS), shape(8, BS, BS)

    *parts, x, g = call(
        first_kernel, (hidden_order, feature_spots, up_where, down_where),
        (*pieces(x_own, "y"), *pieces(g_own, "y"), up_blocks, down_blocks),
        [shape(2, 8, BS, BS)] * 4 + [panel] * 2, [pltpu.VMEM((COLS, BS, BS), F32)], name="first",
    )
    parts = exchange(parts, "row")
    far1 = across(after(g_own, x), 1)
    far2 = across(jnp.stack([g_own, far1]), 2)
    x2, g2 = swap(x, "q"), swap(g, "q")
    (turned,) = call(turn_kernel, (place,), (x, x2), [shape(ROWS, 4, 16, 2 * BS)], name="turn")
    parts[0] = after(parts[0], turned, far2, g2)
    active, own, rows = call(act_kernel, (), parts, [piece, piece, shape(8, 8, 16, BS)], name="act")

    rows = lax.all_to_all(rows, ("z", "q"), 0, 0, tiled=True)
    hidden = jnp.concatenate(pieces(own, "row"), axis=0)
    far = pieces(after(jnp.concatenate([far1[None], far2])[None], own), "y")
    hidden2 = swap(after(hidden, rows, *far[1:]), "q")

    slab = shape(2, BS, 2 * BS)
    into = call(
        into_kernel, (hidden_spots, up_where), (hidden, up_blocks), [slab] * 4, [pltpu.VMEM((ROWS, BS, BS), F32)], name="into"
    )
    turned = after(turned, into[0])
    near0, send0, near1, send1 = call(
        up_terms_kernel, (hidden_spots, up_where), (turned, hidden, hidden2), [shape(2, 64, 16, BS)] * 4, name="up_terms"
    )
    got0, got1 = across(send0, 1), across(send1, 1)
    both = jnp.concatenate([active, rows.reshape(8, BS, BS)])
    both = pieces(after(both, send0), "row")
    last0 = across((near0[1].astype(F32) + got0[1].astype(F32)).astype(BF), 2)
    send2 = (near1[1].astype(F32) + got1[1].astype(F32)).astype(BF)
    last1 = across(send2, 2)
    both[0] = after(both[0], last0, send2)
    *down, a = call(
        down_kernel, (feature_order, down_where), (*both, down_blocks), [slab] * 4 + [shape(64, BS, BS)], name="down"
    )
    outputs = scatter_features(down)
    grad_in = scatter_features(lax.optimization_barrier((*into, got0))[:4])

    far = jnp.concatenate(far, axis=0)
    far3 = swap(after(far, got0), "q")
    (grad_down,) = call(
        down_terms_kernel, (place, feature_spots, down_where), (a, g, g2, far, far3),
        [shape(128, 16, BS, dtype=F32)], name="down_terms",
    )
    (grad_up,) = call(
        close_kernel, (), (after(near0, grad_down), got0, last0, near1, got1, last1), [shape(128, 16, BS, dtype=F32)], name="close"
    )
    return outputs, grad_in, grad_up, grad_down


def solution(mesh):
    fine = Mesh(mesh.devices.reshape(4, 2, 4, 2, 4), ("z", "q", "row", "h", "y"))
    tokens, width = ("z", "q"), ("row", "h", "y")
    placed = (
        P(tokens, width),
        P(tokens, width),
        P(width, None, None),
        P(width),
        P(width, None, None),
        P(width),
    )
    return jax.shard_map(
        local,
        mesh=fine,
        in_specs=placed,
        out_specs=(P(tokens, width), P(tokens, width), P(width, tokens, None), P(width, tokens, None)),
        check_vma=False,
    )
```

time: 208 us -> 188 us (0.904)
  Pallas kernels: 43.1 us -> 27.6 us
  starting transfers between devices: 58.3 us -> 70.6 us
  other arithmetic: 16 us -> 4.94 us
  waiting for transfers between devices: 81 us -> 72.2 us
  local copies, waits for them, and re-layouts: 7.34 us -> 11.4 us
    ppermute x24, waiting for transfers between devices: 54.9 us -> 24.3 us  [shift(): return lax.ppermute(value, axis, [(i, (i + by) % 4) for i in range(4)])]
    ppermute x6, waiting for transfers between devices: 15.1 us -> 37.4 us  [across(): return lax.ppermute(value, 'z', [(i, i ^ by) for i in range(4)])]
    pallas_call x8, Pallas kernels: 43.1 us -> 27.6 us  [call(): pl.pallas_call(kernel, out_shape=outs, in_specs=[SMEM] * len(scalars) + [...]
    ppermute x7 -> x8, starting transfers between devices: 11 us -> 16 us  [swap(): return lax.ppermute(value, axis, [(0, 1), (1, 0)])]
    ppermute x24, starting transfers between devices: 36.3 us -> 40.9 us  [shift(): return lax.ppermute(value, axis, [(i, (i + by) % 4) for i in range(4)])]
    unnamed x52 -> x22, local copies, waits for them, and re-layouts: 6.66 us -> 10.3 us
    ppermute x6, starting transfers between devices: 5.51 us -> 8.46 us  [across(): return lax.ppermute(value, 'z', [(i, i ^ by) for i in range(4)])]
    convert_element_type x3, other arithmetic: 3.46 us -> 1.36 us  [the longest x2 1.29 us: scatter_features(): return (mine[0] + swap(mine[1].astype(BF), 'h').astype(F32)).astype(BF)]
  transfers between devices with their start and end apart: 38 -> 39, of which waited for: 14 -> 17; matrix products, arithmetic and copies ran while one was open for 7% -> 5% of each run, Pallas kernels for 17% -> 7%
where the time goes in v1:
time: 188 us
  waiting for transfers between devices  72.2 us (38%)
  starting transfers between devices  70.6 us (38%)
  Pallas kernels  27.6 us (15%)
  local copies, waits for them, and re-layouts  11.4 us (6%)
  other arithmetic  4.94 us (3%)
    ppermute x24, starting transfers between devices, shift(): return lax.ppermute(value, axis, [(i, (i + by) % 4) for i in range(4)])  40.9 us
    ppermute x6, waiting for transfers between devices, across(): return lax.ppermute(value, 'z', [(i, i ^ by) for i in range(4)])  37.4 us
    pallas_call x8, Pallas kernels, call(): pl.pallas_call(kernel, out_shape=outs, in_specs=[SMEM] * len(scalars) + [...  27.6 us
    ppermute x24, waiting for transfers between devices, shift(): return lax.ppermute(value, axis, [(i, (i + by) % 4) for i in range(4)])  24.3 us
    ppermute x8, starting transfers between devices, swap(): return lax.ppermute(value, axis, [(0, 1), (1, 0)])  16 us
    ppermute x8, waiting for transfers between devices, swap(): return lax.ppermute(value, axis, [(0, 1), (1, 0)])  10.5 us
    unnamed x22, local copies, waits for them, and re-layouts  10.3 us
    ppermute x6, starting transfers between devices, across(): return lax.ppermute(value, 'z', [(i, i ^ by) for i in range(4)])  8.46 us
  transfers between devices with their start and end apart: 39, of which 17 were waited for; matrix products, arithmetic and copies ran while one was open for 5% of the time, Pallas kernels for 7%

profile of v1, /device:TPU:32, one launch (start us, length us, event | category | flops | bytes accessed | tf_op | source)
XLA Modules:
  0.0 187.6 jit_solution(15895093758269560707)
XLA Ops:
  0.6 6.4 %collective-permute-start = (bf16[128,256]{1,0:T(8,128)(2,1)}, bf16[128,256]{1,0:T(8,128)(2,1)S(1)}, u32[]{:S(2)}, u32[]{:S(2)}) collective-permute-start(bf16[128,256]{1,0:T(8,128)(2,1)} %param.6), channel_id=1, source_target_pairs={{0,4},{4,0},{1,5},{5,1},{2,6},{6,2},{3,7},{7,3},{8,12},{12,8},{9,1... | collective-permute-start | bytes 196616 | tf_op jit(solution)/shard_map/ppermute | solution.py:196
  7.1 5.1 %collective-permute-done = bf16[128,256]{1,0:T(8,128)(2,1)S(1)} collective-permute-done((bf16[128,256]{1,0:T(8,128)(2,1)}, bf16[128,256]{1,0:T(8,128)(2,1)S(1)}, u32[]{:S(2)}, u32[]{:S(2)}) %collective-permute-start) | collective-permute-done | bytes 65568 | tf_op jit(solution)/shard_map/ppermute | solution.py:196
  15.4 3.0 %collective-permute-start.2 = (bf16[2,128,256]{2,1,0:T(8,128)(2,1)S(1)}, bf16[2,128,256]{2,1,0:T(8,128)(2,1)S(1)}, u32[]{:S(2)}, u32[]{:S(2)}) collective-permute-start(bf16[2,128,256]{2,1,0:T(8,128)(2,1)S(1)} %pad_maximum_fusion.2.x0), channel_id=1, source_target_pairs={{0,2},{1,3},{2,0},{3,1},{4,6},{5,7},{6,4},{7,5},{8,10},{9,11},{10,... | collective-permute-start | bytes 393224 | tf_op jit(solution)/shard_map/ppermute | solution.py:192
  24.8 3.4 %collective-permute-done.7.g3 = bf16[2,128,256]{2,1,0:T(8,128)(2,1)S(1)} collective-permute-done((bf16[2,128,256]{2,1,0:T(8,128)(2,1)S(1)}, bf16[2,128,256]{2,1,0:T(8,128)(2,1)S(1)}, u32[]{:S(2)}, u32[]{:S(2)}) %collective-permute-start.7) | collective-permute-done | bytes 131104 | tf_op jit(solution)/shard_map/ppermute | solution.py:192
  33.5 7.1 %first.1 = (bf16[2,8,128,128]{3,2,1,0:T(8,128)(2,1)S(1)}, bf16[2,8,128,128]{3,2,1,0:T(8,128)(2,1)}, bf16[2,8,128,128]{3,2,1,0:T(8,128)(2,1)}, bf16[2,8,128,128]{...) custom-call(s32[32]{0:T(128)S(1)} %fusion.19.order, s32[16]{0:T(128)S(1)} %fusion.23.spot, ...), custom_call_target="tpu_custom_call" | custom-call | flops 1024 | bytes 1024 | tf_op jit(solution)/shard_map/first/pallas_call | solution.py:35
  46.6 2.8 %collective-permute-start.14 = (bf16[2,8,128,128]{3,2,1,0:T(8,128)(2,1)}, bf16[2,8,128,128]{3,2,1,0:T(8,128)(2,1)}, u32[]{:S(2)}, u32[]{:S(2)}) collective-permute-start(bf16[2,8,128,128]{3,2,1,0:T(8,128)(2,1)} %get-tuple-element.46), channel_id=1, source_target_pairs={{0,24},{8,0},{16,8},{24,16},{1,25},{9,1},{17,9},{25,17},{2,26},{10... | collective-permute-start | bytes 1572872 | tf_op jit(solution)/shard_map/ppermute | solution.py:192
  52.0 10.2 %collective-permute-done.10 = bf16[2,2,128,256]{3,2,1,0:T(8,128)(2,1)S(1)} collective-permute-done((bf16[2,2,128,256]{3,2,1,0:T(8,128)(2,1)}, bf16[2,2,128,256]{3,2,1,0:T(8,128)(2,1)S(1)}, u32[]{:S(2)}, u32[]{:S(2)}) %collective-permute-start.10) | collective-permute-done | bytes 262176 | tf_op jit(solution)/shard_map/ppermute | solution.py:200
  62.2 6.6 %collective-permute-done.13.p2 = bf16[2,8,128,128]{3,2,1,0:T(8,128)(2,1)S(1)} collective-permute-done((bf16[2,8,128,128]{3,2,1,0:T(8,128)(2,1)}, bf16[2,8,128,128]{3,2,1,0:T(8,128)(2,1)S(1)}, u32[]{:S(2)}, u32[]{:S(2)}) %collective-permute-start.13) | collective-permute-done | bytes 524320 | tf_op jit(solution)/shard_map/ppermute | solution.py:192
  77.5 3.0 %collective-permute-start.19 = (bf16[1,3,2,128,256]{4,3,2,1,0:T(8,128)(2,1)S(1)}, bf16[1,3,2,128,256]{4,3,2,1,0:T(8,128)(2,1)S(1)}, u32[]{:S(2)}, u32[]{:S(2)}) collective-permute-start(bf16[1,3,2,128,256]{4,3,2,1,0:T(8,128)(2,1)S(1)} %maximum_bitcast_fusion), channel_id=1, source_target_pairs={{0,2},{1,3},{2,0},{3,1},{4,6},{5,7},{6,4},{7,5},{8,10},{9,11},{10,... | collective-permute-start | bytes 1179656 | tf_op jit(solution)/shard_map/ppermute | solution.py:192
  80.5 5.3 %all-to-all-start = ((bf16[8,8,16,128]{3,2,1,0:T(8,128)(2,1)}), bf16[8,8,16,128]{3,2,1,0:T(8,128)(2,1)S(1)}, u32[]{:S(2)}, u32[]{:S(2)}) async-start(bf16[8,8,16,128]{3,2,1,0:T(8,128)(2,1)} %get-tuple-element.48), calls=%async_computation | async-start | bytes 524288 | tf_op jit(solution)/shard_map/all_to_all | solution.py:267
  91.4 5.9 %collective-permute-done.19 = bf16[1,3,2,128,256]{4,3,2,1,0:T(8,128)(2,1)S(1)} collective-permute-done((bf16[1,3,2,128,256]{4,3,2,1,0:T(8,128)(2,1)S(1)}, bf16[1,3,2,128,256]{4,3,2,1,0:T(8,128)(2,1)S(1)}, u32[]{:S(2)}, u32[]{:S(2)}) %collective-permute-start.19) | collective-permute-done | bytes 393248 | tf_op jit(solution)/shard_map/ppermute | solution.py:192
  99.6 3.2 %into.1 = (bf16[2,128,256]{2,1,0:T(8,128)(2,1)S(1)}, bf16[2,128,256]{2,1,0:T(8,128)(2,1)S(1)}, bf16[2,128,256]{2,1,0:T(8,128)(2,1)S(1)}, bf16[2,128,256]{2,1,0:T(8,128)(2,1)S(1)}) custom-call(s32[32]{0:T(128)S(1)} %fusion.30.spot, s32[128]{0:T(128)S(1)} %get-tuple-element.77.up_where.where, bf16[32,128,128]{2,1,0:T(8,128)(2,1)S(1)} %constant_dynamic-update-slice_fusion.v.v0, ...), custom_call_target="tpu_custom_call" | custom-call | flops 1024 | bytes 1024 | tf_op jit(solution)/shard_map/into/pallas_call | solution.py:35
  102.8 4.0 %up_terms.1 = (bf16[2,64,16,128]{3,2,1,0:T(8,128)(2,1)S(1)}, bf16[2,64,16,128]{3,2,1,0:T(8,128)(2,1)S(1)}, bf16[2,64,16,128]{3,2,1,0:T(8,128)(2,1)S(1)}, bf16[2,64,16,128]{3,2,1,0:T(8,128)(2,1)S(1)}) custom-call(s32[32]{0:T(128)S(1)} %fusion.30.spot, s32[128]{0:T(128)S(1)} %get-tuple-element.77.up_where.where, bf16[16,4,16,256]{3,2,1,0:T(8,128)(2,1)S(1)} %turn.1.xt, ...), custom_call_target="tpu_custom_call" | custom-call | flops 1024 | bytes 1024 | tf_op jit(solution)/shard_map/up_terms/pallas_call | solution.py:35
  110.2 11.6 %collective-permute-done.22.r0 = bf16[2,64,16,128]{3,2,1,0:T(8,128)(2,1)S(1)} collective-permute-done((bf16[2,64,16,128]{3,2,1,0:T(8,128)(2,1)S(1)}, bf16[2,64,16,128]{3,2,1,0:T(8,128)(2,1)S(1)}, u32[]{:S(2)}, u32[]{:S(2)}) %collective-permute-start.22) | collective-permute-done | bytes 524320 | tf_op jit(solution)/shard_map/ppermute | solution.py:200
  124.2 3.0 %collective-permute-start.26 = (bf16[16,128,128]{2,1,0:T(8,128)(2,1)S(1)}, bf16[16,128,128]{2,1,0:T(8,128)(2,1)S(1)}, u32[]{:S(2)}, u32[]{:S(2)}) collective-permute-start(bf16[16,128,128]{2,1,0:T(8,128)(2,1)S(1)} %pad_maximum_fusion.a0), channel_id=1, source_target_pairs={{0,16},{8,24},{16,0},{24,8},{1,17},{9,25},{17,1},{25,9},{2,18},{10... | collective-permute-start | bytes 1572872 | tf_op jit(solution)/shard_map/ppermute | solution.py:192
  127.5 5.2 %collective-permute-done.24.r1 = bf16[2,64,16,128]{3,2,1,0:T(8,128)(2,1)S(1)} collective-permute-done((bf16[2,64,16,128]{3,2,1,0:T(8,128)(2,1)S(1)}, bf16[2,64,16,128]{3,2,1,0:T(8,128)(2,1)S(1)}, u32[]{:S(2)}, u32[]{:S(2)}) %collective-permute-start.24) | collective-permute-done | bytes 524320 | tf_op jit(solution)/shard_map/ppermute | solution.py:200
  136.4 3.1 %collective-permute-done.33 = bf16[2,128,256]{2,1,0:T(8,128)(2,1)S(1)} collective-permute-done((bf16[2,128,256]{2,1,0:T(8,128)(2,1)S(1)}, bf16[2,128,256]{2,1,0:T(8,128)(2,1)S(1)}, u32[]{:S(2)}, u32[]{:S(2)}) %collective-permute-start.33) | collective-permute-done | bytes 131104 | tf_op jit(solution)/shard_map/ppermute | solution.py:192
  142.3 9.3 %collective-permute-done.23.s0 = bf16[64,16,128]{2,1,0:T(8,128)(2,1)S(1)} collective-permute-done((bf16[64,16,128]{2,1,0:T(8,128)(2,1)S(1)}, bf16[64,16,128]{2,1,0:T(8,128)(2,1)S(1)}, u32[]{:S(2)}, u32[]{:S(2)}) %collective-permute-start.23) | collective-permute-done | bytes 262176 | tf_op jit(solution)/shard_map/ppermute | solution.py:200
  151.6 3.4 %collective-permute-start.37 = (bf16[64,16,128]{2,1,0:T(8,128)(2,1)S(1)}, bf16[64,16,128]{2,1,0:T(8,128)(2,1)S(1)}, u32[]{:S(2)}, u32[]{:S(2)}) collective-permute-start(bf16[64,16,128]{2,1,0:T(8,128)(2,1)S(1)} %fusion.1), channel_id=1, source_target_pairs={{0,128},{64,192},{128,0},{192,64},{1,129},{65,193},{129,1},{193,65... | collective-permute-start | bytes 786440 | tf_op jit(solution)/shard_map/ppermute | solution.py:200
  158.6 3.2 %collective-permute-start.29 = (bf16[2,128,256]{2,1,0:T(8,128)(2,1)S(1)}, bf16[2,128,256]{2,1,0:T(8,128)(2,1)S(1)}, u32[]{:S(2)}, u32[]{:S(2)}) collective-permute-start(bf16[2,128,256]{2,1,0:T(8,128)(2,1)S(1)} %get-tuple-element.62), channel_id=1, source_target_pairs={{0,2},{1,3},{2,0},{3,1},{4,6},{5,7},{6,4},{7,5},{8,10},{9,11},{10,... | collective-permute-start | bytes 393224 | tf_op jit(solution)/shard_map/ppermute | solution.py:192
  161.8 3.0 %collective-permute-done.28 = bf16[2,128,256]{2,1,0:T(8,128)(2,1)S(1)} collective-permute-done((bf16[2,128,256]{2,1,0:T(8,128)(2,1)S(1)}, bf16[2,128,256]{2,1,0:T(8,128)(2,1)S(1)}, u32[]{:S(2)}, u32[]{:S(2)}) %collective-permute-start.28) | collective-permute-done | bytes 131104 | tf_op jit(solution)/shard_map/ppermute | solution.py:192
  164.8 6.6 %collective-permute-start.35 = (bf16[128,256]{1,0:T(8,128)(2,1)S(1)}, bf16[128,256]{1,0:T(8,128)(2,1)S(1)}, u32[]{:S(2)}, u32[]{:S(2)}) collective-permute-start(bf16[128,256]{1,0:T(8,128)(2,1)S(1)} %fusion.7), channel_id=1, source_target_pairs={{0,4},{4,0},{1,5},{5,1},{2,6},{6,2},{3,7},{7,3},{8,12},{12,8},{9,1... | collective-permute-start | bytes 196616 | tf_op jit(solution)/shard_map/ppermute | solution.py:196
  176.4 3.6 %collective-permute-done.31 = bf16[128,256]{1,0:T(8,128)(2,1)S(1)} collective-permute-done((bf16[128,256]{1,0:T(8,128)(2,1)S(1)}, bf16[128,256]{1,0:T(8,128)(2,1)S(1)}, u32[]{:S(2)}, u32[]{:S(2)}) %collective-permute-start.31) | collective-permute-done | bytes 65568 | tf_op jit(solution)/shard_map/ppermute | solution.py:196
  180.6 5.8 %down_terms.1 = f32[128,16,128]{2,1,0:T(8,128)} custom-call(s32[2]{0:T(128)S(1)} %pad_add_fusion.place, s32[16]{0:T(128)S(1)} %fusion.23.spot, s32[128]{0:T(128)S(1)} %get-tuple-element.76.down_where.where, bf16[64,128,128]{2,1,0:T(8,128)(2,1)S(1)} %get-tuple-element.71.a, bf16[8,128,256]{2,1,0:T(8,128)(2,1)} %get-tuple-element.42.g0, ...), custom_call_target="tpu_custom_call" | custom-call | flops 1024 | bytes 1024 | tf_op jit(solution)/shard_map/down_terms/pallas_call | solution.py:35
  (105 shorter events, 63.0 us)
Async XLA Ops:
  0.6 11.6 %collective-permute-start = (bf16[128,256]{1,0:T(8,128)(2,1)}, bf16[128,256]{1,0:T(8,128)(2,1)S(1)}, u32[]{:S(2)}, u32[]{:S(2)}) collective-permute-start(bf16[128,256]{1,0:T(8,128)(2,1)} %param.6), channel_id=1, source_target_pairs={{0,4},{4,0},{1,5},{5,1},{2,6},{6,2},{3,7},{7,3},{8,12},{12,8},{9,1... | collective-permute-start | bytes 196616 | tf_op jit(solution)/shard_map/ppermute | solution.py:196
  7.0 12.7 %collective-permute-start.4 = (bf16[128,256]{1,0:T(8,128)(2,1)}, bf16[128,256]{1,0:T(8,128)(2,1)S(1)}, u32[]{:S(2)}, u32[]{:S(2)}) collective-permute-start(bf16[128,256]{1,0:T(8,128)(2,1)} %param.7), channel_id=1, source_target_pairs={{0,4},{4,0},{1,5},{5,1},{2,6},{6,2},{3,7},{7,3},{8,12},{12,8},{9,1... | collective-permute-start | bytes 196616 | tf_op jit(solution)/shard_map/ppermute | solution.py:196
  40.7 21.5 %collective-permute-start.11 = (bf16[8,128,256]{2,1,0:T(8,128)(2,1)}, bf16[8,128,256]{2,1,0:T(8,128)(2,1)}, u32[]{:S(2)}, u32[]{:S(2)}) collective-permute-start(bf16[8,128,256]{2,1,0:T(8,128)(2,1)} %get-tuple-element.42.g0), channel_id=1, source_target_pairs={{0,32},{32,0},{1,33},{33,1},{2,34},{34,2},{3,35},{35,3},{4,36},{36... | collective-permute-start | bytes 1572872 | tf_op jit(solution)/shard_map/ppermute | solution.py:196
  41.2 21.0 %collective-permute-start.12 = (bf16[2,8,128,128]{3,2,1,0:T(8,128)(2,1)}, bf16[2,8,128,128]{3,2,1,0:T(8,128)(2,1)S(1)}, u32[]{:S(2)}, u32[]{:S(2)}) collective-permute-start(bf16[2,8,128,128]{3,2,1,0:T(8,128)(2,1)} %get-tuple-element.44), channel_id=1, source_target_pairs={{0,8},{8,16},{16,24},{24,0},{1,9},{9,17},{17,25},{25,1},{2,10},{10... | collective-permute-start | bytes 1572872 | tf_op jit(solution)/shard_map/ppermute | solution.py:192
  42.7 26.1 %collective-permute-start.13 = (bf16[2,8,128,128]{3,2,1,0:T(8,128)(2,1)}, bf16[2,8,128,128]{3,2,1,0:T(8,128)(2,1)S(1)}, u32[]{:S(2)}, u32[]{:S(2)}) collective-permute-start(bf16[2,8,128,128]{3,2,1,0:T(8,128)(2,1)} %get-tuple-element.45), channel_id=1, source_target_pairs={{0,16},{8,24},{16,0},{24,8},{1,17},{9,25},{17,1},{25,9},{2,18},{10... | collective-permute-start | bytes 1572872 | tf_op jit(solution)/shard_map/ppermute | solution.py:192
  46.6 22.2 %collective-permute-start.14 = (bf16[2,8,128,128]{3,2,1,0:T(8,128)(2,1)}, bf16[2,8,128,128]{3,2,1,0:T(8,128)(2,1)}, u32[]{:S(2)}, u32[]{:S(2)}) collective-permute-start(bf16[2,8,128,128]{3,2,1,0:T(8,128)(2,1)} %get-tuple-element.46), channel_id=1, source_target_pairs={{0,24},{8,0},{16,8},{24,16},{1,25},{9,1},{17,9},{25,17},{2,26},{10... | collective-permute-start | bytes 1572872 | tf_op jit(solution)/shard_map/ppermute | solution.py:192
  50.1 12.1 %collective-permute-start.10 = (bf16[2,2,128,256]{3,2,1,0:T(8,128)(2,1)}, bf16[2,2,128,256]{3,2,1,0:T(8,128)(2,1)S(1)}, u32[]{:S(2)}, u32[]{:S(2)}) collective-permute-start(bf16[2,2,128,256]{3,2,1,0:T(8,128)(2,1)} %pad_maximum_fusion.1), channel_id=1, source_target_pairs={{0,128},{64,192},{128,0},{192,64},{1,129},{65,193},{129,1},{193,65... | collective-permute-start | bytes 786440 | tf_op jit(solution)/shard_map/ppermute | solution.py:200
  72.1 13.7 %collective-permute-start.15 = (bf16[8,128,128]{2,1,0:T(8,128)(2,1)S(1)}, bf16[8,128,128]{2,1,0:T(8,128)(2,1)}, u32[]{:S(2)}, u32[]{:S(2)}) collective-permute-start(bf16[8,128,128]{2,1,0:T(8,128)(2,1)S(1)} %get-tuple-element.49), channel_id=1, source_target_pairs={{0,24},{8,0},{16,8},{24,16},{1,25},{9,1},{17,9},{25,17},{2,26},{10... | collective-permute-start | bytes 786440 | tf_op jit(solution)/shard_map/ppermute | solution.py:192
  74.4 15.0 %collective-permute-start.16 = (bf16[8,128,128]{2,1,0:T(8,128)(2,1)S(1)}, bf16[8,128,128]{2,1,0:T(8,128)(2,1)}, u32[]{:S(2)}, u32[]{:S(2)}) collective-permute-start(bf16[8,128,128]{2,1,0:T(8,128)(2,1)S(1)} %get-tuple-element.49), channel_id=1, source_target_pairs={{0,16},{8,24},{16,0},{24,8},{1,17},{9,25},{17,1},{25,9},{2,18},{10... | collective-permute-start | bytes 786440 | tf_op jit(solution)/shard_map/ppermute | solution.py:192
  76.3 14.1 %collective-permute-start.17 = (bf16[8,128,128]{2,1,0:T(8,128)(2,1)S(1)}, bf16[8,128,128]{2,1,0:T(8,128)(2,1)}, u32[]{:S(2)}, u32[]{:S(2)}) collective-permute-start(bf16[8,128,128]{2,1,0:T(8,128)(2,1)S(1)} %get-tuple-element.49), channel_id=1, source_target_pairs={{0,8},{8,16},{16,24},{24,0},{1,9},{9,17},{17,25},{25,1},{2,10},{10... | collective-permute-start | bytes 786440 | tf_op jit(solution)/shard_map/ppermute | solution.py:192
  76.4 15.0 %collective-permute-start.20 = (bf16[1,3,2,128,256]{4,3,2,1,0:T(8,128)(2,1)S(1)}, bf16[1,3,2,128,256]{4,3,2,1,0:T(8,128)(2,1)S(1)}, u32[]{:S(2)}, u32[]{:S(2)}) collective-permute-start(bf16[1,3,2,128,256]{4,3,2,1,0:T(8,128)(2,1)S(1)} %maximum_bitcast_fusion), channel_id=1, source_target_pairs={{0,1},{1,2},{2,3},{3,0},{4,5},{5,6},{6,7},{7,4},{8,9},{9,10},{10,1... | collective-permute-start | bytes 1179656 | tf_op jit(solution)/shard_map/ppermute | solution.py:192
  77.5 19.9 %collective-permute-start.19 = (bf16[1,3,2,128,256]{4,3,2,1,0:T(8,128)(2,1)S(1)}, bf16[1,3,2,128,256]{4,3,2,1,0:T(8,128)(2,1)S(1)}, u32[]{:S(2)}, u32[]{:S(2)}) collective-permute-start(bf16[1,3,2,128,256]{4,3,2,1,0:T(8,128)(2,1)S(1)} %maximum_bitcast_fusion), channel_id=1, source_target_pairs={{0,2},{1,3},{2,0},{3,1},{4,6},{5,7},{6,4},{7,5},{8,10},{9,11},{10,... | collective-permute-start | bytes 1179656 | tf_op jit(solution)/shard_map/ppermute | solution.py:192
  80.5 16.9 %all-to-all-start = ((bf16[8,8,16,128]{3,2,1,0:T(8,128)(2,1)}), bf16[8,8,16,128]{3,2,1,0:T(8,128)(2,1)S(1)}, u32[]{:S(2)}, u32[]{:S(2)}) async-start(bf16[8,8,16,128]{3,2,1,0:T(8,128)(2,1)} %get-tuple-element.48), calls=%async_computation | async-start | bytes 524288 | tf_op jit(solution)/shard_map/all_to_all | solution.py:267
  85.8 11.5 %collective-permute-start.18 = (bf16[1,3,2,128,256]{4,3,2,1,0:T(8,128)(2,1)S(1)}, bf16[1,3,2,128,256]{4,3,2,1,0:T(8,128)(2,1)}, u32[]{:S(2)}, u32[]{:S(2)}) collective-permute-start(bf16[1,3,2,128,256]{4,3,2,1,0:T(8,128)(2,1)S(1)} %maximum_bitcast_fusion), channel_id=1, source_target_pairs={{0,3},{1,0},{2,1},{3,2},{4,7},{5,4},{6,5},{7,6},{8,11},{9,8},{10,9... | collective-permute-start | bytes 1179656 | tf_op jit(solution)/shard_map/ppermute | solution.py:192
  106.8 14.9 %collective-permute-start.22 = (bf16[2,64,16,128]{3,2,1,0:T(8,128)(2,1)S(1)}, bf16[2,64,16,128]{3,2,1,0:T(8,128)(2,1)S(1)}, u32[]{:S(2)}, u32[]{:S(2)}) collective-permute-start(bf16[2,64,16,128]{3,2,1,0:T(8,128)(2,1)S(1)} %get-tuple-element.54), channel_id=1, source_target_pairs={{0,64},{64,0},{128,192},{192,128},{1,65},{65,1},{129,193},{193,129... | collective-permute-start | bytes 1572872 | tf_op jit(solution)/shard_map/ppermute | solution.py:200
  108.9 23.8 %collective-permute-start.24 = (bf16[2,64,16,128]{3,2,1,0:T(8,128)(2,1)S(1)}, bf16[2,64,16,128]{3,2,1,0:T(8,128)(2,1)S(1)}, u32[]{:S(2)}, u32[]{:S(2)}) collective-permute-start(bf16[2,64,16,128]{3,2,1,0:T(8,128)(2,1)S(1)} %get-tuple-element.58), channel_id=1, source_target_pairs={{0,64},{64,0},{128,192},{192,128},{1,65},{65,1},{129,193},{193,129... | collective-permute-start | bytes 1572872 | tf_op jit(solution)/shard_map/ppermute | solution.py:200
  121.7 12.5 %collective-permute-start.32 = (bf16[2,128,256]{2,1,0:T(8,128)(2,1)S(1)}, bf16[2,128,256]{2,1,0:T(8,128)(2,1)S(1)}, u32[]{:S(2)}, u32[]{:S(2)}) collective-permute-start(bf16[2,128,256]{2,1,0:T(8,128)(2,1)S(1)} %get-tuple-element.68), channel_id=1, source_target_pairs={{0,1},{1,2},{2,3},{3,0},{4,5},{5,6},{6,7},{7,4},{8,9},{9,10},{10,1... | collective-permute-start | bytes 393224 | tf_op jit(solution)/shard_map/ppermute | solution.py:192
  122.8 32.1 %collective-permute-start.27 = (bf16[16,128,128]{2,1,0:T(8,128)(2,1)S(1)}, bf16[16,128,128]{2,1,0:T(8,128)(2,1)S(1)}, u32[]{:S(2)}, u32[]{:S(2)}) collective-permute-start(bf16[16,128,128]{2,1,0:T(8,128)(2,1)S(1)} %pad_maximum_fusion.a0), channel_id=1, source_target_pairs={{0,8},{8,16},{16,24},{24,0},{1,9},{9,17},{17,25},{25,1},{2,10},{10... | collective-permute-start | bytes 1572872 | tf_op jit(solution)/shard_map/ppermute | solution.py:192
  124.2 30.8 %collective-permute-start.26 = (bf16[16,128,128]{2,1,0:T(8,128)(2,1)S(1)}, bf16[16,128,128]{2,1,0:T(8,128)(2,1)S(1)}, u32[]{:S(2)}, u32[]{:S(2)}) collective-permute-start(bf16[16,128,128]{2,1,0:T(8,128)(2,1)S(1)} %pad_maximum_fusion.a0), channel_id=1, source_target_pairs={{0,16},{8,24},{16,0},{24,8},{1,17},{9,25},{17,1},{25,9},{2,18},{10... | collective-permute-start | bytes 1572872 | tf_op jit(solution)/shard_map/ppermute | solution.py:192
  127.2 27.7 %collective-permute-start.25 = (bf16[16,128,128]{2,1,0:T(8,128)(2,1)S(1)}, bf16[16,128,128]{2,1,0:T(8,128)(2,1)S(1)}, u32[]{:S(2)}, u32[]{:S(2)}) collective-permute-start(bf16[16,128,128]{2,1,0:T(8,128)(2,1)S(1)} %pad_maximum_fusion.a0), channel_id=1, source_target_pairs={{0,24},{8,0},{16,8},{24,16},{1,25},{9,1},{17,9},{25,17},{2,26},{10... | collective-permute-start | bytes 1572872 | tf_op jit(solution)/shard_map/ppermute | solution.py:192
  139.4 12.1 %collective-permute-start.23 = (bf16[64,16,128]{2,1,0:T(8,128)(2,1)S(1)}, bf16[64,16,128]{2,1,0:T(8,128)(2,1)S(1)}, u32[]{:S(2)}, u32[]{:S(2)}) collective-permute-start(bf16[64,16,128]{2,1,0:T(8,128)(2,1)S(1)} %fusion), channel_id=1, source_target_pairs={{0,128},{64,192},{128,0},{192,64},{1,129},{65,193},{129,1},{193,65... | collective-permute-start | bytes 786440 | tf_op jit(solution)/shard_map/ppermute | solution.py:200
  142.1 38.5 %collective-permute-start.36 = (bf16[4,3,2,128,256]{4,3,2,1,0:T(8,128)(2,1)S(1)}, bf16[4,3,2,128,256]{4,3,2,1,0:T(8,128)(2,1)S(1)}, u32[]{:S(2)}, u32[]{:S(2)}) collective-permute-start(bf16[4,3,2,128,256]{4,3,2,1,0:T(8,128)(2,1)S(1)} %constant_dynamic-update-slice_fusion.4.f0), channel_id=1, source_target_pairs={{0,32},{32,0},{1,33},{33,1},{2,34},{34,2},{3,35},{35,3},{4,36},{36... | collective-permute-start | bytes 4718600 | tf_op jit(solution)/shard_map/ppermute | solution.py:196
  151.6 34.9 %collective-permute-start.37 = (bf16[64,16,128]{2,1,0:T(8,128)(2,1)S(1)}, bf16[64,16,128]{2,1,0:T(8,128)(2,1)S(1)}, u32[]{:S(2)}, u32[]{:S(2)}) collective-permute-start(bf16[64,16,128]{2,1,0:T(8,128)(2,1)S(1)} %fusion.1), channel_id=1, source_target_pairs={{0,128},{64,192},{128,0},{192,64},{1,129},{65,193},{129,1},{193,65... | collective-permute-start | bytes 786440 | tf_op jit(solution)/shard_map/ppermute | solution.py:200
  158.6 12.9 %collective-permute-start.29 = (bf16[2,128,256]{2,1,0:T(8,128)(2,1)S(1)}, bf16[2,128,256]{2,1,0:T(8,128)(2,1)S(1)}, u32[]{:S(2)}, u32[]{:S(2)}) collective-permute-start(bf16[2,128,256]{2,1,0:T(8,128)(2,1)S(1)} %get-tuple-element.62), channel_id=1, source_target_pairs={{0,2},{1,3},{2,0},{3,1},{4,6},{5,7},{6,4},{7,5},{8,10},{9,11},{10,... | collective-permute-start | bytes 393224 | tf_op jit(solution)/shard_map/ppermute | solution.py:192
  (23 other events, 185.1 us)

commit v2 on v1

--- a/solution.py
+++ b/solution.py
@@ -38,7 +38,7 @@
         in_specs=[SMEM] * len(scalars) + [VMEM] * len(arrays),
         out_specs=[VMEM] * len(outs),
         scratch_shapes=list(scratch),
-        compiler_params=pltpu.CompilerParams(vmem_limit_bytes=28 * 2**20),
+        compiler_params=pltpu.CompilerParams(vmem_limit_bytes=20 * 2**20),
         cost_estimate=pl.CostEstimate(flops=1024, bytes_accessed=1024, transcendentals=0),
         name=name,
     )(*scalars, *arrays)
@@ -118,21 +118,29 @@
     lax.fori_loop(0, 8, step, 0, unroll=2)
 
 
-def up_terms_kernel(spot, where, xt, v0, v1, *outs):
-    for chunk in range(2):
-        near, far = outs[chunk * 2:chunk * 2 + 2]
-
-        def step(n, carry):
-            j = chunk * 16 + n
-            at = spot[j]
-            lhs = jnp.concatenate([xt[where[j * KB + k]].reshape(64, 2 * BS) for k in range(KB)], axis=0)
-            rhs = jnp.concatenate([v0[at], v1[at]], axis=0)
-            got = jnp.dot(lhs, rhs, preferred_element_type=F32).astype(BF).reshape(KB, 4, 16, BS)
-            for s, out in enumerate((near, far, near, far)):
-                out[s // 2, pl.ds(n * KB, KB)] = got[:, s]
-            return carry
-
-        lax.fori_loop(0, 16, step, 0, unroll=2)
+def join_kernel(p0, p1, p2, p3, out):
+    size = p0.shape[0]
+    for n, piece in enumerate((p0, p1, p2, p3)):
+        out[n * size:(n + 1) * size] = piece[...]
+
+
+def join(parts):
+    first = parts[0]
+    whole = jax.ShapeDtypeStruct((4 * first.shape[0], *first.shape[1:]), first.dtype)
+    return call(join_kernel, (), parts, [whole], name="join")[0]
+
+
+def up_terms_kernel(spot, where, xt, v0, v1, near, far):
+    def step(j, carry):
+        at = spot[j]
+        lhs = jnp.concatenate([xt[where[j * KB + k]].reshape(64, 2 * BS) for k in range(KB)], axis=0)
+        rhs = jnp.concatenate([v0[at], v1[at]], axis=0)
+        got = jnp.dot(lhs, rhs, preferred_element_type=F32).astype(BF).reshape(KB, 4, 16, BS)
+        for s, out in enumerate((near, far, near, far)):
+            out[s // 2, pl.ds(j * KB, KB)] = got[:, s]
+        return carry
+
+    lax.fori_loop(0, COLS, step, 0, unroll=2)
 
 
 def into_kernel(spot, where, v, w, o0, o1, o2, o3, acc):
@@ -183,9 +191,8 @@
     lax.fori_loop(0, ROWS, step, 0, unroll=2)
 
 
-def close_kernel(n0, r0, s0, n1, r1, s1, out):
-    for chunk, (near, got, last) in enumerate(((n0, r0, s0), (n1, r1, s1))):
-        out[chunk * 64:chunk * 64 + 64] = near[0].astype(F32) + got[0].astype(F32) + last[...].astype(F32)
+def close_kernel(near, got, last, out):
+    out[...] = near[0].astype(F32) + got[0].astype(F32) + last[...].astype(F32)
 
 
 def shift(value, axis, by):
@@ -251,54 +258,53 @@
     g_own = jnp.stack([grad_out, swap(grad_out, "h")])
     panel, piece = shape(8, BS, 2 * BS), shape(8, BS, BS)
 
+    far1 = across(after(g_own, x_own), 1)
+    cotangents = pieces(g_own, "y")
+    cotangents[0] = after(cotangents[0], far1)
     *parts, x, g = call(
         first_kernel, (hidden_order, feature_spots, up_where, down_where),
-        (*pieces(x_own, "y"), *pieces(g_own, "y"), up_blocks, down_blocks),
+        (*pieces(x_own, "y"), *cotangents, up_blocks, down_blocks),
         [shape(2, 8, BS, BS)] * 4 + [panel] * 2, [pltpu.VMEM((COLS, BS, BS), F32)], name="first",
     )
     parts = exchange(parts, "row")
-    far1 = across(after(g_own, x), 1)
-    far2 = across(jnp.stack([g_own, far1]), 2)
-    x2, g2 = swap(x, "q"), swap(g, "q")
+    far2 = across(after(jnp.stack([g_own, far1]), x), 2)
+    x2 = swap(x, "q")
     (turned,) = call(turn_kernel, (place,), (x, x2), [shape(ROWS, 4, 16, 2 * BS)], name="turn")
-    parts[0] = after(parts[0], turned, far2, g2)
+    parts[0] = after(parts[0], far2, turned)
     active, own, rows = call(act_kernel, (), parts, [piece, piece, shape(8, 8, 16, BS)], name="act")
-
+    far = pieces(after(jnp.concatenate([far1[None], far2])[None], own), "y")
     rows = lax.all_to_all(rows, ("z", "q"), 0, 0, tiled=True)
-    hidden = jnp.concatenate(pieces(own, "row"), axis=0)
-    far = pieces(after(jnp.concatenate([far1[None], far2])[None], own), "y")
+    hidden = join(pieces(own, "row"))
     hidden2 = swap(after(hidden, rows, *far[1:]), "q")
-
+    near, send = call(
+        up_terms_kernel, (hidden_spots, up_where), (turned, hidden, hidden2), [shape(2, 128, 16, BS)] * 2, name="up_terms"
+    )
+    got = across(send, 1)
+    both = jnp.concatenate([active, rows.reshape(8, BS, BS)])
+    both = pieces(after(both, send), "row")
+    again = (near[1].astype(F32) + got[1].astype(F32)).astype(BF)
+    last = across(again, 2)
     slab = shape(2, BS, 2 * BS)
-    into = call(
-        into_kernel, (hidden_spots, up_where), (hidden, up_blocks), [slab] * 4, [pltpu.VMEM((ROWS, BS, BS), F32)], name="into"
-    )
-    turned = after(turned, into[0])
-    near0, send0, near1, send1 = call(
-        up_terms_kernel, (hidden_spots, up_where), (turned, hidden, hidden2), [shape(2, 64, 16, BS)] * 4, name="up_terms"
-    )
-    got0, got1 = across(send0, 1), across(send1, 1)
-    both = jnp.concatenate([active, rows.reshape(8, BS, BS)])
-    both = pieces(after(both, send0), "row")
-    last0 = across((near0[1].astype(F32) + got0[1].astype(F32)).astype(BF), 2)
-    send2 = (near1[1].astype(F32) + got1[1].astype(F32)).astype(BF)
-    last1 = across(send2, 2)
-    both[0] = after(both[0], last0, send2)
+    both[0] = after(both[0], again)
     *down, a = call(
         down_kernel, (feature_order, down_where), (*both, down_blocks), [slab] * 4 + [shape(64, BS, BS)], name="down"
     )
-    outputs = scatter_features(down)
-    grad_in = scatter_features(lax.optimization_barrier((*into, got0))[:4])
-
-    far = jnp.concatenate(far, axis=0)
-    far3 = swap(after(far, got0), "q")
+    into = call(
+        into_kernel, (hidden_spots, up_where), (after(hidden, a), up_blocks), [slab] * 4,
+        [pltpu.VMEM((ROWS, BS, BS), F32)], name="into",
+    )
+    grad_in = scatter_features(into)
+
+    far[0] = after(far[0], send)
+    far = join(far)
+    g2 = swap(after(g, send), "q")
     (grad_down,) = call(
-        down_terms_kernel, (place, feature_spots, down_where), (a, g, g2, far, far3),
+        down_terms_kernel, (place, feature_spots, down_where), (a, g, g2, far, swap(far, "q")),
         [shape(128, 16, BS, dtype=F32)], name="down_terms",
     )
-    (grad_up,) = call(
-        close_kernel, (), (after(near0, grad_down), got0, last0, near1, got1, last1), [shape(128, 16, BS, dtype=F32)], name="close"
-    )
+    mine = total(exchange(down, "y"))
+    outputs = (mine[0] + swap(after(mine[1].astype(BF), grad_down), "h").astype(F32)).astype(BF)
+    (grad_up,) = call(close_kernel, (), (near, got, last), [shape(128, 16, BS, dtype=F32)], name="close")
     return outputs, grad_in, grad_up, grad_down
 
 

time: 188 us -> 200 us (1.064); the launches traced: 188 us -> 196 us
  waiting for transfers between devices: 72.2 us -> 98.3 us
  starting transfers between devices: 70.6 us -> 56.6 us
  local copies, waits for them, and re-layouts: 11.4 us -> 7.82 us
    ppermute x24, waiting for transfers between devices: 24.3 us -> 43.6 us  [shift(): return lax.ppermute(value, axis, [(i, (i + by) % 4) for i in range(4)])]
    ppermute x6 -> x4, waiting for transfers between devices: 37.4 us -> 46.6 us  [across(): return lax.ppermute(value, 'z', [(i, i ^ by) for i in range(4)])]
    ppermute x24, starting transfers between devices: 40.9 us -> 33.9 us  [shift(): return lax.ppermute(value, axis, [(i, (i + by) % 4) for i in range(4)])]
    ppermute x6 -> x4, starting transfers between devices: 8.46 us -> 4.56 us  [across(): return lax.ppermute(value, 'z', [(i, i ^ by) for i in range(4)])]
    ppermute x8, starting transfers between devices: 16 us -> 12.5 us  [swap(): return lax.ppermute(value, axis, [(0, 1), (1, 0)])]
    unnamed x22 -> x24, local copies, waits for them, and re-layouts: 10.3 us -> 7.8 us
    ppermute x8, waiting for transfers between devices: 10.5 us -> 8.09 us  [swap(): return lax.ppermute(value, axis, [(0, 1), (1, 0)])]
    pallas_call x8 -> x10, Pallas kernels: 27.6 us -> 26.9 us  [call(): pl.pallas_call(kernel, out_shape=outs, in_specs=[SMEM] * len(scalars) + [...]
  transfers between devices with their start and end apart: 39 -> 37, of which waited for: 17 -> 16; matrix products, arithmetic and copies ran while one was open for 5% -> 3% of each run, Pallas kernels for 7% -> 7%
where the time goes in v2:
time: 200 us; the launch traced here: 196 us
  waiting for transfers between devices  98.3 us (49%)
  starting transfers between devices  56.6 us (28%)
  Pallas kernels  26.9 us (13%)
  local copies, waits for them, and re-layouts  7.82 us (4%)
  other arithmetic  5.86 us (3%)
    ppermute x4, waiting for transfers between devices, across(): return lax.ppermute(value, 'z', [(i, i ^ by) for i in range(4)])  46.6 us
    ppermute x24, waiting for transfers between devices, shift(): return lax.ppermute(value, axis, [(i, (i + by) % 4) for i in range(4)])  43.6 us
    ppermute x24, starting transfers between devices, shift(): return lax.ppermute(value, axis, [(i, (i + by) % 4) for i in range(4)])  33.9 us
    pallas_call x10, Pallas kernels, call(): pl.pallas_call(kernel, out_shape=outs, in_specs=[SMEM] * len(scalars) + [...  26.9 us
    ppermute x8, starting transfers between devices, swap(): return lax.ppermute(value, axis, [(0, 1), (1, 0)])  12.5 us
    ppermute x8, waiting for transfers between devices, swap(): return lax.ppermute(value, axis, [(0, 1), (1, 0)])  8.09 us
    unnamed x24, local copies, waits for them, and re-layouts  7.8 us
    all_to_all x1, starting transfers between devices, local(): rows = lax.all_to_all(rows, ('z', 'q'), 0, 0, tiled=True)  5.63 us
  transfers between devices with their start and end apart: 37, of which 16 were waited for; matrix products, arithmetic and copies ran while one was open for 3% of the time, Pallas kernels for 7%

profile of v2, /device:TPU:32, one launch (start us, length us, event | category | flops | bytes accessed | tf_op | source)
XLA Modules:
  0.0 196.3 jit_solution(11597443007053094003)
XLA Ops:
  0.6 6.4 %collective-permute-start.4 = (bf16[128,256]{1,0:T(8,128)(2,1)}, bf16[128,256]{1,0:T(8,128)(2,1)S(1)}, u32[]{:S(2)}, u32[]{:S(2)}) collective-permute-start(bf16[128,256]{1,0:T(8,128)(2,1)} %param.7), channel_id=1, source_target_pairs={{0,4},{4,0},{1,5},{5,1},{2,6},{6,2},{3,7},{7,3},{8,12},{12,8},{9,1... | collective-permute-start | bytes 196616 | tf_op jit(solution)/shard_map/ppermute | solution.py:203
  7.1 5.1 %collective-permute-done.4 = bf16[128,256]{1,0:T(8,128)(2,1)S(1)} collective-permute-done((bf16[128,256]{1,0:T(8,128)(2,1)}, bf16[128,256]{1,0:T(8,128)(2,1)S(1)}, u32[]{:S(2)}, u32[]{:S(2)}) %collective-permute-start.4) | collective-permute-done | bytes 65568 | tf_op jit(solution)/shard_map/ppermute | solution.py:203
  13.0 3.1 %collective-permute-start.6 = (bf16[2,128,256]{2,1,0:T(8,128)(2,1)S(1)}, bf16[2,128,256]{2,1,0:T(8,128)(2,1)S(1)}, u32[]{:S(2)}, u32[]{:S(2)}) collective-permute-start(bf16[2,128,256]{2,1,0:T(8,128)(2,1)S(1)} %get-tuple-element.37.g0), channel_id=1, source_target_pairs={{0,3},{1,0},{2,1},{3,2},{4,7},{5,4},{6,5},{7,6},{8,11},{9,8},{10,9... | collective-permute-start | bytes 393224 | tf_op jit(solution)/shard_map/ppermute | solution.py:199
  18.2 3.6 %collective-permute-start.7 = (bf16[2,128,256]{2,1,0:T(8,128)(2,1)S(1)}, bf16[2,128,256]{2,1,0:T(8,128)(2,1)S(1)}, u32[]{:S(2)}, u32[]{:S(2)}) collective-permute-start(bf16[2,128,256]{2,1,0:T(8,128)(2,1)S(1)} %get-tuple-element.37.g0), channel_id=1, source_target_pairs={{0,2},{1,3},{2,0},{3,1},{4,6},{5,7},{6,4},{7,5},{8,10},{9,11},{10,... | collective-permute-start | bytes 393224 | tf_op jit(solution)/shard_map/ppermute | solution.py:199
  26.3 3.7 %collective-permute-done.8.g3 = bf16[2,128,256]{2,1,0:T(8,128)(2,1)S(1)} collective-permute-done((bf16[2,128,256]{2,1,0:T(8,128)(2,1)S(1)}, bf16[2,128,256]{2,1,0:T(8,128)(2,1)S(1)}, u32[]{:S(2)}, u32[]{:S(2)}) %collective-permute-start.8) | collective-permute-done | bytes 131104 | tf_op jit(solution)/shard_map/ppermute | solution.py:199
  37.2 6.9 %first.1 = (bf16[2,8,128,128]{3,2,1,0:T(8,128)(2,1)S(1)}, bf16[2,8,128,128]{3,2,1,0:T(8,128)(2,1)}, bf16[2,8,128,128]{3,2,1,0:T(8,128)(2,1)}, bf16[2,8,128,128]{...) custom-call(s32[32]{0:T(128)S(1)} %fusion.18.order, s32[16]{0:T(128)S(1)} %fusion.22.spot, ...), custom_call_target="tpu_custom_call" | custom-call | flops 1024 | bytes 1024 | tf_op jit(solution)/shard_map/first/pallas_call | solution.py:35
  46.4 2.7 %collective-permute-start.12 = (bf16[2,8,128,128]{3,2,1,0:T(8,128)(2,1)}, bf16[2,8,128,128]{3,2,1,0:T(8,128)(2,1)S(1)}, u32[]{:S(2)}, u32[]{:S(2)}) collective-permute-start(bf16[2,8,128,128]{3,2,1,0:T(8,128)(2,1)} %get-tuple-element.43), channel_id=1, source_target_pairs={{0,16},{8,24},{16,0},{24,8},{1,17},{9,25},{17,1},{25,9},{2,18},{10... | collective-permute-start | bytes 1572872 | tf_op jit(solution)/shard_map/ppermute | solution.py:199
  53.9 10.2 %collective-permute-done.9 = bf16[2,2,128,256]{3,2,1,0:T(8,128)(2,1)S(1)} collective-permute-done((bf16[2,2,128,256]{3,2,1,0:T(8,128)(2,1)}, bf16[2,2,128,256]{3,2,1,0:T(8,128)(2,1)S(1)}, u32[]{:S(2)}, u32[]{:S(2)}) %collective-permute-start.9) | collective-permute-done | bytes 262176 | tf_op jit(solution)/shard_map/ppermute | solution.py:207
  64.1 8.8 %collective-permute-done.12.p2 = bf16[2,8,128,128]{3,2,1,0:T(8,128)(2,1)S(1)} collective-permute-done((bf16[2,8,128,128]{3,2,1,0:T(8,128)(2,1)}, bf16[2,8,128,128]{3,2,1,0:T(8,128)(2,1)S(1)}, u32[]{:S(2)}, u32[]{:S(2)}) %collective-permute-start.12) | collective-permute-done | bytes 524320 | tf_op jit(solution)/shard_map/ppermute | solution.py:199
  72.9 2.6 %act.1 = (bf16[8,128,128]{2,1,0:T(8,128)(2,1)S(1)}, bf16[8,128,128]{2,1,0:T(8,128)(2,1)S(1)}, bf16[8,8,16,128]{3,2,1,0:T(8,128)(2,1)}) custom-call(bf16[2,8,128,128]{3,2,1,0:T(8,128)(2,1)S(1)} %get-tuple-element.41.p0, bf16[2,8,128,128]{3,2,1,0:T(8,128)(2,1)S(1)} %collective-permute-done.11.p1, bf16[2,8,128,128]{3,2,1,0:T(8,128)(2,1)S(1)} %collective-permute-done.12.p2, ...), custom_call_target="tpu_custom_call" | custom-call | flops 1024 | bytes 1024 | tf_op jit(solution)/shard_map/act/pallas_call | solution.py:35
  77.9 5.6 %all-to-all-start = ((bf16[8,8,16,128]{3,2,1,0:T(8,128)(2,1)}), bf16[8,8,16,128]{3,2,1,0:T(8,128)(2,1)}, u32[]{:S(2)}, u32[]{:S(2)}) async-start(bf16[8,8,16,128]{3,2,1,0:T(8,128)(2,1)} %get-tuple-element.46), calls=%async_computation | async-start | bytes 524288 | tf_op jit(solution)/shard_map/all_to_all | solution.py:276
  89.1 8.3 %collective-permute-done.15.p2 = bf16[8,128,128]{2,1,0:T(8,128)(2,1)S(1)} collective-permute-done((bf16[8,128,128]{2,1,0:T(8,128)(2,1)S(1)}, bf16[8,128,128]{2,1,0:T(8,128)(2,1)S(1)}, u32[]{:S(2)}, u32[]{:S(2)}) %collective-permute-start.15) | collective-permute-done | bytes 262176 | tf_op jit(solution)/shard_map/ppermute | solution.py:199
  97.4 3.8 %collective-permute-done.16.p3 = bf16[8,128,128]{2,1,0:T(8,128)(2,1)S(1)} collective-permute-done((bf16[8,128,128]{2,1,0:T(8,128)(2,1)S(1)}, bf16[8,128,128]{2,1,0:T(8,128)(2,1)S(1)}, u32[]{:S(2)}, u32[]{:S(2)}) %collective-permute-start.16) | collective-permute-done | bytes 262176 | tf_op jit(solution)/shard_map/ppermute | solution.py:199
  105.3 2.6 %collective-permute-done.20.v1 = bf16[32,128,128]{2,1,0:T(8,128)(2,1)S(1)} collective-permute-done((bf16[32,128,128]{2,1,0:T(8,128)(2,1)S(1)}, bf16[32,128,128]{2,1,0:T(8,128)(2,1)S(1)}, u32[]{:S(2)}, u32[]{:S(2)}) %collective-permute-start.20) | collective-permute-done | bytes 1048608 | tf_op jit(solution)/shard_map/ppermute | solution.py:203
  108.0 4.0 %up_terms.1 = (bf16[2,128,16,128]{3,2,1,0:T(8,128)(2,1)S(1)}, bf16[2,128,16,128]{3,2,1,0:T(8,128)(2,1)S(1)}) custom-call(s32[32]{0:T(128)S(1)} %fusion.29.spot, s32[128]{0:T(128)S(1)} %get-tuple-element.71.up_where.where, bf16[16,4,16,256]{3,2,1,0:T(8,128)(2,1)S(1)} %turn.1.xt, bf16[32,128,128]{2,1,0:T(8,128)(2,1)S(1)} %join.2.v0.v, ...), custom_call_target="tpu_custom_call" | custom-call | flops 1024 | bytes 1024 | tf_op jit(solution)/shard_map/up_terms/pallas_call | solution.py:35
  116.3 21.0 %collective-permute-done.21.got = bf16[2,128,16,128]{3,2,1,0:T(8,128)(2,1)S(1)} collective-permute-done((bf16[2,128,16,128]{3,2,1,0:T(8,128)(2,1)S(1)}, bf16[2,128,16,128]{3,2,1,0:T(8,128)(2,1)S(1)}, u32[]{:S(2)}, u32[]{:S(2)}) %collective-permute-start.21) | collective-permute-done | bytes 1048608 | tf_op jit(solution)/shard_map/ppermute | solution.py:207
  137.5 3.2 %collective-permute-done.24.a3 = bf16[16,128,128]{2,1,0:T(8,128)(2,1)S(1)} collective-permute-done((bf16[16,128,128]{2,1,0:T(8,128)(2,1)S(1)}, bf16[16,128,128]{2,1,0:T(8,128)(2,1)S(1)}, u32[]{:S(2)}, u32[]{:S(2)}) %collective-permute-start.24) | collective-permute-done | bytes 524320 | tf_op jit(solution)/shard_map/ppermute | solution.py:199
  143.2 3.2 %into.1 = (bf16[2,128,256]{2,1,0:T(8,128)(2,1)S(1)}, bf16[2,128,256]{2,1,0:T(8,128)(2,1)S(1)}, bf16[2,128,256]{2,1,0:T(8,128)(2,1)S(1)}, bf16[2,128,256]{2,1,0:T(8,128)(2,1)S(1)}) custom-call(s32[32]{0:T(128)S(1)} %fusion.29.spot, s32[128]{0:T(128)S(1)} %get-tuple-element.71.up_where.where, bf16[32,128,128]{2,1,0:T(8,128)(2,1)S(1)} %join.2.v0.v, ...), custom_call_target="tpu_custom_call" | custom-call | flops 1024 | bytes 1024 | tf_op jit(solution)/shard_map/into/pallas_call | solution.py:35
  150.4 5.6 %collective-permute-done.31 = bf16[2,128,256]{2,1,0:T(8,128)(2,1)S(1)} collective-permute-done((bf16[2,128,256]{2,1,0:T(8,128)(2,1)S(1)}, bf16[2,128,256]{2,1,0:T(8,128)(2,1)S(1)}, u32[]{:S(2)}, u32[]{:S(2)}) %collective-permute-start.31) | collective-permute-done | bytes 131104 | tf_op jit(solution)/shard_map/ppermute | solution.py:199
  159.4 5.3 %collective-permute-done.25 = bf16[2,128,256]{2,1,0:T(8,128)(2,1)S(1)} collective-permute-done((bf16[2,128,256]{2,1,0:T(8,128)(2,1)S(1)}, bf16[2,128,256]{2,1,0:T(8,128)(2,1)S(1)}, u32[]{:S(2)}, u32[]{:S(2)}) %collective-permute-start.25) | collective-permute-done | bytes 131104 | tf_op jit(solution)/shard_map/ppermute | solution.py:199
  164.6 2.6 %collective-permute-start.35 = (bf16[128,16,128]{2,1,0:T(8,128)(2,1)S(1)}, bf16[128,16,128]{2,1,0:T(8,128)(2,1)S(1)}, u32[]{:S(2)}, u32[]{:S(2)}) collective-permute-start(bf16[128,16,128]{2,1,0:T(8,128)(2,1)S(1)} %fusion), channel_id=1, source_target_pairs={{0,128},{64,192},{128,0},{192,64},{1,129},{65,193},{129,1},{193,65... | collective-permute-start | bytes 1572872 | tf_op jit(solution)/shard_map/ppermute | solution.py:207
  167.2 5.1 %collective-permute-start.34 = (bf16[128,256]{1,0:T(8,128)(2,1)S(1)}, bf16[128,256]{1,0:T(8,128)(2,1)S(1)}, u32[]{:S(2)}, u32[]{:S(2)}) collective-permute-start(bf16[128,256]{1,0:T(8,128)(2,1)S(1)} %fusion.6), channel_id=1, source_target_pairs={{0,4},{4,0},{1,5},{5,1},{2,6},{6,2},{3,7},{7,3},{8,12},{12,8},{9,1... | collective-permute-start | bytes 196616 | tf_op jit(solution)/shard_map/ppermute | solution.py:203
  172.5 5.2 %down_terms.1 = f32[128,16,128]{2,1,0:T(8,128)} custom-call(s32[2]{0:T(128)S(1)} %pad_add_fusion.place, s32[16]{0:T(128)S(1)} %fusion.22.spot, s32[128]{0:T(128)S(1)} %get-tuple-element.70.down_where.where, bf16[64,128,128]{2,1,0:T(8,128)(2,1)S(1)} %get-tuple-element.58.a, bf16[8,128,256]{2,1,0:T(8,128)(2,1)S(1)} %copy-done.5, ...), custom_call_target="tpu_custom_call" | custom-call | flops 1024 | bytes 1024 | tf_op jit(solution)/shard_map/down_terms/pallas_call | solution.py:35
  179.1 15.4 %collective-permute-done.35.last = bf16[128,16,128]{2,1,0:T(8,128)(2,1)S(1)} collective-permute-done((bf16[128,16,128]{2,1,0:T(8,128)(2,1)S(1)}, bf16[128,16,128]{2,1,0:T(8,128)(2,1)S(1)}, u32[]{:S(2)}, u32[]{:S(2)}) %collective-permute-start.35) | collective-permute-done | bytes 524320 | tf_op jit(solution)/shard_map/ppermute | solution.py:207
  (102 shorter events, 51.4 us)
Async XLA Ops:
  0.6 11.6 %collective-permute-start.4 = (bf16[128,256]{1,0:T(8,128)(2,1)}, bf16[128,256]{1,0:T(8,128)(2,1)S(1)}, u32[]{:S(2)}, u32[]{:S(2)}) collective-permute-start(bf16[128,256]{1,0:T(8,128)(2,1)} %param.7), channel_id=1, source_target_pairs={{0,4},{4,0},{1,5},{5,1},{2,6},{6,2},{3,7},{7,3},{8,12},{12,8},{9,1... | collective-permute-start | bytes 196616 | tf_op jit(solution)/shard_map/ppermute | solution.py:203
  13.0 12.6 %collective-permute-start.6 = (bf16[2,128,256]{2,1,0:T(8,128)(2,1)S(1)}, bf16[2,128,256]{2,1,0:T(8,128)(2,1)S(1)}, u32[]{:S(2)}, u32[]{:S(2)}) collective-permute-start(bf16[2,128,256]{2,1,0:T(8,128)(2,1)S(1)} %get-tuple-element.37.g0), channel_id=1, source_target_pairs={{0,3},{1,0},{2,1},{3,2},{4,7},{5,4},{6,5},{7,6},{8,11},{9,8},{10,9... | collective-permute-start | bytes 393224 | tf_op jit(solution)/shard_map/ppermute | solution.py:199
  45.0 19.2 %collective-permute-start.11 = (bf16[2,8,128,128]{3,2,1,0:T(8,128)(2,1)}, bf16[2,8,128,128]{3,2,1,0:T(8,128)(2,1)S(1)}, u32[]{:S(2)}, u32[]{:S(2)}) collective-permute-start(bf16[2,8,128,128]{3,2,1,0:T(8,128)(2,1)} %get-tuple-element.42), channel_id=1, source_target_pairs={{0,8},{8,16},{16,24},{24,0},{1,9},{9,17},{17,25},{25,1},{2,10},{10... | collective-permute-start | bytes 1572872 | tf_op jit(solution)/shard_map/ppermute | solution.py:199
  46.4 26.5 %collective-permute-start.12 = (bf16[2,8,128,128]{3,2,1,0:T(8,128)(2,1)}, bf16[2,8,128,128]{3,2,1,0:T(8,128)(2,1)S(1)}, u32[]{:S(2)}, u32[]{:S(2)}) collective-permute-start(bf16[2,8,128,128]{3,2,1,0:T(8,128)(2,1)} %get-tuple-element.43), channel_id=1, source_target_pairs={{0,16},{8,24},{16,0},{24,8},{1,17},{9,25},{17,1},{25,9},{2,18},{10... | collective-permute-start | bytes 1572872 | tf_op jit(solution)/shard_map/ppermute | solution.py:199
  49.2 23.8 %collective-permute-start.13 = (bf16[2,8,128,128]{3,2,1,0:T(8,128)(2,1)}, bf16[2,8,128,128]{3,2,1,0:T(8,128)(2,1)}, u32[]{:S(2)}, u32[]{:S(2)}) collective-permute-start(bf16[2,8,128,128]{3,2,1,0:T(8,128)(2,1)} %get-tuple-element.44), channel_id=1, source_target_pairs={{0,24},{8,0},{16,8},{24,16},{1,25},{9,1},{17,9},{25,17},{2,26},{10... | collective-permute-start | bytes 1572872 | tf_op jit(solution)/shard_map/ppermute | solution.py:199
  51.3 12.8 %collective-permute-start.9 = (bf16[2,2,128,256]{3,2,1,0:T(8,128)(2,1)}, bf16[2,2,128,256]{3,2,1,0:T(8,128)(2,1)S(1)}, u32[]{:S(2)}, u32[]{:S(2)}) collective-permute-start(bf16[2,2,128,256]{3,2,1,0:T(8,128)(2,1)} %pad_maximum_fusion.1), channel_id=1, source_target_pairs={{0,128},{64,192},{128,0},{192,64},{1,129},{65,193},{129,1},{193,65... | collective-permute-start | bytes 786440 | tf_op jit(solution)/shard_map/ppermute | solution.py:207
  75.6 12.2 %collective-permute-start.14 = (bf16[8,128,128]{2,1,0:T(8,128)(2,1)S(1)}, bf16[8,128,128]{2,1,0:T(8,128)(2,1)S(1)}, u32[]{:S(2)}, u32[]{:S(2)}) collective-permute-start(bf16[8,128,128]{2,1,0:T(8,128)(2,1)S(1)} %get-tuple-element.47.p0), channel_id=1, source_target_pairs={{0,24},{8,0},{16,8},{24,16},{1,25},{9,1},{17,9},{25,17},{2,26},{10... | collective-permute-start | bytes 786440 | tf_op jit(solution)/shard_map/ppermute | solution.py:199
  77.9 27.4 %all-to-all-start = ((bf16[8,8,16,128]{3,2,1,0:T(8,128)(2,1)}), bf16[8,8,16,128]{3,2,1,0:T(8,128)(2,1)}, u32[]{:S(2)}, u32[]{:S(2)}) async-start(bf16[8,8,16,128]{3,2,1,0:T(8,128)(2,1)} %get-tuple-element.46), calls=%async_computation | async-start | bytes 524288 | tf_op jit(solution)/shard_map/all_to_all | solution.py:276
  83.6 19.6 %collective-permute-start.17 = (bf16[1,3,2,128,256]{4,3,2,1,0:T(8,128)(2,1)S(1)}, bf16[1,3,2,128,256]{4,3,2,1,0:T(8,128)(2,1)S(1)}, u32[]{:S(2)}, u32[]{:S(2)}) collective-permute-start(bf16[1,3,2,128,256]{4,3,2,1,0:T(8,128)(2,1)S(1)} %maximum_bitcast_fusion.p0), channel_id=1, source_target_pairs={{0,3},{1,0},{2,1},{3,2},{4,7},{5,4},{6,5},{7,6},{8,11},{9,8},{10,9... | collective-permute-start | bytes 1179656 | tf_op jit(solution)/shard_map/ppermute | solution.py:199
  84.5 18.7 %collective-permute-start.18 = (bf16[1,3,2,128,256]{4,3,2,1,0:T(8,128)(2,1)S(1)}, bf16[1,3,2,128,256]{4,3,2,1,0:T(8,128)(2,1)S(1)}, u32[]{:S(2)}, u32[]{:S(2)}) collective-permute-start(bf16[1,3,2,128,256]{4,3,2,1,0:T(8,128)(2,1)S(1)} %maximum_bitcast_fusion.p0), channel_id=1, source_target_pairs={{0,2},{1,3},{2,0},{3,1},{4,6},{5,7},{6,4},{7,5},{8,10},{9,11},{10,... | collective-permute-start | bytes 1179656 | tf_op jit(solution)/shard_map/ppermute | solution.py:199
  85.7 19.6 %collective-permute-start.19 = (bf16[1,3,2,128,256]{4,3,2,1,0:T(8,128)(2,1)S(1)}, bf16[1,3,2,128,256]{4,3,2,1,0:T(8,128)(2,1)S(1)}, u32[]{:S(2)}, u32[]{:S(2)}) collective-permute-start(bf16[1,3,2,128,256]{4,3,2,1,0:T(8,128)(2,1)S(1)} %maximum_bitcast_fusion.p0), channel_id=1, source_target_pairs={{0,1},{1,2},{2,3},{3,0},{4,5},{5,6},{6,7},{7,4},{8,9},{9,10},{10,1... | collective-permute-start | bytes 1179656 | tf_op jit(solution)/shard_map/ppermute | solution.py:199
  86.6 10.8 %collective-permute-start.15 = (bf16[8,128,128]{2,1,0:T(8,128)(2,1)S(1)}, bf16[8,128,128]{2,1,0:T(8,128)(2,1)S(1)}, u32[]{:S(2)}, u32[]{:S(2)}) collective-permute-start(bf16[8,128,128]{2,1,0:T(8,128)(2,1)S(1)} %get-tuple-element.47.p0), channel_id=1, source_target_pairs={{0,16},{8,24},{16,0},{24,8},{1,17},{9,25},{17,1},{25,9},{2,18},{10... | collective-permute-start | bytes 786440 | tf_op jit(solution)/shard_map/ppermute | solution.py:199
  88.4 12.8 %collective-permute-start.16 = (bf16[8,128,128]{2,1,0:T(8,128)(2,1)S(1)}, bf16[8,128,128]{2,1,0:T(8,128)(2,1)S(1)}, u32[]{:S(2)}, u32[]{:S(2)}) collective-permute-start(bf16[8,128,128]{2,1,0:T(8,128)(2,1)S(1)} %get-tuple-element.47.p0), channel_id=1, source_target_pairs={{0,8},{8,16},{16,24},{24,0},{1,9},{9,17},{17,25},{25,1},{2,10},{10... | collective-permute-start | bytes 786440 | tf_op jit(solution)/shard_map/ppermute | solution.py:199
  112.0 25.3 %collective-permute-start.21 = (bf16[2,128,16,128]{3,2,1,0:T(8,128)(2,1)S(1)}, bf16[2,128,16,128]{3,2,1,0:T(8,128)(2,1)S(1)}, u32[]{:S(2)}, u32[]{:S(2)}) collective-permute-start(bf16[2,128,16,128]{3,2,1,0:T(8,128)(2,1)S(1)} %get-tuple-element.50), channel_id=1, source_target_pairs={{0,64},{64,0},{128,192},{192,128},{1,65},{65,1},{129,193},{193,129... | collective-permute-start | bytes 3145736 | tf_op jit(solution)/shard_map/ppermute | solution.py:207
  113.4 24.0 %collective-permute-start.22 = (bf16[16,128,128]{2,1,0:T(8,128)(2,1)S(1)}, bf16[16,128,128]{2,1,0:T(8,128)(2,1)S(1)}, u32[]{:S(2)}, u32[]{:S(2)}) collective-permute-start(bf16[16,128,128]{2,1,0:T(8,128)(2,1)S(1)} %pad_maximum_fusion.a0), channel_id=1, source_target_pairs={{0,24},{8,0},{16,8},{24,16},{1,25},{9,1},{17,9},{25,17},{2,26},{10... | collective-permute-start | bytes 1572872 | tf_op jit(solution)/shard_map/ppermute | solution.py:199
  114.5 23.0 %collective-permute-start.23 = (bf16[16,128,128]{2,1,0:T(8,128)(2,1)S(1)}, bf16[16,128,128]{2,1,0:T(8,128)(2,1)S(1)}, u32[]{:S(2)}, u32[]{:S(2)}) collective-permute-start(bf16[16,128,128]{2,1,0:T(8,128)(2,1)S(1)} %pad_maximum_fusion.a0), channel_id=1, source_target_pairs={{0,16},{8,24},{16,0},{24,8},{1,17},{9,25},{17,1},{25,9},{2,18},{10... | collective-permute-start | bytes 1572872 | tf_op jit(solution)/shard_map/ppermute | solution.py:199
  115.3 25.4 %collective-permute-start.24 = (bf16[16,128,128]{2,1,0:T(8,128)(2,1)S(1)}, bf16[16,128,128]{2,1,0:T(8,128)(2,1)S(1)}, u32[]{:S(2)}, u32[]{:S(2)}) collective-permute-start(bf16[16,128,128]{2,1,0:T(8,128)(2,1)S(1)} %pad_maximum_fusion.a0), channel_id=1, source_target_pairs={{0,8},{8,16},{16,24},{24,0},{1,9},{9,17},{17,25},{25,1},{2,10},{10... | collective-permute-start | bytes 1572872 | tf_op jit(solution)/shard_map/ppermute | solution.py:199
  116.2 56.3 %collective-permute-start.29 = (bf16[4,3,2,128,256]{4,3,2,1,0:T(8,128)(2,1)S(1)}, bf16[4,3,2,128,256]{4,3,2,1,0:T(8,128)(2,1)S(1)}, u32[]{:S(2)}, u32[]{:S(2)}) collective-permute-start(bf16[4,3,2,128,256]{4,3,2,1,0:T(8,128)(2,1)S(1)} %join.3.f0), channel_id=1, source_target_pairs={{0,32},{32,0},{1,33},{33,1},{2,34},{34,2},{3,35},{35,3},{4,36},{36... | collective-permute-start | bytes 4718600 | tf_op jit(solution)/shard_map/ppermute | solution.py:203
  150.4 22.1 %collective-permute-start.28 = (bf16[8,128,256]{2,1,0:T(8,128)(2,1)S(1)}, bf16[8,128,256]{2,1,0:T(8,128)(2,1)S(1)}, u32[]{:S(2)}, u32[]{:S(2)}) collective-permute-start(bf16[8,128,256]{2,1,0:T(8,128)(2,1)S(1)} %copy-done.5), channel_id=1, source_target_pairs={{0,32},{32,0},{1,33},{33,1},{2,34},{34,2},{3,35},{35,3},{4,36},{36... | collective-permute-start | bytes 1572872 | tf_op jit(solution)/shard_map/ppermute | solution.py:203
  156.0 11.3 %collective-permute-start.26 = (bf16[2,128,256]{2,1,0:T(8,128)(2,1)S(1)}, bf16[2,128,256]{2,1,0:T(8,128)(2,1)S(1)}, u32[]{:S(2)}, u32[]{:S(2)}) collective-permute-start(bf16[2,128,256]{2,1,0:T(8,128)(2,1)S(1)} %get-tuple-element.56), channel_id=1, source_target_pairs={{0,2},{1,3},{2,0},{3,1},{4,6},{5,7},{6,4},{7,5},{8,10},{9,11},{10,... | collective-permute-start | bytes 393224 | tf_op jit(solution)/shard_map/ppermute | solution.py:199
  157.0 15.4 %collective-permute-start.27 = (bf16[2,128,256]{2,1,0:T(8,128)(2,1)S(1)}, bf16[2,128,256]{2,1,0:T(8,128)(2,1)S(1)}, u32[]{:S(2)}, u32[]{:S(2)}) collective-permute-start(bf16[2,128,256]{2,1,0:T(8,128)(2,1)S(1)} %get-tuple-element.57), channel_id=1, source_target_pairs={{0,3},{1,0},{2,1},{3,2},{4,7},{5,4},{6,5},{7,6},{8,11},{9,8},{10,9... | collective-permute-start | bytes 393224 | tf_op jit(solution)/shard_map/ppermute | solution.py:199
  164.6 29.9 %collective-permute-start.35 = (bf16[128,16,128]{2,1,0:T(8,128)(2,1)S(1)}, bf16[128,16,128]{2,1,0:T(8,128)(2,1)S(1)}, u32[]{:S(2)}, u32[]{:S(2)}) collective-permute-start(bf16[128,16,128]{2,1,0:T(8,128)(2,1)S(1)} %fusion), channel_id=1, source_target_pairs={{0,128},{64,192},{128,0},{192,64},{1,129},{65,193},{129,1},{193,65... | collective-permute-start | bytes 1572872 | tf_op jit(solution)/shard_map/ppermute | solution.py:207
  167.2 11.2 %collective-permute-start.34 = (bf16[128,256]{1,0:T(8,128)(2,1)S(1)}, bf16[128,256]{1,0:T(8,128)(2,1)S(1)}, u32[]{:S(2)}, u32[]{:S(2)}) collective-permute-start(bf16[128,256]{1,0:T(8,128)(2,1)S(1)} %fusion.6), channel_id=1, source_target_pairs={{0,4},{4,0},{1,5},{5,1},{2,6},{6,2},{3,7},{7,3},{8,12},{12,8},{9,1... | collective-permute-start | bytes 196616 | tf_op jit(solution)/shard_map/ppermute | solution.py:203
  177.7 18.0 %collective-permute-start.30 = (bf16[128,256]{1,0:T(8,128)(2,1)S(1)}, bf16[128,256]{1,0:T(8,128)(2,1)S(1)}, u32[]{:S(2)}, u32[]{:S(2)}) collective-permute-start(bf16[128,256]{1,0:T(8,128)(2,1)S(1)} %fusion.5), channel_id=1, source_target_pairs={{0,4},{4,0},{1,5},{5,1},{2,6},{6,2},{3,7},{7,3},{8,12},{12,8},{9,1... | collective-permute-start | bytes 196616 | tf_op jit(solution)/shard_map/ppermute | solution.py:203
  (25 other events, 190.8 us)

commit v3 on v2

--- a/solution.py
+++ b/solution.py
@@ -38,7 +38,7 @@
         in_specs=[SMEM] * len(scalars) + [VMEM] * len(arrays),
         out_specs=[VMEM] * len(outs),
         scratch_shapes=list(scratch),
-        compiler_params=pltpu.CompilerParams(vmem_limit_bytes=20 * 2**20),
+        compiler_params=pltpu.CompilerParams(vmem_limit_bytes=28 * 2**20),
         cost_estimate=pl.CostEstimate(flops=1024, bytes_accessed=1024, transcendentals=0),
         name=name,
     )(*scalars, *arrays)
@@ -104,7 +104,7 @@
 
 
 def turn_kernel(place, x, x2, out):
-    z, q = place[0], place[1]
+    q = place[1]
 
     def step(p, carry):
         for half in range(2):
@@ -112,7 +112,7 @@
                 rows = ref[p, :, half * BS:(half + 1) * BS].T.reshape(4, 2, 16, BS)
                 for zz in range(4):
                     mine = jnp.where(q == 0, rows[zz, 0], rows[zz, 1])
-                    out[p * 2 + half, jnp.bitwise_xor(zz, z), :, group * BS:(group + 1) * BS] = mine
+                    out[p * 2 + half, zz, :, group * BS:(group + 1) * BS] = mine
         return carry
 
     lax.fori_loop(0, 8, step, 0, unroll=2)
@@ -130,44 +130,40 @@
     return call(join_kernel, (), parts, [whole], name="join")[0]
 
 
-def up_terms_kernel(spot, where, xt, v0, v1, near, far):
+def up_terms_kernel(spot, where, xt, v0, v1, out):
     def step(j, carry):
         at = spot[j]
         lhs = jnp.concatenate([xt[where[j * KB + k]].reshape(64, 2 * BS) for k in range(KB)], axis=0)
         rhs = jnp.concatenate([v0[at], v1[at]], axis=0)
         got = jnp.dot(lhs, rhs, preferred_element_type=F32).astype(BF).reshape(KB, 4, 16, BS)
-        for s, out in enumerate((near, far, near, far)):
-            out[s // 2, pl.ds(j * KB, KB)] = got[:, s]
+        for zz in range(4):
+            out[zz, pl.ds(j * KB, KB)] = got[:, zz]
         return carry
 
     lax.fori_loop(0, COLS, step, 0, unroll=2)
 
 
-def into_kernel(spot, where, v, w, o0, o1, o2, o3, acc):
+def ends_kernel(order, spot, up_where, down_where, v, a0, a1, a2, a3, w1, w2, o0, o1, o2, o3, a, acc):
+    for n, piece in enumerate((a0, a1, a2, a3)):
+        a[n * 16:n * 16 + 16] = piece[...]
     acc[...] = jnp.zeros_like(acc)
 
     def step(j, carry):
-        add_back(acc, j, where, KB, v[spot[j]], w)
+        add_back(acc, j, up_where, KB, v[spot[j]], w1)
         return carry
 
     lax.fori_loop(0, COLS, step, 0, unroll=4)
     for slot, out in enumerate((o0, o1, o2, o3)):
         for t in range(2):
             for half in range(2):
-                out[t, :, half * BS:(half + 1) * BS] = acc[slot * 4 + t * 2 + half].astype(BF)
-
-
-def down_kernel(order, where, a0, a1, a2, a3, w, o0, o1, o2, o3, a):
-    for n, piece in enumerate((a0, a1, a2, a3)):
-        a[n * 16:n * 16 + 16] = piece[...]
-    for slot, out in enumerate((o0, o1, o2, o3)):
-        for t in range(2):
-            for half in range(2):
-                i = order[slot * 4 + t * 2 + half]
-                runs = [where[i * KB2 + k] for k in range(KB2)]
+                loc = slot * 4 + t * 2 + half
+                at = slice(half * BS, (half + 1) * BS)
+                out[t, 1, :, at] = acc[loc].astype(BF)
+                i = order[loc]
+                runs = [down_where[i * KB2 + k] for k in range(KB2)]
                 lhs = jnp.concatenate([a[u // 8 * 16 + u % 8] for u in runs], axis=1)
-                rhs = w[pl.ds(i * KB2, KB2)].reshape(KB2 * BS, BS)
-                out[t, :, half * BS:(half + 1) * BS] = jnp.dot(lhs, rhs, preferred_element_type=F32).astype(BF)
+                rhs = w2[pl.ds(i * KB2, KB2)].reshape(KB2 * BS, BS)
+                out[t, 0, :, at] = jnp.dot(lhs, rhs, preferred_element_type=F32).astype(BF)
 
 
 def down_terms_kernel(place, spot, where, a, g0, g1, f0, f1, out):
@@ -191,8 +187,8 @@
     lax.fori_loop(0, ROWS, step, 0, unroll=2)
 
 
-def close_kernel(near, got, last, out):
-    out[...] = near[0].astype(F32) + got[0].astype(F32) + last[...].astype(F32)
+def close_kernel(got, out):
+    out[...] = (got[0].astype(F32) + got[1].astype(F32)) + (got[2].astype(F32) + got[3].astype(F32))
 
 
 def shift(value, axis, by):
@@ -217,11 +213,6 @@
 
 def exchange(parts, axis):
     return [parts[0]] + [shift(parts[s], axis, s) for s in (1, 2, 3)]
-
-
-def scatter_features(parts):
-    mine = total(exchange(parts, "y"))
-    return (mine[0] + swap(mine[1].astype(BF), "h").astype(F32)).astype(BF)
 
 
 def total(parts):
@@ -258,54 +249,44 @@
     g_own = jnp.stack([grad_out, swap(grad_out, "h")])
     panel, piece = shape(8, BS, 2 * BS), shape(8, BS, BS)
 
-    far1 = across(after(g_own, x_own), 1)
-    cotangents = pieces(g_own, "y")
-    cotangents[0] = after(cotangents[0], far1)
     *parts, x, g = call(
         first_kernel, (hidden_order, feature_spots, up_where, down_where),
-        (*pieces(x_own, "y"), *cotangents, up_blocks, down_blocks),
+        (*pieces(x_own, "y"), *pieces(g_own, "y"), up_blocks, down_blocks),
         [shape(2, 8, BS, BS)] * 4 + [panel] * 2, [pltpu.VMEM((COLS, BS, BS), F32)], name="first",
     )
     parts = exchange(parts, "row")
-    far2 = across(after(jnp.stack([g_own, far1]), x), 2)
-    x2 = swap(x, "q")
+    far1 = across(after(g_own, x), 1)
+    far2 = across(jnp.stack([g_own, far1]), 2)
+    x2, g2 = swap(x, "q"), swap(g, "q")
     (turned,) = call(turn_kernel, (place,), (x, x2), [shape(ROWS, 4, 16, 2 * BS)], name="turn")
-    parts[0] = after(parts[0], far2, turned)
+    parts[0] = after(parts[0], turned, far2, g2)
     active, own, rows = call(act_kernel, (), parts, [piece, piece, shape(8, 8, 16, BS)], name="act")
     far = pieces(after(jnp.concatenate([far1[None], far2])[None], own), "y")
     rows = lax.all_to_all(rows, ("z", "q"), 0, 0, tiled=True)
     hidden = join(pieces(own, "row"))
     hidden2 = swap(after(hidden, rows, *far[1:]), "q")
-    near, send = call(
-        up_terms_kernel, (hidden_spots, up_where), (turned, hidden, hidden2), [shape(2, 128, 16, BS)] * 2, name="up_terms"
-    )
-    got = across(send, 1)
+    (terms,) = call(
+        up_terms_kernel, (hidden_spots, up_where), (turned, hidden, hidden2), [shape(4, 128, 16, BS)], name="up_terms"
+    )
+    got = lax.all_to_all(terms, "z", 0, 0, tiled=True)
     both = jnp.concatenate([active, rows.reshape(8, BS, BS)])
-    both = pieces(after(both, send), "row")
-    again = (near[1].astype(F32) + got[1].astype(F32)).astype(BF)
-    last = across(again, 2)
-    slab = shape(2, BS, 2 * BS)
-    both[0] = after(both[0], again)
-    *down, a = call(
-        down_kernel, (feature_order, down_where), (*both, down_blocks), [slab] * 4 + [shape(64, BS, BS)], name="down"
-    )
-    into = call(
-        into_kernel, (hidden_spots, up_where), (after(hidden, a), up_blocks), [slab] * 4,
-        [pltpu.VMEM((ROWS, BS, BS), F32)], name="into",
-    )
-    grad_in = scatter_features(into)
-
-    far[0] = after(far[0], send)
+    both = pieces(after(both, terms), "row")
+    *ends, a = call(
+        ends_kernel, (feature_order, hidden_spots, up_where, down_where), (hidden, *both, up_blocks, down_blocks),
+        [shape(2, 2, BS, 2 * BS)] * 4 + [shape(64, BS, BS)], [pltpu.VMEM((ROWS, BS, BS), F32)], name="ends",
+    )
+    far[0] = after(far[0], *both[1:])
     far = join(far)
-    g2 = swap(after(g, send), "q")
     (grad_down,) = call(
         down_terms_kernel, (place, feature_spots, down_where), (a, g, g2, far, swap(far, "q")),
         [shape(128, 16, BS, dtype=F32)], name="down_terms",
     )
-    mine = total(exchange(down, "y"))
-    outputs = (mine[0] + swap(after(mine[1].astype(BF), grad_down), "h").astype(F32)).astype(BF)
-    (grad_up,) = call(close_kernel, (), (near, got, last), [shape(128, 16, BS, dtype=F32)], name="close")
-    return outputs, grad_in, grad_up, grad_down
+    ends = exchange(ends, "y")
+    ends[0] = after(ends[0], grad_down)
+    mine = total(ends)
+    ends = (mine[0] + swap(mine[1].astype(BF), "h").astype(F32)).astype(BF)
+    (grad_up,) = call(close_kernel, (), (got,), [shape(128, 16, BS, dtype=F32)], name="close")
+    return ends[0], ends[1], grad_up, grad_down
 
 
 def solution(mesh):

time: 200 us -> 184 us (0.920); the launches traced: 196 us -> 183 us
  waiting for transfers between devices: 98.3 us -> 70.6 us
  local copies, waits for them, and re-layouts: 7.82 us -> 16.4 us
  starting transfers between devices: 56.6 us -> 60 us
  Pallas kernels: 26.9 us -> 29.2 us
    ppermute x4 -> x2, waiting for transfers between devices: 46.6 us -> 11.4 us  [across(): return lax.ppermute(value, 'z', [(i, i ^ by) for i in range(4)])]
    unnamed x24 -> x40, local copies, waits for them, and re-layouts: 7.8 us -> 15.7 us
    all_to_all x0 -> x1, starting transfers between devices: none -> 5.12 us  [local(): got = lax.all_to_all(terms, 'z', 0, 0, tiled=True)]
    ppermute x8 -> x7, waiting for transfers between devices: 8.09 us -> 12.1 us  [swap(): return lax.ppermute(value, axis, [(0, 1), (1, 0)])]
    ppermute x4 -> x2, starting transfers between devices: 4.56 us -> 0.76 us  [across(): return lax.ppermute(value, 'z', [(i, i ^ by) for i in range(4)])]
    ppermute x24 -> x21, waiting for transfers between devices: 43.6 us -> 47.1 us  [shift(): return lax.ppermute(value, axis, [(i, (i + by) % 4) for i in range(4)])]
    pallas_call x10 -> x9, Pallas kernels: 26.9 us -> 29.2 us  [call(): pl.pallas_call(kernel, out_shape=outs, in_specs=[SMEM] * len(scalars) + [...]
    ppermute x8 -> x7, starting transfers between devices: 12.5 us -> 13.5 us  [swap(): return lax.ppermute(value, axis, [(0, 1), (1, 0)])]
  transfers between devices with their start and end apart: 37 -> 32, of which waited for: 16 -> 16; matrix products, arithmetic and copies ran while one was open for 3% -> 4% of each run, Pallas kernels for 7% -> 7%
where the time goes in v3:
time: 184 us; the launch traced here: 183 us
  waiting for transfers between devices  70.6 us (38%)
  starting transfers between devices  60 us (33%)
  Pallas kernels  29.2 us (16%)
  local copies, waits for them, and re-layouts  16.4 us (9%)
  other arithmetic  6.4 us (3%)
    ppermute x21, waiting for transfers between devices, shift(): return lax.ppermute(value, axis, [(i, (i + by) % 4) for i in range(4)])  47.1 us
    ppermute x21, starting transfers between devices, shift(): return lax.ppermute(value, axis, [(i, (i + by) % 4) for i in range(4)])  34.7 us
    pallas_call x9, Pallas kernels, call(): pl.pallas_call(kernel, out_shape=outs, in_specs=[SMEM] * len(scalars) + [...  29.2 us
    unnamed x40, local copies, waits for them, and re-layouts  15.7 us
    ppermute x7, starting transfers between devices, swap(): return lax.ppermute(value, axis, [(0, 1), (1, 0)])  13.5 us
    ppermute x7, waiting for transfers between devices, swap(): return lax.ppermute(value, axis, [(0, 1), (1, 0)])  12.1 us
    ppermute x2, waiting for transfers between devices, across(): return lax.ppermute(value, 'z', [(i, i ^ by) for i in range(4)])  11.4 us
    all_to_all x1, starting transfers between devices, local(): rows = lax.all_to_all(rows, ('z', 'q'), 0, 0, tiled=True)  5.85 us
  transfers between devices with their start and end apart: 32, of which 16 were waited for; matrix products, arithmetic and copies ran while one was open for 4% of the time, Pallas kernels for 7%

profile of v3, /device:TPU:32, one launch (start us, length us, event | category | flops | bytes accessed | tf_op | source)
XLA Modules:
  0.0 183.3 jit_solution(16877973143209724683)
XLA Ops:
  0.6 6.4 %collective-permute-start = (bf16[128,256]{1,0:T(8,128)(2,1)}, bf16[128,256]{1,0:T(8,128)(2,1)S(1)}, u32[]{:S(2)}, u32[]{:S(2)}) collective-permute-start(bf16[128,256]{1,0:T(8,128)(2,1)} %param.6), channel_id=1, source_target_pairs={{0,4},{4,0},{1,5},{5,1},{2,6},{6,2},{3,7},{7,3},{8,12},{12,8},{9,1... | collective-permute-start | bytes 196616 | tf_op jit(solution)/shard_map/ppermute | solution.py:199
  7.1 5.1 %collective-permute-done = bf16[128,256]{1,0:T(8,128)(2,1)S(1)} collective-permute-done((bf16[128,256]{1,0:T(8,128)(2,1)}, bf16[128,256]{1,0:T(8,128)(2,1)S(1)}, u32[]{:S(2)}, u32[]{:S(2)}) %collective-permute-start) | collective-permute-done | bytes 65568 | tf_op jit(solution)/shard_map/ppermute | solution.py:199
  15.4 3.0 %collective-permute-start.2 = (bf16[2,128,256]{2,1,0:T(8,128)(2,1)S(1)}, bf16[2,128,256]{2,1,0:T(8,128)(2,1)S(1)}, u32[]{:S(2)}, u32[]{:S(2)}) collective-permute-start(bf16[2,128,256]{2,1,0:T(8,128)(2,1)S(1)} %pad_maximum_fusion.2.x0), channel_id=1, source_target_pairs={{0,2},{1,3},{2,0},{3,1},{4,6},{5,7},{6,4},{7,5},{8,10},{9,11},{10,... | collective-permute-start | bytes 393224 | tf_op jit(solution)/shard_map/ppermute | solution.py:195
  24.8 3.4 %collective-permute-done.7.g3 = bf16[2,128,256]{2,1,0:T(8,128)(2,1)S(1)} collective-permute-done((bf16[2,128,256]{2,1,0:T(8,128)(2,1)S(1)}, bf16[2,128,256]{2,1,0:T(8,128)(2,1)S(1)}, u32[]{:S(2)}, u32[]{:S(2)}) %collective-permute-start.7) | collective-permute-done | bytes 131104 | tf_op jit(solution)/shard_map/ppermute | solution.py:195
  29.2 2.2 %copy-done = bf16[128,128,128]{2,1,0:T(8,128)(2,1)S(1)} copy-done((bf16[128,128,128]{2,1,0:T(8,128)(2,1)S(1)}, bf16[128,128,128]{2,1,0:T(8,128)(2,1)}, u32[]{:S(2)}) %copy-start) | copy-done | bytes 4194328
  33.5 7.1 %first.1 = (bf16[2,8,128,128]{3,2,1,0:T(8,128)(2,1)S(1)}, bf16[2,8,128,128]{3,2,1,0:T(8,128)(2,1)}, bf16[2,8,128,128]{3,2,1,0:T(8,128)(2,1)}, bf16[2,8,128,128]{...) custom-call(s32[32]{0:T(128)S(1)} %fusion.19.order, s32[16]{0:T(128)S(1)} %fusion.23.spot, ...), custom_call_target="tpu_custom_call" | custom-call | flops 1024 | bytes 1024 | tf_op jit(solution)/shard_map/first/pallas_call | solution.py:35
  42.6 2.7 %collective-permute-start.13 = (bf16[2,8,128,128]{3,2,1,0:T(8,128)(2,1)}, bf16[2,8,128,128]{3,2,1,0:T(8,128)(2,1)S(1)}, u32[]{:S(2)}, u32[]{:S(2)}) collective-permute-start(bf16[2,8,128,128]{3,2,1,0:T(8,128)(2,1)} %get-tuple-element.31), channel_id=1, source_target_pairs={{0,16},{8,24},{16,0},{24,8},{1,17},{9,25},{17,1},{25,9},{2,18},{10... | collective-permute-start | bytes 1572872 | tf_op jit(solution)/shard_map/ppermute | solution.py:195
  46.6 2.8 %collective-permute-start.14 = (bf16[2,8,128,128]{3,2,1,0:T(8,128)(2,1)}, bf16[2,8,128,128]{3,2,1,0:T(8,128)(2,1)}, u32[]{:S(2)}, u32[]{:S(2)}) collective-permute-start(bf16[2,8,128,128]{3,2,1,0:T(8,128)(2,1)} %get-tuple-element.32), channel_id=1, source_target_pairs={{0,24},{8,0},{16,8},{24,16},{1,25},{9,1},{17,9},{25,17},{2,26},{10... | collective-permute-start | bytes 1572872 | tf_op jit(solution)/shard_map/ppermute | solution.py:195
  51.9 10.2 %collective-permute-done.10 = bf16[2,2,128,256]{3,2,1,0:T(8,128)(2,1)S(1)} collective-permute-done((bf16[2,2,128,256]{3,2,1,0:T(8,128)(2,1)}, bf16[2,2,128,256]{3,2,1,0:T(8,128)(2,1)S(1)}, u32[]{:S(2)}, u32[]{:S(2)}) %collective-permute-start.10) | collective-permute-done | bytes 262176 | tf_op jit(solution)/shard_map/ppermute | solution.py:203
  62.1 6.6 %collective-permute-done.13.p2 = bf16[2,8,128,128]{3,2,1,0:T(8,128)(2,1)S(1)} collective-permute-done((bf16[2,8,128,128]{3,2,1,0:T(8,128)(2,1)}, bf16[2,8,128,128]{3,2,1,0:T(8,128)(2,1)S(1)}, u32[]{:S(2)}, u32[]{:S(2)}) %collective-permute-start.13) | collective-permute-done | bytes 524320 | tf_op jit(solution)/shard_map/ppermute | solution.py:195
  68.7 2.6 %act.1 = (bf16[8,128,128]{2,1,0:T(8,128)(2,1)S(1)}, bf16[8,128,128]{2,1,0:T(8,128)(2,1)S(1)}, bf16[8,8,16,128]{3,2,1,0:T(8,128)(2,1)}) custom-call(bf16[2,8,128,128]{3,2,1,0:T(8,128)(2,1)S(1)} %get-tuple-element.29.p0, bf16[2,8,128,128]{3,2,1,0:T(8,128)(2,1)S(1)} %collective-permute-done.12.p1, bf16[2,8,128,128]{3,2,1,0:T(8,128)(2,1)S(1)} %collective-permute-done.13.p2, ...), custom_call_target="tpu_custom_call" | custom-call | flops 1024 | bytes 1024 | tf_op jit(solution)/shard_map/act/pallas_call | solution.py:35
  74.1 5.9 %all-to-all-start = ((bf16[8,8,16,128]{3,2,1,0:T(8,128)(2,1)}), bf16[8,8,16,128]{3,2,1,0:T(8,128)(2,1)}, u32[]{:S(2)}, u32[]{:S(2)}) async-start(bf16[8,8,16,128]{3,2,1,0:T(8,128)(2,1)} %get-tuple-element.35), calls=%async_computation | async-start | bytes 524288 | tf_op jit(solution)/shard_map/all_to_all | solution.py:265
  82.1 3.0 %collective-permute-start.19 = (bf16[1,3,2,128,256]{4,3,2,1,0:T(8,128)(2,1)S(1)}, bf16[1,3,2,128,256]{4,3,2,1,0:T(8,128)(2,1)S(1)}, u32[]{:S(2)}, u32[]{:S(2)}) collective-permute-start(bf16[1,3,2,128,256]{4,3,2,1,0:T(8,128)(2,1)S(1)} %maximum_bitcast_fusion.p0), channel_id=1, source_target_pairs={{0,2},{1,3},{2,0},{3,1},{4,6},{5,7},{6,4},{7,5},{8,10},{9,11},{10,... | collective-permute-start | bytes 1179656 | tf_op jit(solution)/shard_map/ppermute | solution.py:195
  89.3 5.1 %collective-permute-done.16.p2 = bf16[8,128,128]{2,1,0:T(8,128)(2,1)S(1)} collective-permute-done((bf16[8,128,128]{2,1,0:T(8,128)(2,1)S(1)}, bf16[8,128,128]{2,1,0:T(8,128)(2,1)S(1)}, u32[]{:S(2)}, u32[]{:S(2)}) %collective-permute-start.16) | collective-permute-done | bytes 262176 | tf_op jit(solution)/shard_map/ppermute | solution.py:195
  94.4 4.1 %collective-permute-done.15.p1 = bf16[8,128,128]{2,1,0:T(8,128)(2,1)S(1)} collective-permute-done((bf16[8,128,128]{2,1,0:T(8,128)(2,1)S(1)}, bf16[8,128,128]{2,1,0:T(8,128)(2,1)S(1)}, u32[]{:S(2)}, u32[]{:S(2)}) %collective-permute-start.15) | collective-permute-done | bytes 262176 | tf_op jit(solution)/shard_map/ppermute | solution.py:195
  105.4 5.4 %up_terms.1 = bf16[4,128,16,128]{3,2,1,0:T(8,128)(2,1)} custom-call(s32[32]{0:T(128)S(1)} %fusion.13.spot, s32[128]{0:T(128)S(1)} %get-tuple-element.50.up_where.where, bf16[16,4,16,256]{3,2,1,0:T(8,128)(2,1)S(1)} %turn.1.xt, bf16[32,128,128]{2,1,0:T(8,128)(2,1)S(1)} %join.2.v0.v, bf16[32,128,128]{2,1,0:T(8,128)(2,1)S(1)} %collective-permute-done.21.v1), custom_call_target="tpu_custom_call" | custom-call | flops 1024 | bytes 1024 | tf_op jit(solution)/shard_map/up_terms/pallas_call | solution.py:35
  115.2 5.1 %all-to-all-start.1 = ((bf16[4,128,16,128]{3,2,1,0:T(8,128)(2,1)}), bf16[4,128,16,128]{3,2,1,0:T(8,128)(2,1)S(1)}, u32[]{:S(2)}, u32[]{:S(2)}) async-start(bf16[4,128,16,128]{3,2,1,0:T(8,128)(2,1)} %up_terms.1), calls=%async_computation.1 | async-start | bytes 4194304 | tf_op jit(solution)/shard_map/all_to_all | solution.py:271
  120.4 17.3 %collective-permute-done.24.a3 = bf16[16,128,128]{2,1,0:T(8,128)(2,1)} collective-permute-done((bf16[16,128,128]{2,1,0:T(8,128)(2,1)}, bf16[16,128,128]{2,1,0:T(8,128)(2,1)}, u32[]{:S(2)}, u32[]{:S(2)}) %collective-permute-start.24) | collective-permute-done | bytes 524320 | tf_op jit(solution)/shard_map/ppermute | solution.py:195
  146.5 5.8 %ends.1 = (bf16[2,2,128,256]{3,2,1,0:T(8,128)(2,1)S(1)}, bf16[2,2,128,256]{3,2,1,0:T(8,128)(2,1)S(1)}, bf16[2,2,128,256]{3,2,1,0:T(8,128)(2,1)S(1)}, bf16[2,2,12...) custom-call(s32[16]{0:T(128)S(1)} %fusion.9.order, s32[32]{0:T(128)S(1)} %copy-done.17, ...), custom_call_target="tpu_custom_call" | custom-call | flops 1024 | bytes 1024 | tf_op jit(solution)/shard_map/ends/pallas_call | solution.py:35
  153.1 3.1 %collective-permute-start.27 = (bf16[2,2,128,256]{3,2,1,0:T(8,128)(2,1)S(1)}, bf16[2,2,128,256]{3,2,1,0:T(8,128)(2,1)S(1)}, u32[]{:S(2)}, u32[]{:S(2)}) collective-permute-start(bf16[2,2,128,256]{3,2,1,0:T(8,128)(2,1)S(1)} %get-tuple-element.44), channel_id=1, source_target_pairs={{0,2},{1,3},{2,0},{3,1},{4,6},{5,7},{6,4},{7,5},{8,10},{9,11},{10,... | collective-permute-start | bytes 786440 | tf_op jit(solution)/shard_map/ppermute | solution.py:195
  156.4 5.8 %down_terms.1 = f32[128,16,128]{2,1,0:T(8,128)} custom-call(s32[2]{0:T(128)S(1)} %pad_add_fusion.place, s32[16]{0:T(128)S(1)} %fusion.23.spot, s32[128]{0:T(128)S(1)} %get-tuple-element.51.down_where.where, bf16[64,128,128]{2,1,0:T(8,128)(2,1)S(1)} %get-tuple-element.40.a, bf16[8,128,256]{2,1,0:T(8,128)(2,1)} %get-tuple-element.28.g0, ...), custom_call_target="tpu_custom_call" | custom-call | flops 1024 | bytes 1024 | tf_op jit(solution)/shard_map/down_terms/pallas_call | solution.py:35
  162.3 6.2 %collective-permute-done.27 = bf16[2,2,128,256]{3,2,1,0:T(8,128)(2,1)S(1)} collective-permute-done((bf16[2,2,128,256]{3,2,1,0:T(8,128)(2,1)S(1)}, bf16[2,2,128,256]{3,2,1,0:T(8,128)(2,1)S(1)}, u32[]{:S(2)}, u32[]{:S(2)}) %collective-permute-start.27) | collective-permute-done | bytes 262176 | tf_op jit(solution)/shard_map/ppermute | solution.py:195
  168.7 6.4 %collective-permute-start.29 = (bf16[2,128,256]{2,1,0:T(8,128)(2,1)S(1)}, bf16[2,128,256]{2,1,0:T(8,128)(2,1)S(1)}, u32[]{:S(2)}, u32[]{:S(2)}) collective-permute-start(bf16[2,128,256]{2,1,0:T(8,128)(2,1)S(1)} %fusion.2), channel_id=1, source_target_pairs={{0,4},{4,0},{1,5},{5,1},{2,6},{6,2},{3,7},{7,3},{8,12},{12,8},{9,1... | collective-permute-start | bytes 393224 | tf_op jit(solution)/shard_map/ppermute | solution.py:199
  175.1 6.3 %collective-permute-done.29 = bf16[2,128,256]{2,1,0:T(8,128)(2,1)S(1)} collective-permute-done((bf16[2,128,256]{2,1,0:T(8,128)(2,1)S(1)}, bf16[2,128,256]{2,1,0:T(8,128)(2,1)S(1)}, u32[]{:S(2)}, u32[]{:S(2)}) %collective-permute-start.29) | collective-permute-done | bytes 131104 | tf_op jit(solution)/shard_map/ppermute | solution.py:199
  (104 shorter events, 51.0 us)
Async XLA Ops:
  0.6 11.6 %collective-permute-start = (bf16[128,256]{1,0:T(8,128)(2,1)}, bf16[128,256]{1,0:T(8,128)(2,1)S(1)}, u32[]{:S(2)}, u32[]{:S(2)}) collective-permute-start(bf16[128,256]{1,0:T(8,128)(2,1)} %param.6), channel_id=1, source_target_pairs={{0,4},{4,0},{1,5},{5,1},{2,6},{6,2},{3,7},{7,3},{8,12},{12,8},{9,1... | collective-permute-start | bytes 196616 | tf_op jit(solution)/shard_map/ppermute | solution.py:199
  7.0 12.7 %collective-permute-start.4 = (bf16[128,256]{1,0:T(8,128)(2,1)}, bf16[128,256]{1,0:T(8,128)(2,1)S(1)}, u32[]{:S(2)}, u32[]{:S(2)}) collective-permute-start(bf16[128,256]{1,0:T(8,128)(2,1)} %param.7), channel_id=1, source_target_pairs={{0,4},{4,0},{1,5},{5,1},{2,6},{6,2},{3,7},{7,3},{8,12},{12,8},{9,1... | collective-permute-start | bytes 196616 | tf_op jit(solution)/shard_map/ppermute | solution.py:199
  13.0 9.1 %collective-permute-start.3 = (bf16[2,128,256]{2,1,0:T(8,128)(2,1)S(1)}, bf16[2,128,256]{2,1,0:T(8,128)(2,1)S(1)}, u32[]{:S(2)}, u32[]{:S(2)}) collective-permute-start(bf16[2,128,256]{2,1,0:T(8,128)(2,1)S(1)} %pad_maximum_fusion.2.x0), channel_id=1, source_target_pairs={{0,1},{1,2},{2,3},{3,0},{4,5},{5,6},{6,7},{7,4},{8,9},{9,10},{10,1... | collective-permute-start | bytes 393224 | tf_op jit(solution)/shard_map/ppermute | solution.py:195
  40.6 9.4 %collective-permute-start.8 = (bf16[8,128,256]{2,1,0:T(8,128)(2,1)S(1)}, bf16[8,128,256]{2,1,0:T(8,128)(2,1)S(1)}, u32[]{:S(2)}, u32[]{:S(2)}) collective-permute-start(bf16[8,128,256]{2,1,0:T(8,128)(2,1)S(1)} %get-tuple-element.26.x), channel_id=1, source_target_pairs={{0,32},{32,0},{1,33},{33,1},{2,34},{34,2},{3,35},{35,3},{4,36},{36... | collective-permute-start | bytes 1572872 | tf_op jit(solution)/shard_map/ppermute | solution.py:199
  40.7 21.5 %collective-permute-start.11 = (bf16[8,128,256]{2,1,0:T(8,128)(2,1)}, bf16[8,128,256]{2,1,0:T(8,128)(2,1)}, u32[]{:S(2)}, u32[]{:S(2)}) collective-permute-start(bf16[8,128,256]{2,1,0:T(8,128)(2,1)} %get-tuple-element.28.g0), channel_id=1, source_target_pairs={{0,32},{32,0},{1,33},{33,1},{2,34},{34,2},{3,35},{35,3},{4,36},{36... | collective-permute-start | bytes 1572872 | tf_op jit(solution)/shard_map/ppermute | solution.py:199
  41.2 21.0 %collective-permute-start.12 = (bf16[2,8,128,128]{3,2,1,0:T(8,128)(2,1)}, bf16[2,8,128,128]{3,2,1,0:T(8,128)(2,1)S(1)}, u32[]{:S(2)}, u32[]{:S(2)}) collective-permute-start(bf16[2,8,128,128]{3,2,1,0:T(8,128)(2,1)} %get-tuple-element.30), channel_id=1, source_target_pairs={{0,8},{8,16},{16,24},{24,0},{1,9},{9,17},{17,25},{25,1},{2,10},{10... | collective-permute-start | bytes 1572872 | tf_op jit(solution)/shard_map/ppermute | solution.py:195
  42.6 26.1 %collective-permute-start.13 = (bf16[2,8,128,128]{3,2,1,0:T(8,128)(2,1)}, bf16[2,8,128,128]{3,2,1,0:T(8,128)(2,1)S(1)}, u32[]{:S(2)}, u32[]{:S(2)}) collective-permute-start(bf16[2,8,128,128]{3,2,1,0:T(8,128)(2,1)} %get-tuple-element.31), channel_id=1, source_target_pairs={{0,16},{8,24},{16,0},{24,8},{1,17},{9,25},{17,1},{25,9},{2,18},{10... | collective-permute-start | bytes 1572872 | tf_op jit(solution)/shard_map/ppermute | solution.py:195
  46.6 22.2 %collective-permute-start.14 = (bf16[2,8,128,128]{3,2,1,0:T(8,128)(2,1)}, bf16[2,8,128,128]{3,2,1,0:T(8,128)(2,1)}, u32[]{:S(2)}, u32[]{:S(2)}) collective-permute-start(bf16[2,8,128,128]{3,2,1,0:T(8,128)(2,1)} %get-tuple-element.32), channel_id=1, source_target_pairs={{0,24},{8,0},{16,8},{24,16},{1,25},{9,1},{17,9},{25,17},{2,26},{10... | collective-permute-start | bytes 1572872 | tf_op jit(solution)/shard_map/ppermute | solution.py:195
  50.1 12.1 %collective-permute-start.10 = (bf16[2,2,128,256]{3,2,1,0:T(8,128)(2,1)}, bf16[2,2,128,256]{3,2,1,0:T(8,128)(2,1)S(1)}, u32[]{:S(2)}, u32[]{:S(2)}) collective-permute-start(bf16[2,2,128,256]{3,2,1,0:T(8,128)(2,1)} %pad_maximum_fusion.1), channel_id=1, source_target_pairs={{0,128},{64,192},{128,0},{192,64},{1,129},{65,193},{129,1},{193,65... | collective-permute-start | bytes 786440 | tf_op jit(solution)/shard_map/ppermute | solution.py:203
  72.0 15.1 %collective-permute-start.17 = (bf16[8,128,128]{2,1,0:T(8,128)(2,1)S(1)}, bf16[8,128,128]{2,1,0:T(8,128)(2,1)S(1)}, u32[]{:S(2)}, u32[]{:S(2)}) collective-permute-start(bf16[8,128,128]{2,1,0:T(8,128)(2,1)S(1)} %get-tuple-element.33.p0), channel_id=1, source_target_pairs={{0,8},{8,16},{16,24},{24,0},{1,9},{9,17},{17,25},{25,1},{2,10},{10... | collective-permute-start | bytes 786440 | tf_op jit(solution)/shard_map/ppermute | solution.py:195
  74.1 28.5 %all-to-all-start = ((bf16[8,8,16,128]{3,2,1,0:T(8,128)(2,1)}), bf16[8,8,16,128]{3,2,1,0:T(8,128)(2,1)}, u32[]{:S(2)}, u32[]{:S(2)}) async-start(bf16[8,8,16,128]{3,2,1,0:T(8,128)(2,1)} %get-tuple-element.35), calls=%async_computation | async-start | bytes 524288 | tf_op jit(solution)/shard_map/all_to_all | solution.py:265
  81.0 19.5 %collective-permute-start.20 = (bf16[1,3,2,128,256]{4,3,2,1,0:T(8,128)(2,1)S(1)}, bf16[1,3,2,128,256]{4,3,2,1,0:T(8,128)(2,1)S(1)}, u32[]{:S(2)}, u32[]{:S(2)}) collective-permute-start(bf16[1,3,2,128,256]{4,3,2,1,0:T(8,128)(2,1)S(1)} %maximum_bitcast_fusion.p0), channel_id=1, source_target_pairs={{0,1},{1,2},{2,3},{3,0},{4,5},{5,6},{6,7},{7,4},{8,9},{9,10},{10,1... | collective-permute-start | bytes 1179656 | tf_op jit(solution)/shard_map/ppermute | solution.py:195
  82.1 20.6 %collective-permute-start.19 = (bf16[1,3,2,128,256]{4,3,2,1,0:T(8,128)(2,1)S(1)}, bf16[1,3,2,128,256]{4,3,2,1,0:T(8,128)(2,1)S(1)}, u32[]{:S(2)}, u32[]{:S(2)}) collective-permute-start(bf16[1,3,2,128,256]{4,3,2,1,0:T(8,128)(2,1)S(1)} %maximum_bitcast_fusion.p0), channel_id=1, source_target_pairs={{0,2},{1,3},{2,0},{3,1},{4,6},{5,7},{6,4},{7,5},{8,10},{9,11},{10,... | collective-permute-start | bytes 1179656 | tf_op jit(solution)/shard_map/ppermute | solution.py:195
  85.1 17.6 %collective-permute-start.18 = (bf16[1,3,2,128,256]{4,3,2,1,0:T(8,128)(2,1)S(1)}, bf16[1,3,2,128,256]{4,3,2,1,0:T(8,128)(2,1)S(1)}, u32[]{:S(2)}, u32[]{:S(2)}) collective-permute-start(bf16[1,3,2,128,256]{4,3,2,1,0:T(8,128)(2,1)S(1)} %maximum_bitcast_fusion.p0), channel_id=1, source_target_pairs={{0,3},{1,0},{2,1},{3,2},{4,7},{5,4},{6,5},{7,6},{8,11},{9,8},{10,9... | collective-permute-start | bytes 1179656 | tf_op jit(solution)/shard_map/ppermute | solution.py:195
  87.8 10.7 %collective-permute-start.15 = (bf16[8,128,128]{2,1,0:T(8,128)(2,1)S(1)}, bf16[8,128,128]{2,1,0:T(8,128)(2,1)S(1)}, u32[]{:S(2)}, u32[]{:S(2)}) collective-permute-start(bf16[8,128,128]{2,1,0:T(8,128)(2,1)S(1)} %get-tuple-element.33.p0), channel_id=1, source_target_pairs={{0,24},{8,0},{16,8},{24,16},{1,25},{9,1},{17,9},{25,17},{2,26},{10... | collective-permute-start | bytes 786440 | tf_op jit(solution)/shard_map/ppermute | solution.py:195
  110.8 26.8 %collective-permute-start.24 = (bf16[16,128,128]{2,1,0:T(8,128)(2,1)}, bf16[16,128,128]{2,1,0:T(8,128)(2,1)}, u32[]{:S(2)}, u32[]{:S(2)}) collective-permute-start(bf16[16,128,128]{2,1,0:T(8,128)(2,1)} %pad_maximum_fusion.a0), channel_id=1, source_target_pairs={{0,8},{8,16},{16,24},{24,0},{1,9},{9,17},{17,25},{25,1},{2,10},{10... | collective-permute-start | bytes 1572872 | tf_op jit(solution)/shard_map/ppermute | solution.py:195
  111.5 26.1 %collective-permute-start.23 = (bf16[16,128,128]{2,1,0:T(8,128)(2,1)}, bf16[16,128,128]{2,1,0:T(8,128)(2,1)}, u32[]{:S(2)}, u32[]{:S(2)}) collective-permute-start(bf16[16,128,128]{2,1,0:T(8,128)(2,1)} %pad_maximum_fusion.a0), channel_id=1, source_target_pairs={{0,16},{8,24},{16,0},{24,8},{1,17},{9,25},{17,1},{25,9},{2,18},{10... | collective-permute-start | bytes 1572872 | tf_op jit(solution)/shard_map/ppermute | solution.py:195
  113.5 24.8 %collective-permute-start.22 = (bf16[16,128,128]{2,1,0:T(8,128)(2,1)}, bf16[16,128,128]{2,1,0:T(8,128)(2,1)}, u32[]{:S(2)}, u32[]{:S(2)}) collective-permute-start(bf16[16,128,128]{2,1,0:T(8,128)(2,1)} %pad_maximum_fusion.a0), channel_id=1, source_target_pairs={{0,24},{8,0},{16,8},{24,16},{1,25},{9,1},{17,9},{25,17},{2,26},{10... | collective-permute-start | bytes 1572872 | tf_op jit(solution)/shard_map/ppermute | solution.py:195
  115.2 66.9 %all-to-all-start.1 = ((bf16[4,128,16,128]{3,2,1,0:T(8,128)(2,1)}), bf16[4,128,16,128]{3,2,1,0:T(8,128)(2,1)S(1)}, u32[]{:S(2)}, u32[]{:S(2)}) async-start(bf16[4,128,16,128]{3,2,1,0:T(8,128)(2,1)} %up_terms.1), calls=%async_computation.1 | async-start | bytes 4194304 | tf_op jit(solution)/shard_map/all_to_all | solution.py:271
  141.3 15.1 %collective-permute-start.25 = (bf16[4,3,2,128,256]{4,3,2,1,0:T(8,128)(2,1)S(1)}, bf16[4,3,2,128,256]{4,3,2,1,0:T(8,128)(2,1)S(1)}, u32[]{:S(2)}, u32[]{:S(2)}) collective-permute-start(bf16[4,3,2,128,256]{4,3,2,1,0:T(8,128)(2,1)S(1)} %join.3.f0), channel_id=1, source_target_pairs={{0,32},{32,0},{1,33},{33,1},{2,34},{34,2},{3,35},{35,3},{4,36},{36... | collective-permute-start | bytes 4718600 | tf_op jit(solution)/shard_map/ppermute | solution.py:199
  152.3 10.0 %collective-permute-start.26 = (bf16[2,2,128,256]{3,2,1,0:T(8,128)(2,1)S(1)}, bf16[2,2,128,256]{3,2,1,0:T(8,128)(2,1)S(1)}, u32[]{:S(2)}, u32[]{:S(2)}) collective-permute-start(bf16[2,2,128,256]{3,2,1,0:T(8,128)(2,1)S(1)} %get-tuple-element.43), channel_id=1, source_target_pairs={{0,1},{1,2},{2,3},{3,0},{4,5},{5,6},{6,7},{7,4},{8,9},{9,10},{10,1... | collective-permute-start | bytes 786440 | tf_op jit(solution)/shard_map/ppermute | solution.py:195
  153.1 15.4 %collective-permute-start.27 = (bf16[2,2,128,256]{3,2,1,0:T(8,128)(2,1)S(1)}, bf16[2,2,128,256]{3,2,1,0:T(8,128)(2,1)S(1)}, u32[]{:S(2)}, u32[]{:S(2)}) collective-permute-start(bf16[2,2,128,256]{3,2,1,0:T(8,128)(2,1)S(1)} %get-tuple-element.44), channel_id=1, source_target_pairs={{0,2},{1,3},{2,0},{3,1},{4,6},{5,7},{6,4},{7,5},{8,10},{9,11},{10,... | collective-permute-start | bytes 786440 | tf_op jit(solution)/shard_map/ppermute | solution.py:195
  156.3 12.3 %collective-permute-start.28 = (bf16[2,2,128,256]{3,2,1,0:T(8,128)(2,1)S(1)}, bf16[2,2,128,256]{3,2,1,0:T(8,128)(2,1)S(1)}, u32[]{:S(2)}, u32[]{:S(2)}) collective-permute-start(bf16[2,2,128,256]{3,2,1,0:T(8,128)(2,1)S(1)} %get-tuple-element.45), channel_id=1, source_target_pairs={{0,3},{1,0},{2,1},{3,2},{4,7},{5,4},{6,5},{7,6},{8,11},{9,8},{10,9... | collective-permute-start | bytes 786440 | tf_op jit(solution)/shard_map/ppermute | solution.py:195
  168.7 12.7 %collective-permute-start.29 = (bf16[2,128,256]{2,1,0:T(8,128)(2,1)S(1)}, bf16[2,128,256]{2,1,0:T(8,128)(2,1)S(1)}, u32[]{:S(2)}, u32[]{:S(2)}) collective-permute-start(bf16[2,128,256]{2,1,0:T(8,128)(2,1)S(1)} %fusion.2), channel_id=1, source_target_pairs={{0,4},{4,0},{1,5},{5,1},{2,6},{6,2},{3,7},{7,3},{8,12},{12,8},{9,1... | collective-permute-start | bytes 393224 | tf_op jit(solution)/shard_map/ppermute | solution.py:199
  (28 other events, 197.6 us)

commit v4 on v3

--- a/solution.py
+++ b/solution.py
@@ -270,12 +270,12 @@
     )
     got = lax.all_to_all(terms, "z", 0, 0, tiled=True)
     both = jnp.concatenate([active, rows.reshape(8, BS, BS)])
-    both = pieces(after(both, terms), "row")
+    both = pieces(after(both, hidden), "row")
     *ends, a = call(
         ends_kernel, (feature_order, hidden_spots, up_where, down_where), (hidden, *both, up_blocks, down_blocks),
         [shape(2, 2, BS, 2 * BS)] * 4 + [shape(64, BS, BS)], [pltpu.VMEM((ROWS, BS, BS), F32)], name="ends",
     )
-    far[0] = after(far[0], *both[1:])
+    far[0] = after(far[0], a)
     far = join(far)
     (grad_down,) = call(
         down_terms_kernel, (place, feature_spots, down_where), (a, g, g2, far, swap(far, "q")),

time: 184 us -> 181 us (0.984)
  starting transfers between devices: 60 us -> 54.9 us
  waiting for transfers between devices: 70.6 us -> 74.5 us
  local copies, waits for them, and re-layouts: 16.4 us -> 13.9 us
    ppermute x21, starting transfers between devices: 34.7 us -> 29.6 us  [shift(): return lax.ppermute(value, axis, [(i, (i + by) % 4) for i in range(4)])]
    ppermute x7, waiting for transfers between devices: 12.1 us -> 15.3 us  [swap(): return lax.ppermute(value, axis, [(0, 1), (1, 0)])]
    unnamed x40, local copies, waits for them, and re-layouts: 15.7 us -> 13.3 us
  transfers between devices with their start and end apart: 32 -> 32, of which waited for: 16 -> 17; matrix products, arithmetic and copies ran while one was open for 4% -> 4% of each run, Pallas kernels for 7% -> 10%
where the time goes in v4:
time: 181 us; the launch traced here: 180 us
  waiting for transfers between devices  74.5 us (41%)
  starting transfers between devices  54.9 us (30%)
  Pallas kernels  29.2 us (16%)
  local copies, waits for them, and re-layouts  13.9 us (8%)
  other arithmetic  6.39 us (4%)
    ppermute x21, waiting for transfers between devices, shift(): return lax.ppermute(value, axis, [(i, (i + by) % 4) for i in range(4)])  48.1 us
    ppermute x21, starting transfers between devices, shift(): return lax.ppermute(value, axis, [(i, (i + by) % 4) for i in range(4)])  29.6 us
    pallas_call x9, Pallas kernels, call(): pl.pallas_call(kernel, out_shape=outs, in_specs=[SMEM] * len(scalars) + [...  29.2 us
    ppermute x7, waiting for transfers between devices, swap(): return lax.ppermute(value, axis, [(0, 1), (1, 0)])  15.3 us
    ppermute x7, starting transfers between devices, swap(): return lax.ppermute(value, axis, [(0, 1), (1, 0)])  13.4 us
    unnamed x40, local copies, waits for them, and re-layouts  13.3 us
    ppermute x2, waiting for transfers between devices, across(): return lax.ppermute(value, 'z', [(i, i ^ by) for i in range(4)])  11.2 us
    all_to_all x1, starting transfers between devices, local(): rows = lax.all_to_all(rows, ('z', 'q'), 0, 0, tiled=True)  5.85 us
  transfers between devices with their start and end apart: 32, of which 17 were waited for; matrix products, arithmetic and copies ran while one was open for 4% of the time, Pallas kernels for 10%

profile of v4, /device:TPU:32, one launch (start us, length us, event | category | flops | bytes accessed | tf_op | source)
XLA Modules:
  0.0 179.8 jit_solution(3423168739170086872)
XLA Ops:
  0.6 6.4 %collective-permute-start.4 = (bf16[128,256]{1,0:T(8,128)(2,1)}, bf16[128,256]{1,0:T(8,128)(2,1)S(1)}, u32[]{:S(2)}, u32[]{:S(2)}) collective-permute-start(bf16[128,256]{1,0:T(8,128)(2,1)} %param.7), channel_id=1, source_target_pairs={{0,4},{4,0},{1,5},{5,1},{2,6},{6,2},{3,7},{7,3},{8,12},{12,8},{9,1... | collective-permute-start | bytes 196616 | tf_op jit(solution)/shard_map/ppermute | solution.py:199
  7.1 5.1 %collective-permute-done.4 = bf16[128,256]{1,0:T(8,128)(2,1)S(1)} collective-permute-done((bf16[128,256]{1,0:T(8,128)(2,1)}, bf16[128,256]{1,0:T(8,128)(2,1)S(1)}, u32[]{:S(2)}, u32[]{:S(2)}) %collective-permute-start.4) | collective-permute-done | bytes 65568 | tf_op jit(solution)/shard_map/ppermute | solution.py:199
  13.0 3.1 %collective-permute-start.5 = (bf16[2,128,256]{2,1,0:T(8,128)(2,1)S(1)}, bf16[2,128,256]{2,1,0:T(8,128)(2,1)S(1)}, u32[]{:S(2)}, u32[]{:S(2)}) collective-permute-start(bf16[2,128,256]{2,1,0:T(8,128)(2,1)S(1)} %get-tuple-element.27.g0), channel_id=1, source_target_pairs={{0,3},{1,0},{2,1},{3,2},{4,7},{5,4},{6,5},{7,6},{8,11},{9,8},{10,9... | collective-permute-start | bytes 393224 | tf_op jit(solution)/shard_map/ppermute | solution.py:195
  24.8 2.4 %collective-permute-done.7.g3 = bf16[2,128,256]{2,1,0:T(8,128)(2,1)S(1)} collective-permute-done((bf16[2,128,256]{2,1,0:T(8,128)(2,1)S(1)}, bf16[2,128,256]{2,1,0:T(8,128)(2,1)S(1)}, u32[]{:S(2)}, u32[]{:S(2)}) %collective-permute-start.7) | collective-permute-done | bytes 131104 | tf_op jit(solution)/shard_map/ppermute | solution.py:195
  34.4 7.1 %first.1 = (bf16[2,8,128,128]{3,2,1,0:T(8,128)(2,1)S(1)}, bf16[2,8,128,128]{3,2,1,0:T(8,128)(2,1)}, bf16[2,8,128,128]{3,2,1,0:T(8,128)(2,1)}, bf16[2,8,128,128]{...) custom-call(s32[32]{0:T(128)S(1)} %fusion.19.order, s32[16]{0:T(128)S(1)} %fusion.23.spot, ...), custom_call_target="tpu_custom_call" | custom-call | flops 1024 | bytes 1024 | tf_op jit(solution)/shard_map/first/pallas_call | solution.py:35
  43.5 2.7 %collective-permute-start.13 = (bf16[2,8,128,128]{3,2,1,0:T(8,128)(2,1)}, bf16[2,8,128,128]{3,2,1,0:T(8,128)(2,1)S(1)}, u32[]{:S(2)}, u32[]{:S(2)}) collective-permute-start(bf16[2,8,128,128]{3,2,1,0:T(8,128)(2,1)} %get-tuple-element.31), channel_id=1, source_target_pairs={{0,16},{8,24},{16,0},{24,8},{1,17},{9,25},{17,1},{25,9},{2,18},{10... | collective-permute-start | bytes 1572872 | tf_op jit(solution)/shard_map/ppermute | solution.py:195
  47.4 2.8 %collective-permute-start.14 = (bf16[2,8,128,128]{3,2,1,0:T(8,128)(2,1)}, bf16[2,8,128,128]{3,2,1,0:T(8,128)(2,1)}, u32[]{:S(2)}, u32[]{:S(2)}) collective-permute-start(bf16[2,8,128,128]{3,2,1,0:T(8,128)(2,1)} %get-tuple-element.32), channel_id=1, source_target_pairs={{0,24},{8,0},{16,8},{24,16},{1,25},{9,1},{17,9},{25,17},{2,26},{10... | collective-permute-start | bytes 1572872 | tf_op jit(solution)/shard_map/ppermute | solution.py:195
  52.9 10.0 %collective-permute-done.10 = bf16[2,2,128,256]{3,2,1,0:T(8,128)(2,1)S(1)} collective-permute-done((bf16[2,2,128,256]{3,2,1,0:T(8,128)(2,1)}, bf16[2,2,128,256]{3,2,1,0:T(8,128)(2,1)S(1)}, u32[]{:S(2)}, u32[]{:S(2)}) %collective-permute-start.10) | collective-permute-done | bytes 262176 | tf_op jit(solution)/shard_map/ppermute | solution.py:203
  62.9 6.7 %collective-permute-done.13.p2 = bf16[2,8,128,128]{3,2,1,0:T(8,128)(2,1)S(1)} collective-permute-done((bf16[2,8,128,128]{3,2,1,0:T(8,128)(2,1)}, bf16[2,8,128,128]{3,2,1,0:T(8,128)(2,1)S(1)}, u32[]{:S(2)}, u32[]{:S(2)}) %collective-permute-start.13) | collective-permute-done | bytes 524320 | tf_op jit(solution)/shard_map/ppermute | solution.py:195
  69.6 2.6 %act.1 = (bf16[8,128,128]{2,1,0:T(8,128)(2,1)S(1)}, bf16[8,128,128]{2,1,0:T(8,128)(2,1)S(1)}, bf16[8,8,16,128]{3,2,1,0:T(8,128)(2,1)}) custom-call(bf16[2,8,128,128]{3,2,1,0:T(8,128)(2,1)S(1)} %get-tuple-element.29.p0, bf16[2,8,128,128]{3,2,1,0:T(8,128)(2,1)S(1)} %collective-permute-done.12.p1, bf16[2,8,128,128]{3,2,1,0:T(8,128)(2,1)S(1)} %collective-permute-done.13.p2, ...), custom_call_target="tpu_custom_call" | custom-call | flops 1024 | bytes 1024 | tf_op jit(solution)/shard_map/act/pallas_call | solution.py:35
  72.9 2.4 %collective-permute-start.15 = (bf16[8,128,128]{2,1,0:T(8,128)(2,1)S(1)}, bf16[8,128,128]{2,1,0:T(8,128)(2,1)S(1)}, u32[]{:S(2)}, u32[]{:S(2)}) collective-permute-start(bf16[8,128,128]{2,1,0:T(8,128)(2,1)S(1)} %get-tuple-element.33.p0), channel_id=1, source_target_pairs={{0,24},{8,0},{16,8},{24,16},{1,25},{9,1},{17,9},{25,17},{2,26},{10... | collective-permute-start | bytes 786440 | tf_op jit(solution)/shard_map/ppermute | solution.py:195
  75.3 5.9 %all-to-all-start = ((bf16[8,8,16,128]{3,2,1,0:T(8,128)(2,1)}), bf16[8,8,16,128]{3,2,1,0:T(8,128)(2,1)}, u32[]{:S(2)}, u32[]{:S(2)}) async-start(bf16[8,8,16,128]{3,2,1,0:T(8,128)(2,1)} %get-tuple-element.35), calls=%async_computation | async-start | bytes 524288 | tf_op jit(solution)/shard_map/all_to_all | solution.py:265
  87.4 8.3 %collective-permute-done.16.p2 = bf16[8,128,128]{2,1,0:T(8,128)(2,1)S(1)} collective-permute-done((bf16[8,128,128]{2,1,0:T(8,128)(2,1)S(1)}, bf16[8,128,128]{2,1,0:T(8,128)(2,1)S(1)}, u32[]{:S(2)}, u32[]{:S(2)}) %collective-permute-start.16) | collective-permute-done | bytes 262176 | tf_op jit(solution)/shard_map/ppermute | solution.py:195
  95.7 3.8 %collective-permute-done.17.p3 = bf16[8,128,128]{2,1,0:T(8,128)(2,1)S(1)} collective-permute-done((bf16[8,128,128]{2,1,0:T(8,128)(2,1)S(1)}, bf16[8,128,128]{2,1,0:T(8,128)(2,1)S(1)}, u32[]{:S(2)}, u32[]{:S(2)}) %collective-permute-start.17) | collective-permute-done | bytes 262176 | tf_op jit(solution)/shard_map/ppermute | solution.py:195
  101.6 2.3 %collective-permute-done.23.p3 = bf16[1,3,2,128,256]{4,3,2,1,0:T(8,128)(2,1)S(1)} collective-permute-done((bf16[1,3,2,128,256]{4,3,2,1,0:T(8,128)(2,1)S(1)}, bf16[1,3,2,128,256]{4,3,2,1,0:T(8,128)(2,1)S(1)}, u32[]{:S(2)}, u32[]{:S(2)}) %collective-permute-start.23) | collective-permute-done | bytes 393248 | tf_op jit(solution)/shard_map/ppermute | solution.py:195
  109.1 5.4 %up_terms.1 = bf16[4,128,16,128]{3,2,1,0:T(8,128)(2,1)} custom-call(s32[32]{0:T(128)S(1)} %fusion.13.spot, s32[128]{0:T(128)S(1)} %get-tuple-element.50.up_where.where, bf16[16,4,16,256]{3,2,1,0:T(8,128)(2,1)S(1)} %turn.1.xt, bf16[32,128,128]{2,1,0:T(8,128)(2,1)S(1)} %join.2.v.v0, bf16[32,128,128]{2,1,0:T(8,128)(2,1)S(1)} %collective-permute-done.29.v1), custom_call_target="tpu_custom_call" | custom-call | flops 1024 | bytes 1024 | tf_op jit(solution)/shard_map/up_terms/pallas_call | solution.py:35
  115.0 5.1 %all-to-all-start.1 = ((bf16[4,128,16,128]{3,2,1,0:T(8,128)(2,1)}), bf16[4,128,16,128]{3,2,1,0:T(8,128)(2,1)S(1)}, u32[]{:S(2)}, u32[]{:S(2)}) async-start(bf16[4,128,16,128]{3,2,1,0:T(8,128)(2,1)} %up_terms.1), calls=%async_computation.1 | async-start | bytes 4194304 | tf_op jit(solution)/shard_map/all_to_all | solution.py:271
  120.9 2.6 %collective-permute-done.19.a2 = bf16[16,128,128]{2,1,0:T(8,128)(2,1)} collective-permute-done((bf16[16,128,128]{2,1,0:T(8,128)(2,1)}, bf16[16,128,128]{2,1,0:T(8,128)(2,1)}, u32[]{:S(2)}, u32[]{:S(2)}) %collective-permute-start.19) | collective-permute-done | bytes 524320 | tf_op jit(solution)/shard_map/ppermute | solution.py:195
  123.5 10.3 %collective-permute-done.20.a3 = bf16[16,128,128]{2,1,0:T(8,128)(2,1)} collective-permute-done((bf16[16,128,128]{2,1,0:T(8,128)(2,1)}, bf16[16,128,128]{2,1,0:T(8,128)(2,1)}, u32[]{:S(2)}, u32[]{:S(2)}) %collective-permute-start.20) | collective-permute-done | bytes 524320 | tf_op jit(solution)/shard_map/ppermute | solution.py:195
  138.8 5.9 %ends.1 = (bf16[2,2,128,256]{3,2,1,0:T(8,128)(2,1)S(1)}, bf16[2,2,128,256]{3,2,1,0:T(8,128)(2,1)S(1)}, bf16[2,2,128,256]{3,2,1,0:T(8,128)(2,1)S(1)}, bf16[2,2,12...) custom-call(s32[16]{0:T(128)S(1)} %fusion.9.order, s32[32]{0:T(128)S(1)} %copy-done.17, ...), custom_call_target="tpu_custom_call" | custom-call | flops 1024 | bytes 1024 | tf_op jit(solution)/shard_map/ends/pallas_call | solution.py:35
  148.7 5.8 %down_terms.1 = f32[128,16,128]{2,1,0:T(8,128)} custom-call(s32[2]{0:T(128)S(1)} %pad_add_fusion.place, s32[16]{0:T(128)S(1)} %fusion.23.spot, s32[128]{0:T(128)S(1)} %get-tuple-element.51.down_where.where, bf16[64,128,128]{2,1,0:T(8,128)(2,1)S(1)} %get-tuple-element.38.a, bf16[8,128,256]{2,1,0:T(8,128)(2,1)} %get-tuple-element.28.g0, ...), custom_call_target="tpu_custom_call" | custom-call | flops 1024 | bytes 1024 | tf_op jit(solution)/shard_map/down_terms/pallas_call | solution.py:35
  154.5 6.1 %collective-permute-done.25 = bf16[2,2,128,256]{3,2,1,0:T(8,128)(2,1)S(1)} collective-permute-done((bf16[2,2,128,256]{3,2,1,0:T(8,128)(2,1)S(1)}, bf16[2,2,128,256]{3,2,1,0:T(8,128)(2,1)S(1)}, u32[]{:S(2)}, u32[]{:S(2)}) %collective-permute-start.25) | collective-permute-done | bytes 262176 | tf_op jit(solution)/shard_map/ppermute | solution.py:195
  161.4 6.3 %collective-permute-start.28 = (bf16[2,128,256]{2,1,0:T(8,128)(2,1)S(1)}, bf16[2,128,256]{2,1,0:T(8,128)(2,1)S(1)}, u32[]{:S(2)}, u32[]{:S(2)}) collective-permute-start(bf16[2,128,256]{2,1,0:T(8,128)(2,1)S(1)} %fusion.2), channel_id=1, source_target_pairs={{0,4},{4,0},{1,5},{5,1},{2,6},{6,2},{3,7},{7,3},{8,12},{12,8},{9,1... | collective-permute-start | bytes 393224 | tf_op jit(solution)/shard_map/ppermute | solution.py:199
  167.7 10.2 %collective-permute-done.28 = bf16[2,128,256]{2,1,0:T(8,128)(2,1)S(1)} collective-permute-done((bf16[2,128,256]{2,1,0:T(8,128)(2,1)S(1)}, bf16[2,128,256]{2,1,0:T(8,128)(2,1)S(1)}, u32[]{:S(2)}, u32[]{:S(2)}) %collective-permute-start.28) | collective-permute-done | bytes 131104 | tf_op jit(solution)/shard_map/ppermute | solution.py:199
  (104 shorter events, 49.7 us)
Async XLA Ops:
  0.6 11.6 %collective-permute-start.4 = (bf16[128,256]{1,0:T(8,128)(2,1)}, bf16[128,256]{1,0:T(8,128)(2,1)S(1)}, u32[]{:S(2)}, u32[]{:S(2)}) collective-permute-start(bf16[128,256]{1,0:T(8,128)(2,1)} %param.7), channel_id=1, source_target_pairs={{0,4},{4,0},{1,5},{5,1},{2,6},{6,2},{3,7},{7,3},{8,12},{12,8},{9,1... | collective-permute-start | bytes 196616 | tf_op jit(solution)/shard_map/ppermute | solution.py:199
  7.0 11.5 %collective-permute-start = (bf16[128,256]{1,0:T(8,128)(2,1)}, bf16[128,256]{1,0:T(8,128)(2,1)S(1)}, u32[]{:S(2)}, u32[]{:S(2)}) collective-permute-start(bf16[128,256]{1,0:T(8,128)(2,1)} %param.6), channel_id=1, source_target_pairs={{0,4},{4,0},{1,5},{5,1},{2,6},{6,2},{3,7},{7,3},{8,12},{12,8},{9,1... | collective-permute-start | bytes 196616 | tf_op jit(solution)/shard_map/ppermute | solution.py:199
  13.0 10.4 %collective-permute-start.5 = (bf16[2,128,256]{2,1,0:T(8,128)(2,1)S(1)}, bf16[2,128,256]{2,1,0:T(8,128)(2,1)S(1)}, u32[]{:S(2)}, u32[]{:S(2)}) collective-permute-start(bf16[2,128,256]{2,1,0:T(8,128)(2,1)S(1)} %get-tuple-element.27.g0), channel_id=1, source_target_pairs={{0,3},{1,0},{2,1},{3,2},{4,7},{5,4},{6,5},{7,6},{8,11},{9,8},{10,9... | collective-permute-start | bytes 393224 | tf_op jit(solution)/shard_map/ppermute | solution.py:195
  17.6 9.6 %collective-permute-start.7 = (bf16[2,128,256]{2,1,0:T(8,128)(2,1)S(1)}, bf16[2,128,256]{2,1,0:T(8,128)(2,1)S(1)}, u32[]{:S(2)}, u32[]{:S(2)}) collective-permute-start(bf16[2,128,256]{2,1,0:T(8,128)(2,1)S(1)} %get-tuple-element.27.g0), channel_id=1, source_target_pairs={{0,1},{1,2},{2,3},{3,0},{4,5},{5,6},{6,7},{7,4},{8,9},{9,10},{10,1... | collective-permute-start | bytes 393224 | tf_op jit(solution)/shard_map/ppermute | solution.py:195
  41.5 21.3 %collective-permute-start.11 = (bf16[8,128,256]{2,1,0:T(8,128)(2,1)}, bf16[8,128,256]{2,1,0:T(8,128)(2,1)}, u32[]{:S(2)}, u32[]{:S(2)}) collective-permute-start(bf16[8,128,256]{2,1,0:T(8,128)(2,1)} %get-tuple-element.28.g0), channel_id=1, source_target_pairs={{0,32},{32,0},{1,33},{33,1},{2,34},{34,2},{3,35},{35,3},{4,36},{36... | collective-permute-start | bytes 1572872 | tf_op jit(solution)/shard_map/ppermute | solution.py:199
  42.0 20.8 %collective-permute-start.12 = (bf16[2,8,128,128]{3,2,1,0:T(8,128)(2,1)}, bf16[2,8,128,128]{3,2,1,0:T(8,128)(2,1)S(1)}, u32[]{:S(2)}, u32[]{:S(2)}) collective-permute-start(bf16[2,8,128,128]{3,2,1,0:T(8,128)(2,1)} %get-tuple-element.30), channel_id=1, source_target_pairs={{0,8},{8,16},{16,24},{24,0},{1,9},{9,17},{17,25},{25,1},{2,10},{10... | collective-permute-start | bytes 1572872 | tf_op jit(solution)/shard_map/ppermute | solution.py:195
  43.5 26.1 %collective-permute-start.13 = (bf16[2,8,128,128]{3,2,1,0:T(8,128)(2,1)}, bf16[2,8,128,128]{3,2,1,0:T(8,128)(2,1)S(1)}, u32[]{:S(2)}, u32[]{:S(2)}) collective-permute-start(bf16[2,8,128,128]{3,2,1,0:T(8,128)(2,1)} %get-tuple-element.31), channel_id=1, source_target_pairs={{0,16},{8,24},{16,0},{24,8},{1,17},{9,25},{17,1},{25,9},{2,18},{10... | collective-permute-start | bytes 1572872 | tf_op jit(solution)/shard_map/ppermute | solution.py:195
  47.4 22.2 %collective-permute-start.14 = (bf16[2,8,128,128]{3,2,1,0:T(8,128)(2,1)}, bf16[2,8,128,128]{3,2,1,0:T(8,128)(2,1)}, u32[]{:S(2)}, u32[]{:S(2)}) collective-permute-start(bf16[2,8,128,128]{3,2,1,0:T(8,128)(2,1)} %get-tuple-element.32), channel_id=1, source_target_pairs={{0,24},{8,0},{16,8},{24,16},{1,25},{9,1},{17,9},{25,17},{2,26},{10... | collective-permute-start | bytes 1572872 | tf_op jit(solution)/shard_map/ppermute | solution.py:195
  50.9 11.9 %collective-permute-start.10 = (bf16[2,2,128,256]{3,2,1,0:T(8,128)(2,1)}, bf16[2,2,128,256]{3,2,1,0:T(8,128)(2,1)S(1)}, u32[]{:S(2)}, u32[]{:S(2)}) collective-permute-start(bf16[2,2,128,256]{3,2,1,0:T(8,128)(2,1)} %pad_maximum_fusion.1), channel_id=1, source_target_pairs={{0,128},{64,192},{128,0},{192,64},{1,129},{65,193},{129,1},{193,65... | collective-permute-start | bytes 786440 | tf_op jit(solution)/shard_map/ppermute | solution.py:203
  72.9 13.8 %collective-permute-start.15 = (bf16[8,128,128]{2,1,0:T(8,128)(2,1)S(1)}, bf16[8,128,128]{2,1,0:T(8,128)(2,1)S(1)}, u32[]{:S(2)}, u32[]{:S(2)}) collective-permute-start(bf16[8,128,128]{2,1,0:T(8,128)(2,1)S(1)} %get-tuple-element.33.p0), channel_id=1, source_target_pairs={{0,24},{8,0},{16,8},{24,16},{1,25},{9,1},{17,9},{25,17},{2,26},{10... | collective-permute-start | bytes 786440 | tf_op jit(solution)/shard_map/ppermute | solution.py:195
  75.3 28.6 %all-to-all-start = ((bf16[8,8,16,128]{3,2,1,0:T(8,128)(2,1)}), bf16[8,8,16,128]{3,2,1,0:T(8,128)(2,1)}, u32[]{:S(2)}, u32[]{:S(2)}) async-start(bf16[8,8,16,128]{3,2,1,0:T(8,128)(2,1)} %get-tuple-element.35), calls=%async_computation | async-start | bytes 524288 | tf_op jit(solution)/shard_map/all_to_all | solution.py:265
  82.1 19.4 %collective-permute-start.21 = (bf16[1,3,2,128,256]{4,3,2,1,0:T(8,128)(2,1)S(1)}, bf16[1,3,2,128,256]{4,3,2,1,0:T(8,128)(2,1)S(1)}, u32[]{:S(2)}, u32[]{:S(2)}) collective-permute-start(bf16[1,3,2,128,256]{4,3,2,1,0:T(8,128)(2,1)S(1)} %maximum_bitcast_fusion.p0), channel_id=1, source_target_pairs={{0,3},{1,0},{2,1},{3,2},{4,7},{5,4},{6,5},{7,6},{8,11},{9,8},{10,9... | collective-permute-start | bytes 1179656 | tf_op jit(solution)/shard_map/ppermute | solution.py:195
  83.1 18.5 %collective-permute-start.22 = (bf16[1,3,2,128,256]{4,3,2,1,0:T(8,128)(2,1)S(1)}, bf16[1,3,2,128,256]{4,3,2,1,0:T(8,128)(2,1)S(1)}, u32[]{:S(2)}, u32[]{:S(2)}) collective-permute-start(bf16[1,3,2,128,256]{4,3,2,1,0:T(8,128)(2,1)S(1)} %maximum_bitcast_fusion.p0), channel_id=1, source_target_pairs={{0,2},{1,3},{2,0},{3,1},{4,6},{5,7},{6,4},{7,5},{8,10},{9,11},{10,... | collective-permute-start | bytes 1179656 | tf_op jit(solution)/shard_map/ppermute | solution.py:195
  84.0 19.9 %collective-permute-start.23 = (bf16[1,3,2,128,256]{4,3,2,1,0:T(8,128)(2,1)S(1)}, bf16[1,3,2,128,256]{4,3,2,1,0:T(8,128)(2,1)S(1)}, u32[]{:S(2)}, u32[]{:S(2)}) collective-permute-start(bf16[1,3,2,128,256]{4,3,2,1,0:T(8,128)(2,1)S(1)} %maximum_bitcast_fusion.p0), channel_id=1, source_target_pairs={{0,1},{1,2},{2,3},{3,0},{4,5},{5,6},{6,7},{7,4},{8,9},{9,10},{10,1... | collective-permute-start | bytes 1179656 | tf_op jit(solution)/shard_map/ppermute | solution.py:195
  84.9 10.8 %collective-permute-start.16 = (bf16[8,128,128]{2,1,0:T(8,128)(2,1)S(1)}, bf16[8,128,128]{2,1,0:T(8,128)(2,1)S(1)}, u32[]{:S(2)}, u32[]{:S(2)}) collective-permute-start(bf16[8,128,128]{2,1,0:T(8,128)(2,1)S(1)} %get-tuple-element.33.p0), channel_id=1, source_target_pairs={{0,16},{8,24},{16,0},{24,8},{1,17},{9,25},{17,1},{25,9},{2,18},{10... | collective-permute-start | bytes 786440 | tf_op jit(solution)/shard_map/ppermute | solution.py:195
  87.4 12.1 %collective-permute-start.17 = (bf16[8,128,128]{2,1,0:T(8,128)(2,1)S(1)}, bf16[8,128,128]{2,1,0:T(8,128)(2,1)S(1)}, u32[]{:S(2)}, u32[]{:S(2)}) collective-permute-start(bf16[8,128,128]{2,1,0:T(8,128)(2,1)S(1)} %get-tuple-element.33.p0), channel_id=1, source_target_pairs={{0,8},{8,16},{16,24},{24,0},{1,9},{9,17},{17,25},{25,1},{2,10},{10... | collective-permute-start | bytes 786440 | tf_op jit(solution)/shard_map/ppermute | solution.py:195
  105.9 15.1 %collective-permute-start.18 = (bf16[16,128,128]{2,1,0:T(8,128)(2,1)}, bf16[16,128,128]{2,1,0:T(8,128)(2,1)}, u32[]{:S(2)}, u32[]{:S(2)}) collective-permute-start(bf16[16,128,128]{2,1,0:T(8,128)(2,1)} %pad_maximum_fusion.a0), channel_id=1, source_target_pairs={{0,24},{8,0},{16,8},{24,16},{1,25},{9,1},{17,9},{25,17},{2,26},{10... | collective-permute-start | bytes 1572872 | tf_op jit(solution)/shard_map/ppermute | solution.py:195
  106.8 16.6 %collective-permute-start.19 = (bf16[16,128,128]{2,1,0:T(8,128)(2,1)}, bf16[16,128,128]{2,1,0:T(8,128)(2,1)}, u32[]{:S(2)}, u32[]{:S(2)}) collective-permute-start(bf16[16,128,128]{2,1,0:T(8,128)(2,1)} %pad_maximum_fusion.a0), channel_id=1, source_target_pairs={{0,16},{8,24},{16,0},{24,8},{1,17},{9,25},{17,1},{25,9},{2,18},{10... | collective-permute-start | bytes 1572872 | tf_op jit(solution)/shard_map/ppermute | solution.py:195
  107.9 25.9 %collective-permute-start.20 = (bf16[16,128,128]{2,1,0:T(8,128)(2,1)}, bf16[16,128,128]{2,1,0:T(8,128)(2,1)}, u32[]{:S(2)}, u32[]{:S(2)}) collective-permute-start(bf16[16,128,128]{2,1,0:T(8,128)(2,1)} %pad_maximum_fusion.a0), channel_id=1, source_target_pairs={{0,8},{8,16},{16,24},{24,0},{1,9},{9,17},{17,25},{25,1},{2,10},{10... | collective-permute-start | bytes 1572872 | tf_op jit(solution)/shard_map/ppermute | solution.py:195
  115.0 63.5 %all-to-all-start.1 = ((bf16[4,128,16,128]{3,2,1,0:T(8,128)(2,1)}), bf16[4,128,16,128]{3,2,1,0:T(8,128)(2,1)S(1)}, u32[]{:S(2)}, u32[]{:S(2)}) async-start(bf16[4,128,16,128]{3,2,1,0:T(8,128)(2,1)} %up_terms.1), calls=%async_computation.1 | async-start | bytes 4194304 | tf_op jit(solution)/shard_map/all_to_all | solution.py:271
  145.0 15.5 %collective-permute-start.25 = (bf16[2,2,128,256]{3,2,1,0:T(8,128)(2,1)S(1)}, bf16[2,2,128,256]{3,2,1,0:T(8,128)(2,1)S(1)}, u32[]{:S(2)}, u32[]{:S(2)}) collective-permute-start(bf16[2,2,128,256]{3,2,1,0:T(8,128)(2,1)S(1)} %get-tuple-element.42), channel_id=1, source_target_pairs={{0,1},{1,2},{2,3},{3,0},{4,5},{5,6},{6,7},{7,4},{8,9},{9,10},{10,1... | collective-permute-start | bytes 786440 | tf_op jit(solution)/shard_map/ppermute | solution.py:195
  145.1 15.5 %collective-permute-start.26 = (bf16[2,2,128,256]{3,2,1,0:T(8,128)(2,1)S(1)}, bf16[2,2,128,256]{3,2,1,0:T(8,128)(2,1)S(1)}, u32[]{:S(2)}, u32[]{:S(2)}) collective-permute-start(bf16[2,2,128,256]{3,2,1,0:T(8,128)(2,1)S(1)} %get-tuple-element.43), channel_id=1, source_target_pairs={{0,2},{1,3},{2,0},{3,1},{4,6},{5,7},{6,4},{7,5},{8,10},{9,11},{10,... | collective-permute-start | bytes 786440 | tf_op jit(solution)/shard_map/ppermute | solution.py:195
  147.2 14.0 %collective-permute-start.27 = (bf16[2,2,128,256]{3,2,1,0:T(8,128)(2,1)S(1)}, bf16[2,2,128,256]{3,2,1,0:T(8,128)(2,1)S(1)}, u32[]{:S(2)}, u32[]{:S(2)}) collective-permute-start(bf16[2,2,128,256]{3,2,1,0:T(8,128)(2,1)S(1)} %get-tuple-element.44), channel_id=1, source_target_pairs={{0,3},{1,0},{2,1},{3,2},{4,7},{5,4},{6,5},{7,6},{8,11},{9,8},{10,9... | collective-permute-start | bytes 786440 | tf_op jit(solution)/shard_map/ppermute | solution.py:195
  161.4 16.5 %collective-permute-start.28 = (bf16[2,128,256]{2,1,0:T(8,128)(2,1)S(1)}, bf16[2,128,256]{2,1,0:T(8,128)(2,1)S(1)}, u32[]{:S(2)}, u32[]{:S(2)}) collective-permute-start(bf16[2,128,256]{2,1,0:T(8,128)(2,1)S(1)} %fusion.2), channel_id=1, source_target_pairs={{0,4},{4,0},{1,5},{5,1},{2,6},{6,2},{3,7},{7,3},{8,12},{12,8},{9,1... | collective-permute-start | bytes 393224 | tf_op jit(solution)/shard_map/ppermute | solution.py:199
  (28 other events, 215.3 us)

commit v5 on v4

--- a/solution.py
+++ b/solution.py
@@ -261,10 +261,12 @@
     (turned,) = call(turn_kernel, (place,), (x, x2), [shape(ROWS, 4, 16, 2 * BS)], name="turn")
     parts[0] = after(parts[0], turned, far2, g2)
     active, own, rows = call(act_kernel, (), parts, [piece, piece, shape(8, 8, 16, BS)], name="act")
-    far = pieces(after(jnp.concatenate([far1[None], far2])[None], own), "y")
     rows = lax.all_to_all(rows, ("z", "q"), 0, 0, tiled=True)
-    hidden = join(pieces(own, "row"))
-    hidden2 = swap(after(hidden, rows, *far[1:]), "q")
+    hidden = pieces(own, "row")
+    hidden[0] = after(hidden[0], rows)
+    hidden = join(hidden)
+    far = pieces(after(jnp.concatenate([far1[None], far2])[None], hidden), "y")
+    hidden2 = swap(hidden, "q")
     (terms,) = call(
         up_terms_kernel, (hidden_spots, up_where), (turned, hidden, hidden2), [shape(4, 128, 16, BS)], name="up_terms"
     )

time: 181 us -> 171 us (0.945)
  local copies, waits for them, and re-layouts: 13.9 us -> 10.4 us
  waiting for transfers between devices: 74.5 us -> 71.2 us
    ppermute x21, waiting for transfers between devices: 48.1 us -> 40.4 us  [shift(): return lax.ppermute(value, axis, [(i, (i + by) % 4) for i in range(4)])]
    all_to_all x1, waiting for transfers between devices: 0.01 us -> 3.71 us  [local(): rows = lax.all_to_all(rows, ('z', 'q'), 0, 0, tiled=True)]
    unnamed x40 -> x14, local copies, waits for them, and re-layouts: 13.3 us -> 9.71 us
  transfers between devices with their start and end apart: 32 -> 32, of which waited for: 17 -> 16; matrix products, arithmetic and copies ran while one was open for 4% -> 3% of each run, Pallas kernels for 10% -> 11%
where the time goes in v5:
time: 171 us; the launch traced here: 170 us
  waiting for transfers between devices  71.2 us (42%)
  starting transfers between devices  53.4 us (31%)
  Pallas kernels  29.1 us (17%)
  local copies, waits for them, and re-layouts  10.4 us (6%)
  other arithmetic  5.26 us (3%)
    ppermute x21, waiting for transfers between devices, shift(): return lax.ppermute(value, axis, [(i, (i + by) % 4) for i in range(4)])  40.4 us
    pallas_call x9, Pallas kernels, call(): pl.pallas_call(kernel, out_shape=outs, in_specs=[SMEM] * len(scalars) + [...  29.1 us
    ppermute x21, starting transfers between devices, shift(): return lax.ppermute(value, axis, [(i, (i + by) % 4) for i in range(4)])  28.7 us
    ppermute x7, waiting for transfers between devices, swap(): return lax.ppermute(value, axis, [(0, 1), (1, 0)])  15.8 us
    ppermute x7, starting transfers between devices, swap(): return lax.ppermute(value, axis, [(0, 1), (1, 0)])  13.5 us
    ppermute x2, waiting for transfers between devices, across(): return lax.ppermute(value, 'z', [(i, i ^ by) for i in range(4)])  11.2 us
    unnamed x14, local copies, waits for them, and re-layouts  9.71 us
    all_to_all x1, starting transfers between devices, local(): rows = lax.all_to_all(rows, ('z', 'q'), 0, 0, tiled=True)  5.25 us
  transfers between devices with their start and end apart: 32, of which 16 were waited for; matrix products, arithmetic and copies ran while one was open for 3% of the time, Pallas kernels for 11%

profile of v5, /device:TPU:32, one launch (start us, length us, event | category | flops | bytes accessed | tf_op | source)
XLA Modules:
  0.0 170.0 jit_solution(13880389686130227102)
XLA Ops:
  0.6 6.4 %collective-permute-start = (bf16[128,256]{1,0:T(8,128)(2,1)}, bf16[128,256]{1,0:T(8,128)(2,1)S(1)}, u32[]{:S(2)}, u32[]{:S(2)}) collective-permute-start(bf16[128,256]{1,0:T(8,128)(2,1)} %param.6), channel_id=1, source_target_pairs={{0,4},{4,0},{1,5},{5,1},{2,6},{6,2},{3,7},{7,3},{8,12},{12,8},{9,1... | collective-permute-start | bytes 196616 | tf_op jit(solution)/shard_map/ppermute | solution.py:199
  7.1 5.1 %collective-permute-done = bf16[128,256]{1,0:T(8,128)(2,1)S(1)} collective-permute-done((bf16[128,256]{1,0:T(8,128)(2,1)}, bf16[128,256]{1,0:T(8,128)(2,1)S(1)}, u32[]{:S(2)}, u32[]{:S(2)}) %collective-permute-start) | collective-permute-done | bytes 65568 | tf_op jit(solution)/shard_map/ppermute | solution.py:199
  13.0 3.1 %collective-permute-start.1 = (bf16[2,128,256]{2,1,0:T(8,128)(2,1)S(1)}, bf16[2,128,256]{2,1,0:T(8,128)(2,1)S(1)}, u32[]{:S(2)}, u32[]{:S(2)}) collective-permute-start(bf16[2,128,256]{2,1,0:T(8,128)(2,1)S(1)} %pad_maximum_fusion.2.x0), channel_id=1, source_target_pairs={{0,3},{1,0},{2,1},{3,2},{4,7},{5,4},{6,5},{7,6},{8,11},{9,8},{10,9... | collective-permute-start | bytes 393224 | tf_op jit(solution)/shard_map/ppermute | solution.py:195
  24.8 2.4 %collective-permute-done.3.x3 = bf16[2,128,256]{2,1,0:T(8,128)(2,1)S(1)} collective-permute-done((bf16[2,128,256]{2,1,0:T(8,128)(2,1)S(1)}, bf16[2,128,256]{2,1,0:T(8,128)(2,1)S(1)}, u32[]{:S(2)}, u32[]{:S(2)}) %collective-permute-start.3) | collective-permute-done | bytes 131104 | tf_op jit(solution)/shard_map/ppermute | solution.py:195
  34.4 7.1 %first.1 = (bf16[2,8,128,128]{3,2,1,0:T(8,128)(2,1)S(1)}, bf16[2,8,128,128]{3,2,1,0:T(8,128)(2,1)}, bf16[2,8,128,128]{3,2,1,0:T(8,128)(2,1)}, bf16[2,8,128,128]{...) custom-call(s32[32]{0:T(128)S(1)} %fusion.19.order, s32[16]{0:T(128)S(1)} %fusion.23.spot, ...), custom_call_target="tpu_custom_call" | custom-call | flops 1024 | bytes 1024 | tf_op jit(solution)/shard_map/first/pallas_call | solution.py:35
  43.5 2.7 %collective-permute-start.13 = (bf16[2,8,128,128]{3,2,1,0:T(8,128)(2,1)}, bf16[2,8,128,128]{3,2,1,0:T(8,128)(2,1)S(1)}, u32[]{:S(2)}, u32[]{:S(2)}) collective-permute-start(bf16[2,8,128,128]{3,2,1,0:T(8,128)(2,1)} %get-tuple-element.31), channel_id=1, source_target_pairs={{0,16},{8,24},{16,0},{24,8},{1,17},{9,25},{17,1},{25,9},{2,18},{10... | collective-permute-start | bytes 1572872 | tf_op jit(solution)/shard_map/ppermute | solution.py:195
  47.4 2.8 %collective-permute-start.14 = (bf16[2,8,128,128]{3,2,1,0:T(8,128)(2,1)}, bf16[2,8,128,128]{3,2,1,0:T(8,128)(2,1)}, u32[]{:S(2)}, u32[]{:S(2)}) collective-permute-start(bf16[2,8,128,128]{3,2,1,0:T(8,128)(2,1)} %get-tuple-element.32), channel_id=1, source_target_pairs={{0,24},{8,0},{16,8},{24,16},{1,25},{9,1},{17,9},{25,17},{2,26},{10... | collective-permute-start | bytes 1572872 | tf_op jit(solution)/shard_map/ppermute | solution.py:195
  52.8 10.0 %collective-permute-done.10 = bf16[2,2,128,256]{3,2,1,0:T(8,128)(2,1)S(1)} collective-permute-done((bf16[2,2,128,256]{3,2,1,0:T(8,128)(2,1)}, bf16[2,2,128,256]{3,2,1,0:T(8,128)(2,1)S(1)}, u32[]{:S(2)}, u32[]{:S(2)}) %collective-permute-start.10) | collective-permute-done | bytes 262176 | tf_op jit(solution)/shard_map/ppermute | solution.py:203
  62.9 6.7 %collective-permute-done.13.p2 = bf16[2,8,128,128]{3,2,1,0:T(8,128)(2,1)S(1)} collective-permute-done((bf16[2,8,128,128]{3,2,1,0:T(8,128)(2,1)}, bf16[2,8,128,128]{3,2,1,0:T(8,128)(2,1)S(1)}, u32[]{:S(2)}, u32[]{:S(2)}) %collective-permute-start.13) | collective-permute-done | bytes 524320 | tf_op jit(solution)/shard_map/ppermute | solution.py:195
  69.6 2.6 %act.1 = (bf16[8,128,128]{2,1,0:T(8,128)(2,1)S(1)}, bf16[8,128,128]{2,1,0:T(8,128)(2,1)S(1)}, bf16[8,8,16,128]{3,2,1,0:T(8,128)(2,1)}) custom-call(bf16[2,8,128,128]{3,2,1,0:T(8,128)(2,1)S(1)} %get-tuple-element.29.p0, bf16[2,8,128,128]{3,2,1,0:T(8,128)(2,1)S(1)} %collective-permute-done.12.p1, bf16[2,8,128,128]{3,2,1,0:T(8,128)(2,1)S(1)} %collective-permute-done.13.p2, ...), custom_call_target="tpu_custom_call" | custom-call | flops 1024 | bytes 1024 | tf_op jit(solution)/shard_map/act/pallas_call | solution.py:35
  72.2 5.3 %all-to-all-start = ((bf16[8,8,16,128]{3,2,1,0:T(8,128)(2,1)}), bf16[8,8,16,128]{3,2,1,0:T(8,128)(2,1)S(1)}, u32[]{:S(2)}, u32[]{:S(2)}) async-start(bf16[8,8,16,128]{3,2,1,0:T(8,128)(2,1)} %get-tuple-element.34), calls=%async_computation | async-start | bytes 524288 | tf_op jit(solution)/shard_map/all_to_all | solution.py:264
  77.4 2.4 %collective-permute-start.15 = (bf16[8,128,128]{2,1,0:T(8,128)(2,1)S(1)}, bf16[8,128,128]{2,1,0:T(8,128)(2,1)S(1)}, u32[]{:S(2)}, u32[]{:S(2)}) collective-permute-start(bf16[8,128,128]{2,1,0:T(8,128)(2,1)S(1)} %get-tuple-element.35.p0), channel_id=1, source_target_pairs={{0,24},{8,0},{16,8},{24,16},{1,25},{9,1},{17,9},{25,17},{2,26},{10... | collective-permute-start | bytes 786440 | tf_op jit(solution)/shard_map/ppermute | solution.py:195
  81.6 3.7 %all-to-all-done = bf16[8,8,16,128]{3,2,1,0:T(8,128)(2,1)S(1)} async-done(((bf16[8,8,16,128]{3,2,1,0:T(8,128)(2,1)}), bf16[8,8,16,128]{3,2,1,0:T(8,128)(2,1)S(1)}, u32[]{:S(2)}, u32[]{:S(2)}) %all-to-all-start) | async-done | bytes 262176 | tf_op jit(solution)/shard_map/all_to_all | solution.py:264
  85.3 6.0 %collective-permute-done.15.p1 = bf16[8,128,128]{2,1,0:T(8,128)(2,1)S(1)} collective-permute-done((bf16[8,128,128]{2,1,0:T(8,128)(2,1)S(1)}, bf16[8,128,128]{2,1,0:T(8,128)(2,1)S(1)}, u32[]{:S(2)}, u32[]{:S(2)}) %collective-permute-start.15) | collective-permute-done | bytes 262176 | tf_op jit(solution)/shard_map/ppermute | solution.py:195
  91.3 3.7 %collective-permute-done.17.p3 = bf16[8,128,128]{2,1,0:T(8,128)(2,1)S(1)} collective-permute-done((bf16[8,128,128]{2,1,0:T(8,128)(2,1)S(1)}, bf16[8,128,128]{2,1,0:T(8,128)(2,1)S(1)}, u32[]{:S(2)}, u32[]{:S(2)}) %collective-permute-start.17) | collective-permute-done | bytes 262176 | tf_op jit(solution)/shard_map/ppermute | solution.py:195
  100.2 5.4 %up_terms.1 = bf16[4,128,16,128]{3,2,1,0:T(8,128)(2,1)} custom-call(s32[32]{0:T(128)S(1)} %fusion.13.spot, s32[128]{0:T(128)S(1)} %get-tuple-element.50.up_where.where, bf16[16,4,16,256]{3,2,1,0:T(8,128)(2,1)S(1)} %turn.1.xt, bf16[32,128,128]{2,1,0:T(8,128)(2,1)S(1)} %join.2.v.v0, bf16[32,128,128]{2,1,0:T(8,128)(2,1)S(1)} %collective-permute-done.29.v1), custom_call_target="tpu_custom_call" | custom-call | flops 1024 | bytes 1024 | tf_op jit(solution)/shard_map/up_terms/pallas_call | solution.py:35
  105.5 5.1 %all-to-all-start.1 = ((bf16[4,128,16,128]{3,2,1,0:T(8,128)(2,1)}), bf16[4,128,16,128]{3,2,1,0:T(8,128)(2,1)S(1)}, u32[]{:S(2)}, u32[]{:S(2)}) async-start(bf16[4,128,16,128]{3,2,1,0:T(8,128)(2,1)} %up_terms.1), calls=%async_computation.1 | async-start | bytes 4194304 | tf_op jit(solution)/shard_map/all_to_all | solution.py:273
  114.4 10.3 %collective-permute-done.20.a3 = bf16[16,128,128]{2,1,0:T(8,128)(2,1)} collective-permute-done((bf16[16,128,128]{2,1,0:T(8,128)(2,1)}, bf16[16,128,128]{2,1,0:T(8,128)(2,1)}, u32[]{:S(2)}, u32[]{:S(2)}) %collective-permute-start.20) | collective-permute-done | bytes 524320 | tf_op jit(solution)/shard_map/ppermute | solution.py:195
  129.0 5.8 %ends.1 = (bf16[2,2,128,256]{3,2,1,0:T(8,128)(2,1)S(1)}, bf16[2,2,128,256]{3,2,1,0:T(8,128)(2,1)S(1)}, bf16[2,2,128,256]{3,2,1,0:T(8,128)(2,1)S(1)}, bf16[2,2,12...) custom-call(s32[16]{0:T(128)S(1)} %fusion.9.order, s32[32]{0:T(128)S(1)} %fusion.13.spot, ...), custom_call_target="tpu_custom_call" | custom-call | flops 1024 | bytes 1024 | tf_op jit(solution)/shard_map/ends/pallas_call | solution.py:35
  138.5 5.8 %down_terms.1 = f32[128,16,128]{2,1,0:T(8,128)} custom-call(s32[2]{0:T(128)S(1)} %pad_add_fusion.place, s32[16]{0:T(128)S(1)} %fusion.23.spot, s32[128]{0:T(128)S(1)} %get-tuple-element.51.down_where.where, bf16[64,128,128]{2,1,0:T(8,128)(2,1)S(1)} %get-tuple-element.39.a, bf16[8,128,256]{2,1,0:T(8,128)(2,1)} %get-tuple-element.28.g0, ...), custom_call_target="tpu_custom_call" | custom-call | flops 1024 | bytes 1024 | tf_op jit(solution)/shard_map/down_terms/pallas_call | solution.py:35
  144.3 2.4 %collective-permute-done.26 = bf16[2,2,128,256]{3,2,1,0:T(8,128)(2,1)S(1)} collective-permute-done((bf16[2,2,128,256]{3,2,1,0:T(8,128)(2,1)S(1)}, bf16[2,2,128,256]{3,2,1,0:T(8,128)(2,1)S(1)}, u32[]{:S(2)}, u32[]{:S(2)}) %collective-permute-start.26) | collective-permute-done | bytes 262176 | tf_op jit(solution)/shard_map/ppermute | solution.py:195
  146.7 4.8 %collective-permute-done.25 = bf16[2,2,128,256]{3,2,1,0:T(8,128)(2,1)S(1)} collective-permute-done((bf16[2,2,128,256]{3,2,1,0:T(8,128)(2,1)S(1)}, bf16[2,2,128,256]{3,2,1,0:T(8,128)(2,1)S(1)}, u32[]{:S(2)}, u32[]{:S(2)}) %collective-permute-start.25) | collective-permute-done | bytes 262176 | tf_op jit(solution)/shard_map/ppermute | solution.py:195
  151.7 6.4 %collective-permute-start.28 = (bf16[2,128,256]{2,1,0:T(8,128)(2,1)S(1)}, bf16[2,128,256]{2,1,0:T(8,128)(2,1)S(1)}, u32[]{:S(2)}, u32[]{:S(2)}) collective-permute-start(bf16[2,128,256]{2,1,0:T(8,128)(2,1)S(1)} %fusion.2), channel_id=1, source_target_pairs={{0,4},{4,0},{1,5},{5,1},{2,6},{6,2},{3,7},{7,3},{8,12},{12,8},{9,1... | collective-permute-start | bytes 393224 | tf_op jit(solution)/shard_map/ppermute | solution.py:199
  158.0 10.1 %collective-permute-done.28 = bf16[2,128,256]{2,1,0:T(8,128)(2,1)S(1)} collective-permute-done((bf16[2,128,256]{2,1,0:T(8,128)(2,1)S(1)}, bf16[2,128,256]{2,1,0:T(8,128)(2,1)S(1)}, u32[]{:S(2)}, u32[]{:S(2)}) %collective-permute-start.28) | collective-permute-done | bytes 131104 | tf_op jit(solution)/shard_map/ppermute | solution.py:199
  (78 shorter events, 43.4 us)
Async XLA Ops:
  0.6 11.6 %collective-permute-start = (bf16[128,256]{1,0:T(8,128)(2,1)}, bf16[128,256]{1,0:T(8,128)(2,1)S(1)}, u32[]{:S(2)}, u32[]{:S(2)}) collective-permute-start(bf16[128,256]{1,0:T(8,128)(2,1)} %param.6), channel_id=1, source_target_pairs={{0,4},{4,0},{1,5},{5,1},{2,6},{6,2},{3,7},{7,3},{8,12},{12,8},{9,1... | collective-permute-start | bytes 196616 | tf_op jit(solution)/shard_map/ppermute | solution.py:199
  7.0 11.5 %collective-permute-start.4 = (bf16[128,256]{1,0:T(8,128)(2,1)}, bf16[128,256]{1,0:T(8,128)(2,1)S(1)}, u32[]{:S(2)}, u32[]{:S(2)}) collective-permute-start(bf16[128,256]{1,0:T(8,128)(2,1)} %param.7), channel_id=1, source_target_pairs={{0,4},{4,0},{1,5},{5,1},{2,6},{6,2},{3,7},{7,3},{8,12},{12,8},{9,1... | collective-permute-start | bytes 196616 | tf_op jit(solution)/shard_map/ppermute | solution.py:199
  13.0 10.4 %collective-permute-start.1 = (bf16[2,128,256]{2,1,0:T(8,128)(2,1)S(1)}, bf16[2,128,256]{2,1,0:T(8,128)(2,1)S(1)}, u32[]{:S(2)}, u32[]{:S(2)}) collective-permute-start(bf16[2,128,256]{2,1,0:T(8,128)(2,1)S(1)} %pad_maximum_fusion.2.x0), channel_id=1, source_target_pairs={{0,3},{1,0},{2,1},{3,2},{4,7},{5,4},{6,5},{7,6},{8,11},{9,8},{10,9... | collective-permute-start | bytes 393224 | tf_op jit(solution)/shard_map/ppermute | solution.py:195
  17.6 9.6 %collective-permute-start.3 = (bf16[2,128,256]{2,1,0:T(8,128)(2,1)S(1)}, bf16[2,128,256]{2,1,0:T(8,128)(2,1)S(1)}, u32[]{:S(2)}, u32[]{:S(2)}) collective-permute-start(bf16[2,128,256]{2,1,0:T(8,128)(2,1)S(1)} %pad_maximum_fusion.2.x0), channel_id=1, source_target_pairs={{0,1},{1,2},{2,3},{3,0},{4,5},{5,6},{6,7},{7,4},{8,9},{9,10},{10,1... | collective-permute-start | bytes 393224 | tf_op jit(solution)/shard_map/ppermute | solution.py:195
  41.5 9.4 %collective-permute-start.8 = (bf16[8,128,256]{2,1,0:T(8,128)(2,1)S(1)}, bf16[8,128,256]{2,1,0:T(8,128)(2,1)S(1)}, u32[]{:S(2)}, u32[]{:S(2)}) collective-permute-start(bf16[8,128,256]{2,1,0:T(8,128)(2,1)S(1)} %get-tuple-element.26.x), channel_id=1, source_target_pairs={{0,32},{32,0},{1,33},{33,1},{2,34},{34,2},{3,35},{35,3},{4,36},{36... | collective-permute-start | bytes 1572872 | tf_op jit(solution)/shard_map/ppermute | solution.py:199
  41.5 21.3 %collective-permute-start.11 = (bf16[8,128,256]{2,1,0:T(8,128)(2,1)}, bf16[8,128,256]{2,1,0:T(8,128)(2,1)}, u32[]{:S(2)}, u32[]{:S(2)}) collective-permute-start(bf16[8,128,256]{2,1,0:T(8,128)(2,1)} %get-tuple-element.28.g0), channel_id=1, source_target_pairs={{0,32},{32,0},{1,33},{33,1},{2,34},{34,2},{3,35},{35,3},{4,36},{36... | collective-permute-start | bytes 1572872 | tf_op jit(solution)/shard_map/ppermute | solution.py:199
  42.0 20.8 %collective-permute-start.12 = (bf16[2,8,128,128]{3,2,1,0:T(8,128)(2,1)}, bf16[2,8,128,128]{3,2,1,0:T(8,128)(2,1)S(1)}, u32[]{:S(2)}, u32[]{:S(2)}) collective-permute-start(bf16[2,8,128,128]{3,2,1,0:T(8,128)(2,1)} %get-tuple-element.30), channel_id=1, source_target_pairs={{0,8},{8,16},{16,24},{24,0},{1,9},{9,17},{17,25},{25,1},{2,10},{10... | collective-permute-start | bytes 1572872 | tf_op jit(solution)/shard_map/ppermute | solution.py:195
  43.5 26.1 %collective-permute-start.13 = (bf16[2,8,128,128]{3,2,1,0:T(8,128)(2,1)}, bf16[2,8,128,128]{3,2,1,0:T(8,128)(2,1)S(1)}, u32[]{:S(2)}, u32[]{:S(2)}) collective-permute-start(bf16[2,8,128,128]{3,2,1,0:T(8,128)(2,1)} %get-tuple-element.31), channel_id=1, source_target_pairs={{0,16},{8,24},{16,0},{24,8},{1,17},{9,25},{17,1},{25,9},{2,18},{10... | collective-permute-start | bytes 1572872 | tf_op jit(solution)/shard_map/ppermute | solution.py:195
  47.4 22.2 %collective-permute-start.14 = (bf16[2,8,128,128]{3,2,1,0:T(8,128)(2,1)}, bf16[2,8,128,128]{3,2,1,0:T(8,128)(2,1)}, u32[]{:S(2)}, u32[]{:S(2)}) collective-permute-start(bf16[2,8,128,128]{3,2,1,0:T(8,128)(2,1)} %get-tuple-element.32), channel_id=1, source_target_pairs={{0,24},{8,0},{16,8},{24,16},{1,25},{9,1},{17,9},{25,17},{2,26},{10... | collective-permute-start | bytes 1572872 | tf_op jit(solution)/shard_map/ppermute | solution.py:195
  50.9 11.9 %collective-permute-start.10 = (bf16[2,2,128,256]{3,2,1,0:T(8,128)(2,1)}, bf16[2,2,128,256]{3,2,1,0:T(8,128)(2,1)S(1)}, u32[]{:S(2)}, u32[]{:S(2)}) collective-permute-start(bf16[2,2,128,256]{3,2,1,0:T(8,128)(2,1)} %pad_maximum_fusion.1), channel_id=1, source_target_pairs={{0,128},{64,192},{128,0},{192,64},{1,129},{65,193},{129,1},{193,65... | collective-permute-start | bytes 786440 | tf_op jit(solution)/shard_map/ppermute | solution.py:203
  72.2 13.2 %all-to-all-start = ((bf16[8,8,16,128]{3,2,1,0:T(8,128)(2,1)}), bf16[8,8,16,128]{3,2,1,0:T(8,128)(2,1)S(1)}, u32[]{:S(2)}, u32[]{:S(2)}) async-start(bf16[8,8,16,128]{3,2,1,0:T(8,128)(2,1)} %get-tuple-element.34), calls=%async_computation | async-start | bytes 524288 | tf_op jit(solution)/shard_map/all_to_all | solution.py:264
  77.4 13.9 %collective-permute-start.15 = (bf16[8,128,128]{2,1,0:T(8,128)(2,1)S(1)}, bf16[8,128,128]{2,1,0:T(8,128)(2,1)S(1)}, u32[]{:S(2)}, u32[]{:S(2)}) collective-permute-start(bf16[8,128,128]{2,1,0:T(8,128)(2,1)S(1)} %get-tuple-element.35.p0), channel_id=1, source_target_pairs={{0,24},{8,0},{16,8},{24,16},{1,25},{9,1},{17,9},{25,17},{2,26},{10... | collective-permute-start | bytes 786440 | tf_op jit(solution)/shard_map/ppermute | solution.py:195
  79.8 11.5 %collective-permute-start.16 = (bf16[8,128,128]{2,1,0:T(8,128)(2,1)S(1)}, bf16[8,128,128]{2,1,0:T(8,128)(2,1)S(1)}, u32[]{:S(2)}, u32[]{:S(2)}) collective-permute-start(bf16[8,128,128]{2,1,0:T(8,128)(2,1)S(1)} %get-tuple-element.35.p0), channel_id=1, source_target_pairs={{0,16},{8,24},{16,0},{24,8},{1,17},{9,25},{17,1},{25,9},{2,18},{10... | collective-permute-start | bytes 786440 | tf_op jit(solution)/shard_map/ppermute | solution.py:195
  81.6 13.4 %collective-permute-start.17 = (bf16[8,128,128]{2,1,0:T(8,128)(2,1)S(1)}, bf16[8,128,128]{2,1,0:T(8,128)(2,1)S(1)}, u32[]{:S(2)}, u32[]{:S(2)}) collective-permute-start(bf16[8,128,128]{2,1,0:T(8,128)(2,1)S(1)} %get-tuple-element.35.p0), channel_id=1, source_target_pairs={{0,8},{8,16},{16,24},{24,0},{1,9},{9,17},{17,25},{25,1},{2,10},{10... | collective-permute-start | bytes 786440 | tf_op jit(solution)/shard_map/ppermute | solution.py:195
  97.0 16.6 %collective-permute-start.18 = (bf16[16,128,128]{2,1,0:T(8,128)(2,1)}, bf16[16,128,128]{2,1,0:T(8,128)(2,1)}, u32[]{:S(2)}, u32[]{:S(2)}) collective-permute-start(bf16[16,128,128]{2,1,0:T(8,128)(2,1)} %pad_maximum_fusion.a0), channel_id=1, source_target_pairs={{0,24},{8,0},{16,8},{24,16},{1,25},{9,1},{17,9},{25,17},{2,26},{10... | collective-permute-start | bytes 1572872 | tf_op jit(solution)/shard_map/ppermute | solution.py:195
  97.6 16.8 %collective-permute-start.19 = (bf16[16,128,128]{2,1,0:T(8,128)(2,1)}, bf16[16,128,128]{2,1,0:T(8,128)(2,1)}, u32[]{:S(2)}, u32[]{:S(2)}) collective-permute-start(bf16[16,128,128]{2,1,0:T(8,128)(2,1)} %pad_maximum_fusion.a0), channel_id=1, source_target_pairs={{0,16},{8,24},{16,0},{24,8},{1,17},{9,25},{17,1},{25,9},{2,18},{10... | collective-permute-start | bytes 1572872 | tf_op jit(solution)/shard_map/ppermute | solution.py:195
  99.4 25.3 %collective-permute-start.20 = (bf16[16,128,128]{2,1,0:T(8,128)(2,1)}, bf16[16,128,128]{2,1,0:T(8,128)(2,1)}, u32[]{:S(2)}, u32[]{:S(2)}) collective-permute-start(bf16[16,128,128]{2,1,0:T(8,128)(2,1)} %pad_maximum_fusion.a0), channel_id=1, source_target_pairs={{0,8},{8,16},{16,24},{24,0},{1,9},{9,17},{17,25},{25,1},{2,10},{10... | collective-permute-start | bytes 1572872 | tf_op jit(solution)/shard_map/ppermute | solution.py:195
  105.5 63.3 %all-to-all-start.1 = ((bf16[4,128,16,128]{3,2,1,0:T(8,128)(2,1)}), bf16[4,128,16,128]{3,2,1,0:T(8,128)(2,1)S(1)}, u32[]{:S(2)}, u32[]{:S(2)}) async-start(bf16[4,128,16,128]{3,2,1,0:T(8,128)(2,1)} %up_terms.1), calls=%async_computation.1 | async-start | bytes 4194304 | tf_op jit(solution)/shard_map/all_to_all | solution.py:273
  111.6 23.2 %collective-permute-start.21 = (bf16[1,3,2,128,256]{4,3,2,1,0:T(8,128)(2,1)S(1)}, bf16[1,3,2,128,256]{4,3,2,1,0:T(8,128)(2,1)S(1)}, u32[]{:S(2)}, u32[]{:S(2)}) collective-permute-start(bf16[1,3,2,128,256]{4,3,2,1,0:T(8,128)(2,1)S(1)} %maximum_bitcast_fusion.p0), channel_id=1, source_target_pairs={{0,3},{1,0},{2,1},{3,2},{4,7},{5,4},{6,5},{7,6},{8,11},{9,8},{10,9... | collective-permute-start | bytes 1179656 | tf_op jit(solution)/shard_map/ppermute | solution.py:195
  112.6 22.3 %collective-permute-start.22 = (bf16[1,3,2,128,256]{4,3,2,1,0:T(8,128)(2,1)S(1)}, bf16[1,3,2,128,256]{4,3,2,1,0:T(8,128)(2,1)S(1)}, u32[]{:S(2)}, u32[]{:S(2)}) collective-permute-start(bf16[1,3,2,128,256]{4,3,2,1,0:T(8,128)(2,1)S(1)} %maximum_bitcast_fusion.p0), channel_id=1, source_target_pairs={{0,2},{1,3},{2,0},{3,1},{4,6},{5,7},{6,4},{7,5},{8,10},{9,11},{10,... | collective-permute-start | bytes 1179656 | tf_op jit(solution)/shard_map/ppermute | solution.py:195
  113.5 21.3 %collective-permute-start.23 = (bf16[1,3,2,128,256]{4,3,2,1,0:T(8,128)(2,1)S(1)}, bf16[1,3,2,128,256]{4,3,2,1,0:T(8,128)(2,1)S(1)}, u32[]{:S(2)}, u32[]{:S(2)}) collective-permute-start(bf16[1,3,2,128,256]{4,3,2,1,0:T(8,128)(2,1)S(1)} %maximum_bitcast_fusion.p0), channel_id=1, source_target_pairs={{0,1},{1,2},{2,3},{3,0},{4,5},{5,6},{6,7},{7,4},{8,9},{9,10},{10,1... | collective-permute-start | bytes 1179656 | tf_op jit(solution)/shard_map/ppermute | solution.py:195
  136.0 10.7 %collective-permute-start.26 = (bf16[2,2,128,256]{3,2,1,0:T(8,128)(2,1)S(1)}, bf16[2,2,128,256]{3,2,1,0:T(8,128)(2,1)S(1)}, u32[]{:S(2)}, u32[]{:S(2)}) collective-permute-start(bf16[2,2,128,256]{3,2,1,0:T(8,128)(2,1)S(1)} %get-tuple-element.44), channel_id=1, source_target_pairs={{0,2},{1,3},{2,0},{3,1},{4,6},{5,7},{6,4},{7,5},{8,10},{9,11},{10,... | collective-permute-start | bytes 786440 | tf_op jit(solution)/shard_map/ppermute | solution.py:195
  137.0 14.5 %collective-permute-start.25 = (bf16[2,2,128,256]{3,2,1,0:T(8,128)(2,1)S(1)}, bf16[2,2,128,256]{3,2,1,0:T(8,128)(2,1)S(1)}, u32[]{:S(2)}, u32[]{:S(2)}) collective-permute-start(bf16[2,2,128,256]{3,2,1,0:T(8,128)(2,1)S(1)} %get-tuple-element.43), channel_id=1, source_target_pairs={{0,1},{1,2},{2,3},{3,0},{4,5},{5,6},{6,7},{7,4},{8,9},{9,10},{10,1... | collective-permute-start | bytes 786440 | tf_op jit(solution)/shard_map/ppermute | solution.py:195
  151.7 16.5 %collective-permute-start.28 = (bf16[2,128,256]{2,1,0:T(8,128)(2,1)S(1)}, bf16[2,128,256]{2,1,0:T(8,128)(2,1)S(1)}, u32[]{:S(2)}, u32[]{:S(2)}) collective-permute-start(bf16[2,128,256]{2,1,0:T(8,128)(2,1)S(1)} %fusion.2), channel_id=1, source_target_pairs={{0,4},{4,0},{1,5},{5,1},{2,6},{6,2},{3,7},{7,3},{8,12},{12,8},{9,1... | collective-permute-start | bytes 393224 | tf_op jit(solution)/shard_map/ppermute | solution.py:199
  (15 other events, 117.5 us)
